TPU v7x, 32 devices: a whole 2x2x4 slice. The times are simulated.
32 devices in a mesh: wide: 16 (over z, y, core), narrow: 2 (over x).
Axes of the slice: x: 2, y: 2, z: 4, core: 2. Of those that a mesh axis runs over, the one named last changes fastest.
Arguments:
- target: bfloat16 [65536, 512], P(('wide', 'narrow')), may hold values from -6 to 6
- memory: bfloat16 [65536, 512], P(('wide', 'narrow')), may hold values from -6 to 6
- out_grad: bfloat16 [65536, 512], P(('wide', 'narrow')), may hold values from -6 to 6
- target_segments: int32 [64, 1024], P(('wide', 'narrow')), may hold values from 0 to 24, as said below
- source_segments: int32 [64, 1024], P(('wide', 'narrow')), may hold values from 0 to 24, as said below
- target_positions: int32 [64, 1024], P(('wide', 'narrow')), may hold values from 0 to 999, as said below
- self_qkv: bfloat16 [512, 1536], P(('wide', 'narrow')), may hold values from -0.25 to 0.25
- self_out: bfloat16 [512, 512], P(('wide', 'narrow')), may hold values from -1 to 1
- cross_query: bfloat16 [512, 512], P(('wide', 'narrow')), may hold values from -0.25 to 0.25
- cross_kv: bfloat16 [512, 1024], P(('wide', 'narrow')), may hold values from -0.25 to 0.25
- cross_out: bfloat16 [512, 512], P(('wide', 'narrow')), may hold values from -1 to 1
- ffn_in: bfloat16 [512, 2048], P(('wide', 'narrow')), may hold values from -0.25 to 0.25
- ffn_out: bfloat16 [2048, 512], P(('wide', 'narrow')), may hold values from -0.125 to 0.125
- self_bias: bfloat16 [1536], P(('wide', 'narrow')), may hold values from -3 to 3
- self_gain: bfloat16 [512], P(('wide', 'narrow')), may hold values from 0.5 to 1.5
- self_shift: bfloat16 [512], P(('wide', 'narrow')), may hold values from -2 to 2
- cross_bias: bfloat16 [1536], P(('wide', 'narrow')), may hold values from -3 to 3
- cross_gain: bfloat16 [512], P(('wide', 'narrow')), may hold values from 0.5 to 1.5
- cross_shift: bfloat16 [512], P(('wide', 'narrow')), may hold values from -2 to 2
- ffn_in_bias: bfloat16 [2048], P(('wide', 'narrow')), may hold values from -3 to 3
- ffn_out_bias: bfloat16 [512], P(('wide', 'narrow')), may hold values from -2 to 2
- ffn_gain: bfloat16 [512], P(('wide', 'narrow')), may hold values from 0.5 to 1.5
- ffn_shift: bfloat16 [512], P(('wide', 'narrow')), may hold values from -2 to 2
Outputs:
- output: bfloat16 [65536, 512], P(('wide', 'narrow'))
- target_grad: bfloat16 [65536, 512], P(('wide', 'narrow'))
- memory_grad: bfloat16 [65536, 512], P(('wide', 'narrow'))
- self_qkv_grad: float32 [512, 1536], P(('wide', 'narrow'))
- self_out_grad: float32 [512, 512], P(('wide', 'narrow'))
- cross_query_grad: float32 [512, 512], P(('wide', 'narrow'))
- cross_kv_grad: float32 [512, 1024], P(('wide', 'narrow'))
- cross_out_grad: float32 [512, 512], P(('wide', 'narrow'))
- ffn_in_grad: float32 [512, 2048], P(('wide', 'narrow'))
- ffn_out_grad: float32 [2048, 512], P(('wide', 'narrow'))
- self_bias_grad: float32 [1536], P(('wide', 'narrow'))
- self_gain_grad: float32 [512], P(('wide', 'narrow'))
- self_shift_grad: float32 [512], P(('wide', 'narrow'))
- cross_bias_grad: float32 [1536], P(('wide', 'narrow'))
- cross_gain_grad: float32 [512], P(('wide', 'narrow'))
- cross_shift_grad: float32 [512], P(('wide', 'narrow'))
- ffn_in_bias_grad: float32 [2048], P(('wide', 'narrow'))
- ffn_out_bias_grad: float32 [512], P(('wide', 'narrow'))
- ffn_gain_grad: float32 [512], P(('wide', 'narrow'))
- ffn_shift_grad: float32 [512], P(('wide', 'narrow'))
Inputs may be any that keep to these rules, and one draw needn't show every extreme that they name: `target_segments`: each row holds 24 target sentences numbered 1 to 24 in order, each a run of consecutive tokens, then padding numbered 0 of 1 to 64 tokens at its end. In one row, drawn from the seed, sentences 1 to 23 have one token each and the padding is one token. `source_segments`: each row holds 24 source sentences numbered 1 to 24 in order, each a run of consecutive tokens, then padding numbered 0 of 1 to 64 tokens at its end. `target_positions`: A token's offset from the first token of its sentence (of its padding for padding tokens).
All inputs are finite; a program needn't handle non-finite values.
Results may differ from a plain program's by a relative error of at most 0.028.
Values may be sent and summed in bfloat16 or wider, within the bound.
No kernel may reach another device: no remote copies, remote signals or barrier semaphores. Data moves between devices by JAX's collectives and lax.ppermute only.
A program may use at most 256 MiB of HBM per device.

v0:
```python
import math

import jax
import jax.numpy as jnp
from jax import lax
from jax.sharding import PartitionSpec as P

HEADS = 8


EPSILON = 1e-05
MASKED = -1e30


def shortened(x):

    def short(part):
        return part.astype(jnp.bfloat16) if part.dtype == jnp.float32 else part

    return jax.tree.map(short, x)


def matmul_plain(left_side, right_side):
    return jnp.dot(left_side, right_side, preferred_element_type=jnp.float32)


def matmul_left_t(left_side, right_side):
    return lax.dot_general(
        left_side, right_side, (((0,), (0,)), ((), ())), preferred_element_type=jnp.float32
    )


def matmul_right_t(left_side, right_side):
    return lax.dot_general(
        left_side, right_side, (((1,), (1,)), ((), ())), preferred_element_type=jnp.float32
    )


def column_sums(values):
    return jnp.sum(values, axis=0, dtype=jnp.float32)


def fetch(pieces):
    return jax.tree.map(
        lambda part, own: part.astype(own.dtype),
        lax.all_gather(shortened(pieces), ("wide", "narrow"), axis=0, tiled=True),
        pieces,
    )


def fetch_again(pieces):
    return jax.tree.map(
        lambda part, own: part.astype(own.dtype),
        lax.all_gather(shortened(pieces), ("wide", "narrow"), axis=0, tiled=True),
        pieces,
    )


def to_grid(grads):
    outer_count = lax.axis_size("wide")
    inner_count = lax.axis_size("narrow")
    return tuple(
        (
            member.reshape(
                (outer_count, inner_count, member.shape[0] // (outer_count * inner_count))
                + member.shape[1:]
            )
            for member in grads
        )
    )


def from_grid(grids):
    return tuple((member.reshape((member.shape[2],) + member.shape[3:]) for member in grids))


def reduce_each(grads):
    inner_sums = jax.tree.map(
        lambda part: part.astype(jnp.float32),
        lax.psum_scatter(shortened(to_grid(grads)), "narrow", scatter_dimension=1, tiled=True),
    )
    return from_grid(
        jax.tree.map(
            lambda part: part.astype(jnp.float32),
            lax.psum_scatter(shortened(inner_sums), "wide", scatter_dimension=0, tiled=True),
        )
    )


def norm_forward(hidden, gain, shift):
    average = jnp.mean(hidden, axis=-1, keepdims=True)
    centred = hidden - average
    inverse = lax.rsqrt(jnp.mean(centred * centred, axis=-1, keepdims=True) + EPSILON)
    normed = centred * inverse
    return (normed * gain + shift, normed, inverse)


def norm_backward(grad_in, normed, inverse, gain):
    gain_grad = jnp.sum(grad_in * normed, axis=0)
    shift_grad = jnp.sum(grad_in, axis=0)
    scaled = grad_in * gain
    hidden_grad = inverse * (
        scaled
        - jnp.mean(scaled, axis=-1, keepdims=True)
        - normed * jnp.mean(scaled * normed, axis=-1, keepdims=True)
    )
    return (gain_grad, shift_grad, hidden_grad)


def causal_allow(query_info, key_info):
    return (query_info[0][:, None] == key_info[0][None, :]) & (
        key_info[1][None, :] <= query_info[1][:, None]
    )


def cross_allow(query_info, key_info):
    return query_info[0][:, None] == key_info[0][None, :]


def block_layout(queries, keys_all, values_all, query_info):
    row_count, length = query_info[0].shape
    head_size = queries.shape[1] // HEADS
    block_rows = min(512, length)
    block_count = length // block_rows
    query_blocks = queries.reshape(row_count * block_count, block_rows, HEADS, head_size)
    key_rows = keys_all.reshape(row_count, length, HEADS, head_size)
    value_rows = values_all.reshape(row_count, length, HEADS, head_size)
    info_blocks = tuple(
        (member.reshape(row_count * block_count, block_rows) for member in query_info)
    )
    row_of_block = jnp.arange(row_count * block_count, dtype=jnp.int32) // block_count
    return (query_blocks, key_rows, value_rows, info_blocks, row_of_block, head_size, block_count)


def masked_scores(query_block, keys_here, allowed, scaling):
    scores = (
        jnp.einsum("qhe,khe->hqk", query_block, keys_here, preferred_element_type=jnp.float32)
        * scaling
    )
    return jnp.where(allowed[None], scores, MASKED)


def attend_forward(queries, keys_all, values_all, query_info, key_info, allow):
    query_blocks, key_rows, value_rows, info_blocks, row_of_block, head_size, block_count = (
        block_layout(queries, keys_all, values_all, query_info)
    )
    scaling = 1.0 / math.sqrt(head_size)

    def one_block(pieces):
        query_block, block_info, row_index = pieces
        keys_here = lax.dynamic_index_in_dim(key_rows, row_index, 0, keepdims=False)
        values_here = lax.dynamic_index_in_dim(value_rows, row_index, 0, keepdims=False)
        key_here_info = tuple(
            (lax.dynamic_index_in_dim(member, row_index, 0, keepdims=False) for member in key_info)
        )
        scores = masked_scores(query_block, keys_here, allow(block_info, key_here_info), scaling)
        highest = jnp.max(scores, axis=-1, keepdims=True)
        weights = jnp.exp(scores - highest)
        totals = jnp.sum(weights, axis=-1, keepdims=True)
        prob_rows = (weights / totals).astype(jnp.bfloat16)
        mixture = jnp.einsum(
            "hqk,khe->qhe", prob_rows, values_here, preferred_element_type=jnp.float32
        )
        return (mixture, highest[..., 0] + jnp.log(totals[..., 0]))

    mixture, logsum = lax.map(one_block, (query_blocks, info_blocks, row_of_block))
    return (mixture.reshape(queries.shape), logsum)


def attend_backward(queries, keys_all, values_all, grad_mixed, logsum, query_info, key_info, allow):
    query_blocks, key_rows, value_rows, info_blocks, row_of_block, head_size, block_count = (
        block_layout(queries, keys_all, values_all, query_info)
    )
    scaling = 1.0 / math.sqrt(head_size)
    grad_blocks = grad_mixed.reshape(query_blocks.shape)

    def one_block(pieces):
        query_block, grad_block, logsum_block, block_info, row_index = pieces
        keys_here = lax.dynamic_index_in_dim(key_rows, row_index, 0, keepdims=False)
        values_here = lax.dynamic_index_in_dim(value_rows, row_index, 0, keepdims=False)
        key_here_info = tuple(
            (lax.dynamic_index_in_dim(member, row_index, 0, keepdims=False) for member in key_info)
        )
        scores = masked_scores(query_block, keys_here, allow(block_info, key_here_info), scaling)
        prob_full = jnp.exp(scores - logsum_block[..., None])
        prob_rows = prob_full.astype(jnp.bfloat16)
        grad_values = jnp.einsum(
            "hqk,qhe->khe", prob_rows, grad_block, preferred_element_type=jnp.float32
        )
        grad_probs = jnp.einsum(
            "qhe,khe->hqk", grad_block, values_here, preferred_element_type=jnp.float32
        )
        centred = grad_probs - jnp.sum(prob_full * grad_probs, axis=-1, keepdims=True)
        grad_scores = (prob_full * centred).astype(jnp.bfloat16)
        grad_queries = (
            jnp.einsum("hqk,khe->qhe", grad_scores, keys_here, preferred_element_type=jnp.float32)
            * scaling
        )
        grad_keys = (
            jnp.einsum("hqk,qhe->khe", grad_scores, query_block, preferred_element_type=jnp.float32)
            * scaling
        )
        return (grad_queries, grad_keys, grad_values)

    grad_queries, grad_keys, grad_values = lax.map(
        one_block, (query_blocks, grad_blocks, logsum, info_blocks, row_of_block)
    )
    row_count = key_rows.shape[0]
    grad_keys = jnp.sum(grad_keys.reshape(row_count, block_count, -1), axis=1).reshape(
        keys_all.shape
    )
    grad_values = jnp.sum(grad_values.reshape(row_count, block_count, -1), axis=1).reshape(
        values_all.shape
    )
    return (grad_queries.reshape(queries.shape), grad_keys, grad_values)


def per_device(
    target,
    memory,
    out_grad,
    target_segments,
    source_segments,
    target_positions,
    self_qkv,
    self_out,
    cross_query,
    cross_kv,
    cross_out,
    ffn_in,
    ffn_out,
    self_bias,
    self_gain,
    self_shift,
    cross_bias,
    cross_gain,
    cross_shift,
    ffn_in_bias,
    ffn_out_bias,
    ffn_gain,
    ffn_shift,
):
    model_width = target.shape[1]
    zeros_row = jnp.zeros((model_width,), jnp.float32)
    self_info = (target_segments, target_positions)
    query_info = (target_segments,)
    source_info = (source_segments,)
    qkv_full, self_out_full, self_bias_full, self_gain_full, self_shift_full = fetch(
        (self_qkv, self_out, self_bias, self_gain, self_shift)
    )
    self_bias_wide = self_bias_full.astype(jnp.float32)
    joined_bias = jnp.concatenate(
        [self_bias_wide[:model_width], zeros_row, self_bias_wide[model_width : 2 * model_width]]
    )
    projected = (matmul_plain(target, qkv_full) + joined_bias).astype(jnp.bfloat16)
    self_queries = projected[:, :model_width]
    self_keys = projected[:, model_width : 2 * model_width]
    self_values = projected[:, 2 * model_width :]
    self_mixture, self_logsum = attend_forward(
        self_queries, self_keys, self_values, self_info, self_info, causal_allow
    )
    self_mix_low = self_mixture.astype(jnp.bfloat16)
    hidden_one = (
        target.astype(jnp.float32)
        + matmul_plain(self_mix_low, self_out_full)
        + self_bias_wide[2 * model_width :]
    )
    first_out, normed_one, inverse_one = norm_forward(
        hidden_one, self_gain_full.astype(jnp.float32), self_shift_full.astype(jnp.float32)
    )
    first_low = first_out.astype(jnp.bfloat16)
    (
        cross_query_full,
        cross_kv_full,
        cross_out_full,
        cross_bias_full,
        cross_gain_full,
        cross_shift_full,
    ) = fetch((cross_query, cross_kv, cross_out, cross_bias, cross_gain, cross_shift))
    cross_bias_wide = cross_bias_full.astype(jnp.float32)
    cross_queries = (
        matmul_plain(first_low, cross_query_full) + cross_bias_wide[:model_width]
    ).astype(jnp.bfloat16)
    cross_pairs = (
        matmul_plain(memory, cross_kv_full)
        + jnp.concatenate([zeros_row, cross_bias_wide[model_width : 2 * model_width]])
    ).astype(jnp.bfloat16)
    cross_keys = cross_pairs[:, :model_width]
    cross_values = cross_pairs[:, model_width:]
    cross_mixture, cross_logsum = attend_forward(
        cross_queries, cross_keys, cross_values, query_info, source_info, cross_allow
    )
    cross_mix_low = cross_mixture.astype(jnp.bfloat16)
    hidden_two = (
        first_out + matmul_plain(cross_mix_low, cross_out_full) + cross_bias_wide[2 * model_width :]
    )
    second_out, normed_two, inverse_two = norm_forward(
        hidden_two, cross_gain_full.astype(jnp.float32), cross_shift_full.astype(jnp.float32)
    )
    second_low = second_out.astype(jnp.bfloat16)
    ffn_in_full, ffn_out_full, in_bias_full, out_bias_full, ffn_gain_full, ffn_shift_full = fetch(
        (ffn_in, ffn_out, ffn_in_bias, ffn_out_bias, ffn_gain, ffn_shift)
    )
    pre_act = matmul_plain(second_low, ffn_in_full) + in_bias_full.astype(jnp.float32)
    act_low = jax.nn.silu(pre_act).astype(jnp.bfloat16)
    hidden_three = (
        second_out + matmul_plain(act_low, ffn_out_full) + out_bias_full.astype(jnp.float32)
    )
    final_out, normed_three, inverse_three = norm_forward(
        hidden_three, ffn_gain_full.astype(jnp.float32), ffn_shift_full.astype(jnp.float32)
    )
    output = final_out.astype(jnp.bfloat16)
    ffn_in_back, ffn_out_back, ffn_gain_back = fetch_again((ffn_in, ffn_out, ffn_gain))
    gain_grad_three, shift_grad_three, hidden_grad_three = norm_backward(
        out_grad.astype(jnp.float32), normed_three, inverse_three, ffn_gain_back.astype(jnp.float32)
    )
    branch_grad_three = hidden_grad_three.astype(jnp.bfloat16)
    out_bias_grad = column_sums(branch_grad_three)
    ffn_out_grad = matmul_left_t(act_low, branch_grad_three)
    act_grad = matmul_right_t(branch_grad_three, ffn_out_back)
    sigmoid_pre = jax.nn.sigmoid(pre_act)
    pre_grad = (act_grad * sigmoid_pre * (1.0 + pre_act * (1.0 - sigmoid_pre))).astype(jnp.bfloat16)
    in_bias_grad = column_sums(pre_grad)
    ffn_in_grad = matmul_left_t(second_low, pre_grad)
    second_grad = hidden_grad_three + matmul_right_t(pre_grad, ffn_in_back)
    ffn_grads = (
        ffn_in_grad,
        ffn_out_grad,
        in_bias_grad,
        out_bias_grad,
        gain_grad_three,
        shift_grad_three,
    )
    ffn_grads = reduce_each(ffn_grads)
    cross_query_back, cross_kv_back, cross_out_back, cross_gain_back = fetch_again(
        (cross_query, cross_kv, cross_out, cross_gain)
    )
    gain_grad_two, shift_grad_two, hidden_grad_two = norm_backward(
        second_grad, normed_two, inverse_two, cross_gain_back.astype(jnp.float32)
    )
    branch_grad_two = hidden_grad_two.astype(jnp.bfloat16)
    cross_out_grad = matmul_left_t(cross_mix_low, branch_grad_two)
    cross_mix_grad = matmul_right_t(branch_grad_two, cross_out_back).astype(jnp.bfloat16)
    cross_query_raw, cross_key_raw, cross_value_raw = attend_backward(
        cross_queries,
        cross_keys,
        cross_values,
        cross_mix_grad,
        cross_logsum,
        query_info,
        source_info,
        cross_allow,
    )
    cross_query_low = cross_query_raw.astype(jnp.bfloat16)
    pair_grad = jnp.concatenate([cross_key_raw, cross_value_raw], axis=1).astype(jnp.bfloat16)
    cross_query_grad = matmul_left_t(first_low, cross_query_low)
    cross_kv_grad = matmul_left_t(memory, pair_grad)
    memory_grad = matmul_right_t(pair_grad, cross_kv_back).astype(jnp.bfloat16)
    cross_bias_grad = jnp.concatenate(
        [
            column_sums(cross_query_low),
            column_sums(pair_grad[:, model_width:]),
            column_sums(branch_grad_two),
        ]
    )
    first_grad = hidden_grad_two + matmul_right_t(cross_query_low, cross_query_back)
    cross_grads = (
        cross_query_grad,
        cross_kv_grad,
        cross_out_grad,
        cross_bias_grad,
        gain_grad_two,
        shift_grad_two,
    )
    cross_grads = reduce_each(cross_grads)
    qkv_back, self_out_back, self_gain_back = fetch_again((self_qkv, self_out, self_gain))
    gain_grad_one, shift_grad_one, hidden_grad_one = norm_backward(
        first_grad, normed_one, inverse_one, self_gain_back.astype(jnp.float32)
    )
    branch_grad_one = hidden_grad_one.astype(jnp.bfloat16)
    self_out_grad = matmul_left_t(self_mix_low, branch_grad_one)
    self_mix_grad = matmul_right_t(branch_grad_one, self_out_back).astype(jnp.bfloat16)
    self_query_raw, self_key_raw, self_value_raw = attend_backward(
        self_queries,
        self_keys,
        self_values,
        self_mix_grad,
        self_logsum,
        self_info,
        self_info,
        causal_allow,
    )
    joined_grad = jnp.concatenate([self_query_raw, self_key_raw, self_value_raw], axis=1).astype(
        jnp.bfloat16
    )
    self_qkv_grad = matmul_left_t(target, joined_grad)
    self_bias_grad = jnp.concatenate(
        [
            column_sums(joined_grad[:, :model_width]),
            column_sums(joined_grad[:, 2 * model_width :]),
            column_sums(branch_grad_one),
        ]
    )
    target_grad = (hidden_grad_one + matmul_right_t(joined_grad, qkv_back)).astype(jnp.bfloat16)
    self_grads = (self_qkv_grad, self_out_grad, self_bias_grad, gain_grad_one, shift_grad_one)
    self_grads = reduce_each(self_grads)
    return (
        output,
        target_grad,
        memory_grad,
        self_grads[0],
        self_grads[1],
        cross_grads[0],
        cross_grads[1],
        cross_grads[2],
        ffn_grads[0],
        ffn_grads[1],
        self_grads[2],
        self_grads[3],
        self_grads[4],
        cross_grads[3],
        cross_grads[4],
        cross_grads[5],
        ffn_grads[2],
        ffn_grads[3],
        ffn_grads[4],
        ffn_grads[5],
    )


def solution(mesh):
    return jax.shard_map(
        per_device,
        mesh=mesh,
        in_specs=(
            P(("wide", "narrow"), None),
            P(("wide", "narrow"), None),
            P(("wide", "narrow"), None),
            P(("wide", "narrow"), None),
            P(("wide", "narrow"), None),
            P(("wide", "narrow"), None),
            P(("wide", "narrow"), None),
            P(("wide", "narrow"), None),
            P(("wide", "narrow"), None),
            P(("wide", "narrow"), None),
            P(("wide", "narrow"), None),
            P(("wide", "narrow"), None),
            P(("wide", "narrow"), None),
            P(("wide", "narrow")),
            P(("wide", "narrow")),
            P(("wide", "narrow")),
            P(("wide", "narrow")),
            P(("wide", "narrow")),
            P(("wide", "narrow")),
            P(("wide", "narrow")),
            P(("wide", "narrow")),
            P(("wide", "narrow")),
            P(("wide", "narrow")),
        ),
        out_specs=(
            P(("wide", "narrow"), None),
            P(("wide", "narrow"), None),
            P(("wide", "narrow"), None),
            P(("wide", "narrow"), None),
            P(("wide", "narrow"), None),
            P(("wide", "narrow"), None),
            P(("wide", "narrow"), None),
            P(("wide", "narrow"), None),
            P(("wide", "narrow"), None),
            P(("wide", "narrow"), None),
            P(("wide", "narrow")),
            P(("wide", "narrow")),
            P(("wide", "narrow")),
            P(("wide", "narrow")),
            P(("wide", "narrow")),
            P(("wide", "narrow")),
            P(("wide", "narrow")),
            P(("wide", "narrow")),
            P(("wide", "narrow")),
            P(("wide", "narrow")),
        ),
        check_vma=False,
    )
```

profile of v0, /device:TPU:0, one launch (start us, length us, event | category | flops | bytes accessed | tf_op | source)
XLA Modules:
  0.0 2114.6 jit_solution(6977936958382268338)
XLA Ops:
  18.6 42.6 %all-reduce.28 = (bf16[1536]{0:T(1024)(128)(2,1)S(1)}, bf16[1536]{0:T(1024)(128)(2,1)S(1)}, bf16[512]{0:T(512)(128)(2,1)S(1)}, bf16[512]{0:T(512)(128)(2,1)S(1)}...) all-reduce(bf16[1536]{0:T(1024)(128)(2,1)S(1)} %dynamic-update-slic, ...), channel_id=1, replica_groups=mesh['wide'=16,'narrow'=2] {'wide','narrow'}, use_global_device_ids=true, to_apply=%add.1 | all-reduce | flops 8704 | bytes 34816
  68.4 74.8 %all_gather.63 = bf16[512,512]{1,0:T(8,128)(2,1)} all-gather(bf16[16,512]{1,0:T(8,128)(2,1)} %param.38), channel_id=1, replica_groups=mesh['wide'=16,'narrow'=2] {'wide','narrow'}, dimensions={0}, use_global_device_ids=true | all-gather | bytes 540672 | tf_op jit(solution)/shard_map/all_gather | solution.py:46
  143.2 71.9 %all_gather.68 = bf16[512,512]{1,0:T(8,128)(2,1)} all-gather(bf16[16,512]{1,0:T(8,128)(2,1)} %param.39), channel_id=1, replica_groups=mesh['wide'=16,'narrow'=2] {'wide','narrow'}, dimensions={0}, use_global_device_ids=true | all-gather | bytes 540672 | tf_op jit(solution)/shard_map/all_gather | solution.py:46
  215.1 75.0 %all_gather.69 = bf16[512,512]{1,0:T(8,128)(2,1)} all-gather(bf16[16,512]{1,0:T(8,128)(2,1)} %param.41), channel_id=1, replica_groups=mesh['wide'=16,'narrow'=2] {'wide','narrow'}, dimensions={0}, use_global_device_ids=true | all-gather | bytes 540672 | tf_op jit(solution)/shard_map/all_gather | solution.py:46
  372.2 75.2 %while.52 = (s32[]{:T(128)}, bf16[4,512,8,64]{1,3,2,0:T(8,128)(2,1)}, f32[4,8,512]{2,1,0:T(8,128)S(1)}, s32[4]{0:T(128)S(1)}, bf16[2,1024,8,64]{1,3,2,0:T(8,128)...) while((s32[]{:T(128)}, ...), condition=%wide.region_3.4_spmd, body=%wide.region_0.3_spmd.sunk | while | flops 1125642240 | bytes 81432872 | solution.py:166
  472.2 74.8 %while.53 = (s32[]{:T(128)}, bf16[4,512,8,64]{1,3,2,0:T(8,128)(2,1)}, f32[4,8,512]{2,1,0:T(8,128)S(1)}, s32[4]{0:T(128)S(1)}, bf16[2,1024,8,64]{1,3,2,0:T(8,128)...) while((s32[]{:T(128)}, ...), condition=%wide.region_9.10_spmd, body=%wide.region_6.9_spmd.sunk | while | flops 1124593664 | bytes 81414424 | solution.py:166
  555.8 14.4 multiply_convert_fusion.3
  595.6 16.4 fusion.148
  660.5 216.3 %while.54 = (s32[]{:T(128)}, bf16[4,512,8,64]{1,3,2,0:T(8,128)(2,1)}, f32[4,1024,8,64]{1,3,2,0:T(8,128)}, f32[4,1024,8,64]{1,3,2,0:T(8,128)}, s32[4]{0:T(128)S(1...) while((s32[]{:T(128)}, ...), condition=%wide.region_20.21_spmd, body=%wide.region_18.20_spmd.sunk | while | flops 2723409920 | bytes 212963632 | solution.py:205
  674.0 12.7 multiply_reduce_fusion.13
  686.7 11.5 multiply_convert_fusion.6
  728.0 12.7 multiply_reduce_fusion.13
  740.7 11.5 multiply_convert_fusion.6
  782.0 12.7 multiply_reduce_fusion.13
  794.7 11.5 multiply_convert_fusion.6
  836.0 12.7 multiply_reduce_fusion.13
  848.7 11.5 multiply_convert_fusion.6
  916.4 219.8 %while.55 = (s32[]{:T(128)}, bf16[4,512,8,64]{1,3,2,0:T(8,128)(2,1)}, f32[4,1024,8,64]{1,3,2,0:T(8,128)}, f32[4,1024,8,64]{1,3,2,0:T(8,128)}, s32[4]{0:T(128)S(1...) while((s32[]{:T(128)}, ...), condition=%wide.region_25.26_spmd, body=%wide.region_23.25_spmd.sunk | while | flops 2724458496 | bytes 212982064 | solution.py:205
  930.9 12.7 multiply_reduce_fusion.14
  985.7 12.7 multiply_reduce_fusion.14
  1040.5 12.7 multiply_reduce_fusion.14
  1095.3 12.7 multiply_reduce_fusion.14
  1141.4 12.3 copy.299
  1153.7 18.8 reshape.573
  1172.4 15.6 reduce_sum.330
  1196.9 12.3 copy.304
  1209.2 18.8 reshape.577
  1227.9 15.8 reduce_sum.332
  1248.6 12.3 copy.298
  1260.9 18.8 reshape.571
  1279.7 15.6 reduce_sum.329
  1304.1 12.3 copy.303
  1316.4 18.8 reshape.575
  1335.2 15.6 reduce_sum.331
  1390.1 180.2 %all-reduce.33.cloned.1.call-done = (bf16[16,2,16,1536]{3,2,1,0:T(8,128)(2,1)}, bf16[16,2,16,512]{3,2,1,0:T(8,128)(2,1)}, bf16[16,2,16,512]{3,2,1,0:T(8,128)(2,1...) async-done(((bf16[16,2,16,1536]{3,2,1,0:T(8,128)(2,1)}, ...) | async-done | bytes 8388624
  1619.5 11.7 reduce-scatter.63.cloned.1.call-done
  1631.9 11.9 reduce-scatter.55.cloned.1.call-done
  1644.4 11.7 reduce-scatter.57.cloned.1.call-done
  1656.8 11.8 reduce-scatter.53.cloned.1.call-done
  1669.3 11.7 reduce-scatter.59.cloned.1.call-done
  1681.7 11.7 reduce-scatter.65.cloned.1.call-done
  1694.1 61.7 %all-reduce.29 = (bf16[16,1,48]{2,1,0:T(2,128)(2,1)S(1)}, bf16[16,1,16]{2,1,0:T(2,128)(2,1)S(1)}, bf16[16,1,16]{2,1,0:T(2,128)(2,1)S(1)}, bf16[16,1,48]{2,1,0:T(...) all-reduce(bf16[16,1,48]{2,1,0:T(2,128)(2,1)S(1)} %copy.309, ...), channel_id=17, replica_groups=mesh['wide'=16,'narrow'=2] {'wide'}, use_global_device_ids=true, to_apply=%region_48.49.clone | all-reduce | flops 4352 | bytes 17408
  1771.4 38.4 %reduce-scatter.43.cloned.1.call-done = bf16[1,1,16,512]{3,2,1,0:T(8,128)(2,1)} async-done(((bf16[16,1,16,512]{3,2,1,0:T(8,128)(2,1)}), bf16[1,1,16,512]{3,2,1,0:T(8,128)(2,1)}) %reduce-scatter.43.cloned.1.call-update) | async-done | bytes 16400 | tf_op jit(solution)/shard_map/reduce_scatter | solution.py:85
  1811.2 56.4 %reduce-scatter.47.cloned.1.call-done = bf16[1,1,16,512]{3,2,1,0:T(8,128)(2,1)} async-done(((bf16[16,1,16,512]{3,2,1,0:T(8,128)(2,1)}), bf16[1,1,16,512]{3,2,1,0:T(8,128)(2,1)}) %reduce-scatter.47.cloned.1.call-update) | async-done | bytes 16400 | tf_op jit(solution)/shard_map/reduce_scatter | solution.py:85
  1868.9 57.1 %reduce-scatter.45.cloned.1.call-done = bf16[1,1,16,1024]{3,2,1,0:T(8,128)(2,1)} async-done(((bf16[16,1,16,1024]{3,2,1,0:T(8,128)(2,1)}), bf16[1,1,16,1024]{3,2,1,0:T(8,128)(2,1)}) %reduce-scatter.45.cloned.1.call-update) | async-done | bytes 32784 | tf_op jit(solution)/shard_map/reduce_scatter | solution.py:85
  1927.4 58.1 %reduce-scatter.39.cloned.1.call-done = bf16[1,1,16,1536]{3,2,1,0:T(8,128)(2,1)} async-done(((bf16[16,1,16,1536]{3,2,1,0:T(8,128)(2,1)}), bf16[1,1,16,1536]{3,2,1,0:T(8,128)(2,1)}) %reduce-scatter.39.cloned.1.call-update) | async-done | bytes 49168 | tf_op jit(solution)/shard_map/reduce_scatter | solution.py:85
  1986.9 58.6 %reduce-scatter.49.cloned.1.call-done = bf16[1,1,16,2048]{3,2,1,0:T(8,128)(2,1)} async-done(((bf16[16,1,16,2048]{3,2,1,0:T(8,128)(2,1)}), bf16[1,1,16,2048]{3,2,1,0:T(8,128)(2,1)}) %reduce-scatter.49.cloned.1.call-update) | async-done | bytes 65552 | tf_op jit(solution)/shard_map/reduce_scatter | solution.py:85
  2047.0 59.0 %reduce-scatter.51.cloned.1.call-done = bf16[1,1,64,512]{3,2,1,0:T(8,128)(2,1)} async-done(((bf16[16,1,64,512]{3,2,1,0:T(8,128)(2,1)}), bf16[1,1,64,512]{3,2,1,0:T(8,128)(2,1)}) %reduce-scatter.51.cloned.1.call-update) | async-done | bytes 65552 | tf_op jit(solution)/shard_map/reduce_scatter | solution.py:85
  (610 shorter events, 795.9 us)
Async XLA Ops:
  7.2 290.8 %copy-start = (bf16[2048,512]{1,0:T(8,128)(2,1)S(1)}, bf16[2048,512]{1,0:T(8,128)(2,1)}, u32[]{:S(2)}) copy-start(bf16[2048,512]{1,0:T(8,128)(2,1)} %param.32) | copy-start | bytes 6291460
  7.2 290.8 %all-gather.7.cloned.1.call-start = ((), (), s32[]{:S(2)}) async-start(), calls=%async_computation.18 | async-start | bytes 1081344 | tf_op jit(solution)/shard_map/all_gather | solution.py:46
  7.9 319.3 %all-gather.5.cloned.1.call-start = ((), (), s32[]{:S(2)}) async-start(), calls=%async_computation.17 | async-start | bytes 1622016 | tf_op jit(solution)/shard_map/all_gather | solution.py:46
  8.7 547.0 %all-gather.9.cloned.1.call-start = ((), (), s32[]{:S(2)}) async-start(), calls=%async_computation.19 | async-start | bytes 2162688 | tf_op jit(solution)/shard_map/all_gather | solution.py:46
  9.4 560.8 %all-gather.11.cloned.1.call-start = ((), (), s32[]{:S(2)}) async-start(), calls=%async_computation.20 | async-start | bytes 2162688 | tf_op jit(solution)/shard_map/all_gather | solution.py:46
  10.0 1560.2 %all-reduce.33.cloned.1.call-start = ((), (), s32[]{:S(2)}) async-start(), calls=%async_computation.38 | async-start | bytes 16777216
  555.7 14.5 copy-start.71
  595.5 16.5 copy-start.15
  612.0 9.6 copy-start.77
  664.3 9.7 copy-start.4
  686.7 15.4 copy-start.1
  718.3 9.7 copy-start.4
  740.7 15.4 copy-start.1
  772.3 9.7 copy-start.4
  794.7 15.4 copy-start.1
  826.3 9.7 copy-start.4
  848.7 15.4 copy-start.1
  921.2 9.7 copy-start.3
  943.6 15.4 copy-start.2
  976.0 9.7 copy-start.3
  998.4 15.4 copy-start.2
  1030.8 9.7 copy-start.3
  1053.2 15.4 copy-start.2
  1085.6 9.7 copy-start.3
  1108.0 15.4 copy-start.2
  1373.0 11.8 copy-start.66
  1373.1 14.8 copy-start.63
  1373.1 15.6 copy-start.80
  1373.1 16.2 copy-start.69
  1373.1 209.3 %reduce-scatter.71.cloned.1.call-start = ((), (), s32[]{:S(2)}) async-start(), calls=%async_computation.37 | async-start | bytes 12288 | tf_op jit(solution)/shard_map/reduce_scatter | solution.py:80
  1376.1 234.5 %reduce-scatter.69.cloned.1.call-start = ((), (), s32[]{:S(2)}) async-start(), calls=%async_computation.36 | async-start | bytes 12288 | tf_op jit(solution)/shard_map/reduce_scatter | solution.py:80
  1376.9 234.4 %reduce-scatter.61.cloned.1.call-start = ((), (), s32[]{:S(2)}) async-start(), calls=%async_computation.32 | async-start | bytes 12288 | tf_op jit(solution)/shard_map/reduce_scatter | solution.py:80
  1377.7 241.2 %reduce-scatter.67.cloned.1.call-start = ((), (), s32[]{:S(2)}) async-start(), calls=%async_computation.35 | async-start | bytes 12288 | tf_op jit(solution)/shard_map/reduce_scatter | solution.py:80
  1378.4 252.8 %reduce-scatter.63.cloned.1.call-start = ((), (), s32[]{:S(2)}) async-start(), calls=%async_computation.33 | async-start | bytes 12288 | tf_op jit(solution)/shard_map/reduce_scatter | solution.py:80
  1379.2 264.5 %reduce-scatter.55.cloned.1.call-start = ((), (), s32[]{:S(2)}) async-start(), calls=%async_computation.29 | async-start | bytes 12288 | tf_op jit(solution)/shard_map/reduce_scatter | solution.py:80
  1380.0 276.1 %reduce-scatter.57.cloned.1.call-start = ((), (), s32[]{:S(2)}) async-start(), calls=%async_computation.30 | async-start | bytes 12288 | tf_op jit(solution)/shard_map/reduce_scatter | solution.py:80
  1382.7 197.3 %copy-start.79 = (u32[32]{0:T(128)S(1)}, u32[32]{0:T(128)}, u32[]{:S(2)}) copy-start(u32[32]{0:T(128)} %constant.267) | copy-start | bytes 388
  1384.7 283.9 %reduce-scatter.53.cloned.1.call-start = ((), (), s32[]{:S(2)}) async-start(), calls=%async_computation.28 | async-start | bytes 12288 | tf_op jit(solution)/shard_map/reduce_scatter | solution.py:80
  1387.8 293.2 %reduce-scatter.59.cloned.1.call-start = ((), (), s32[]{:S(2)}) async-start(), calls=%async_computation.31 | async-start | bytes 12288 | tf_op jit(solution)/shard_map/reduce_scatter | solution.py:80
  1388.6 304.8 %reduce-scatter.65.cloned.1.call-start = ((), (), s32[]{:S(2)}) async-start(), calls=%async_computation.34 | async-start | bytes 12288 | tf_op jit(solution)/shard_map/reduce_scatter | solution.py:80
  1390.0 380.1 %reduce-scatter.41.cloned.1.call-start = ((), (), s32[]{:S(2)}) async-start(), calls=%async_computation.22 | async-start | bytes 278528 | tf_op jit(solution)/shard_map/reduce_scatter | solution.py:85
  1572.6 237.3 %reduce-scatter.43.cloned.1.call-start = ((), (), s32[]{:S(2)}) async-start(), calls=%async_computation.23 | async-start | bytes 278528 | tf_op jit(solution)/shard_map/reduce_scatter | solution.py:85
  1575.0 292.6 %reduce-scatter.47.cloned.1.call-start = ((), (), s32[]{:S(2)}) async-start(), calls=%async_computation.25 | async-start | bytes 278528 | tf_op jit(solution)/shard_map/reduce_scatter | solution.py:85
  1577.4 348.6 %reduce-scatter.45.cloned.1.call-start = ((), (), s32[]{:S(2)}) async-start(), calls=%async_computation.24 | async-start | bytes 557056 | tf_op jit(solution)/shard_map/reduce_scatter | solution.py:85
  1580.0 405.5 %reduce-scatter.39.cloned.1.call-start = ((), (), s32[]{:S(2)}) async-start(), calls=%async_computation.21 | async-start | bytes 835584 | tf_op jit(solution)/shard_map/reduce_scatter | solution.py:85
  1590.0 455.5 %reduce-scatter.49.cloned.1.call-start = ((), (), s32[]{:S(2)}) async-start(), calls=%async_computation.26 | async-start | bytes 1114112 | tf_op jit(solution)/shard_map/reduce_scatter | solution.py:85
  1597.6 7.1 copy-start.78
  1604.7 501.4 %reduce-scatter.51.cloned.1.call-start = ((), (), s32[]{:S(2)}) async-start(), calls=%async_computation.27 | async-start | bytes 1114112 | tf_op jit(solution)/shard_map/reduce_scatter | solution.py:85
  (89 other events, 313.8 us)
Sparse Core Ops, SparseCore 0:
  10.9 56.6 all-gather.6
  70.5 54.5 all-gather.4
  128.0 56.5 all-gather.8
  187.4 56.7 all-gather.10
  1373.2 197.0 all-reduce.32
  1572.3 10.0 reduce-scatter.70
  1584.5 9.7 reduce-scatter.68
  1597.1 9.7 reduce-scatter.60
  1609.0 9.7 reduce-scatter.66
  1621.4 9.7 reduce-scatter.62
  1634.0 9.7 reduce-scatter.54
  1646.3 9.7 reduce-scatter.56
  1658.9 9.7 reduce-scatter.52
  1671.3 9.7 reduce-scatter.58
  1683.6 9.7 reduce-scatter.64
  1696.8 55.2 reduce-scatter.40
  1755.4 54.3 reduce-scatter.42
  1813.2 54.3 reduce-scatter.46
  1871.2 54.8 reduce-scatter.44
  1929.8 55.5 reduce-scatter.38
  1989.1 56.3 reduce-scatter.48
  2049.6 56.3 reduce-scatter.50
where the time goes:
time: 2130 us; the launch traced here: 2110 us
  waiting for transfers between devices  590 us (28%)
  matrix products  484 us (23%)
  local copies, waits for them, and re-layouts  421 us (20%)
  blocking collectives  326 us (15%)
  other arithmetic  244 us (11%)
  loops' own time  33.7 us (2%)
    reduce_scatter x7, waiting for transfers between devices, reduce_each(): lax.psum_scatter(shortened(inner_sums), 'wide', scatter_dimension=0, tile...  328 us
    all_gather x3, blocking collectives, fetch(): lax.all_gather(shortened(pieces), ('wide', 'narrow'), axis=0, tiled=True)  222 us
    unnamed x23, waiting for transfers between devices  183 us
    dot_general x16, matrix products, masked_scores(): jnp.einsum('qhe,khe->hqk', query_block, keys_here, preferred_element_type...  141 us
    unnamed x2, blocking collectives  104 us
    convert_element_type x8, other arithmetic, one_block(): grad_scores = (prob_full * centred).astype(jnp.bfloat16)  91.8 us
    reduce_scatter x10, waiting for transfers between devices, reduce_each(): lax.psum_scatter(shortened(to_grid(grads)), 'narrow', scatter_dimension=1...  79.1 us
    dot_general x8, matrix products, one_block(): jnp.einsum('qhe,khe->hqk', grad_block, values_here, preferred_element_typ...  77.2 us
  transfers between devices with their start and end apart: 22, of which 15 were waited for; matrix products, arithmetic and copies ran while one was open for 16% of the time, Pallas kernels for 0%

commit v1 on v0

v1 whole, which is shorter than its diff:
```python
import functools

import jax
import jax.numpy as jnp
from jax import lax
from jax.experimental import pallas as pl
from jax.experimental.pallas import tpu as pltpu
from jax.sharding import PartitionSpec as P

HEADS = 8
MASKED = -1e30
BLOCK = 128
WINDOW = 256
NT = (((1,), (1,)), ((), ()))
TN = (((0,), (0,)), ((), ()))
NN = (((1,), (0,)), ((), ()))


def mxu(a, b, dims):
    return lax.dot_general(a, b, dims, preferred_element_type=jnp.float32)


def lane_masks(scale):
    lane = lax.broadcasted_iota(jnp.int32, (1, 128), 1)
    low = jnp.where(lane < 64, scale, 0.0).astype(jnp.bfloat16)
    high = jnp.where(lane < 64, 0.0, scale).astype(jnp.bfloat16)
    return low, high


def stacked(pair, masks):
    return jnp.concatenate([pair * masks[0], pair * masks[1]], axis=0)


def pick(both):
    sub = lax.broadcasted_iota(jnp.int32, (128, BLOCK), 0)
    return jnp.where(sub < 64, both[:, :BLOCK], both[:, BLOCK:])


def columns_of(row):
    return jnp.transpose(jnp.broadcast_to(row, (128, row.shape[1])))


def bias_of(seg_cols, seg_row, q0, start, low, causal):
    allowed = seg_cols == seg_row
    key = lax.broadcasted_iota(jnp.int32, (WINDOW, BLOCK), 0) + start
    if causal == "diag":
        query = lax.broadcasted_iota(jnp.int32, (WINDOW, BLOCK), 1) + q0
        allowed = allowed & (key <= query)
    elif causal == "left":
        allowed = allowed & (key < low)
    else:
        allowed = allowed & (key >= low)
    return jnp.where(allowed, 0.0, MASKED)


def window(causal, info, r, qb, c, length):
    if causal:
        end = (qb + 1) * BLOCK - c * WINDOW
        return pl.multiple_of(jnp.maximum(end - WINDOW, 0), BLOCK), end
    low = info[r, qb] + c * WINDOW
    return pl.multiple_of(jnp.minimum(low, length - WINDOW), 16), low


def forward_kernel(causal, first_ref, extra_ref, q_ref, k_ref, v_ref, qseg_ref, kseg_ref,
                   out_ref, lse_ref, cols, top, total, mix):
    r = pl.program_id(0)
    length = q_ref.shape[0]
    cols[...] = columns_of(kseg_ref[0])
    masks = lane_masks(0.125)

    def block(qb, _):
        q0 = pl.multiple_of(qb * BLOCK, BLOCK)
        seg_row = qseg_ref[0, :, pl.ds(q0, BLOCK)]

        def piece(c, kind):
            start, low = window(causal, first_ref, r, qb, c, length)
            bias = bias_of(cols[pl.ds(start, WINDOW), :], seg_row, q0, start, low, kind)
            bias = jnp.concatenate([bias, bias], axis=1)
            for p in range(4):
                lanes = slice(128 * p, 128 * p + 128)
                qs = stacked(q_ref[pl.ds(q0, BLOCK), lanes], masks)
                scores = mxu(k_ref[pl.ds(start, WINDOW), lanes], qs, NT) + bias
                yield p, scores, v_ref[pl.ds(start, WINDOW), lanes]

        for p, scores, values in piece(0, "diag" if causal else "from"):
            high = jnp.max(scores, axis=0, keepdims=True)
            weights = jnp.exp(scores - high)
            top[p] = high
            total[p] = jnp.sum(weights, axis=0, keepdims=True)
            mix[p] = pick(mxu(values, weights.astype(jnp.bfloat16), TN))

        def more(c, _):
            for p, scores, values in piece(c + 1, "left" if causal else "from"):
                old = top[p]
                high = jnp.maximum(old, jnp.max(scores, axis=0, keepdims=True))
                weights = jnp.exp(scores - high)
                fade = jnp.exp(old - high)
                top[p] = high
                total[p] = total[p] * fade + jnp.sum(weights, axis=0, keepdims=True)
                both = pick(jnp.broadcast_to(fade, (128, 2 * BLOCK)))
                mix[p] = mix[p] * both + pick(mxu(values, weights.astype(jnp.bfloat16), TN))
            return 0

        lax.fori_loop(0, extra_ref[r, qb], more, 0)
        for p in range(4):
            sums = total[p]
            inverse = pick(jnp.broadcast_to(1.0 / sums, (128, 2 * BLOCK)))
            out_ref[pl.ds(q0, BLOCK), 128 * p:128 * p + 128] = jnp.transpose(mix[p] * inverse).astype(jnp.bfloat16)
            lse = top[p] + jnp.log(sums)
            lse_ref[0, 2 * p:2 * p + 1, pl.ds(q0, BLOCK)] = lse[:, :BLOCK]
            lse_ref[0, 2 * p + 1:2 * p + 2, pl.ds(q0, BLOCK)] = lse[:, BLOCK:]
        return 0

    lax.fori_loop(0, length // BLOCK, block, 0)


def smem():
    return pl.BlockSpec(memory_space=pltpu.SMEM)


def attend_forward(first, extra, queries, keys, values, qseg, kseg, causal):
    rows, length = qseg.shape
    spec = lambda col: pl.BlockSpec((length, 512), lambda r, col=col: (r, col))
    seg = pl.BlockSpec((1, 1, length), lambda r: (r, 0, 0))
    return pl.pallas_call(
        functools.partial(forward_kernel, causal),
        grid=(rows,),
        in_specs=[smem(), smem(), spec(queries[1]), spec(keys[1]), spec(values[1]), seg, seg],
        out_specs=[spec(0), pl.BlockSpec((1, 8, length), lambda r: (r, 0, 0))],
        out_shape=[jax.ShapeDtypeStruct((rows * length, 512), jnp.bfloat16),
                   jax.ShapeDtypeStruct((rows, 8, length), jnp.float32)],
        scratch_shapes=[pltpu.VMEM((length, 128), jnp.float32),
                        pltpu.VMEM((4, 1, 2 * BLOCK), jnp.float32),
                        pltpu.VMEM((4, 1, 2 * BLOCK), jnp.float32),
                        pltpu.VMEM((4, 128, BLOCK), jnp.float32)],
        compiler_params=pltpu.CompilerParams(vmem_limit_bytes=40 << 20),
        cost_estimate=pl.CostEstimate(flops=2 * 10**9, bytes_accessed=10 << 20, transcendentals=0),
        name="attend_self" if causal else "attend_cross",
    )(first, extra, queries[0], keys[0], values[0], qseg[:, None, :].astype(jnp.float32), kseg[:, None, :].astype(jnp.float32))


def backward_kernel(causal, first_ref, extra_ref, q_ref, k_ref, v_ref, mix_ref, grad_ref, lse_ref, qseg_ref, kseg_ref,
                    dq_ref, dk_ref, dv_ref, cols, dk, dv, dq):
    r = pl.program_id(0)
    length = q_ref.shape[0]
    cols[...] = columns_of(kseg_ref[0])
    dk[...] = jnp.zeros_like(dk)
    dv[...] = jnp.zeros_like(dv)
    masks = lane_masks(0.125)
    ones = lane_masks(1.0)
    pair_rows = jnp.concatenate([ones[0], ones[1], jnp.zeros((14, 128), jnp.bfloat16)], axis=0)

    def block(qb, _):
        q0 = pl.multiple_of(qb * BLOCK, BLOCK)
        seg_row = qseg_ref[0, :, pl.ds(q0, BLOCK)]

        def piece(c, kind, first):
            start, low = window(causal, first_ref, r, qb, c, length)
            bias = bias_of(cols[pl.ds(start, WINDOW), :], seg_row, q0, start, low, kind)
            bias = jnp.concatenate([bias, bias], axis=1)
            for p in range(4):
                lanes = slice(128 * p, 128 * p + 128)
                qs = stacked(q_ref[pl.ds(q0, BLOCK), lanes], masks)
                grad = grad_ref[pl.ds(q0, BLOCK), lanes]
                gs = stacked(grad, ones)
                prod = grad.astype(jnp.float32) * mix_ref[pl.ds(q0, BLOCK), lanes].astype(jnp.float32)
                upper = prod.astype(jnp.bfloat16)
                lower = (prod - upper.astype(jnp.float32)).astype(jnp.bfloat16)
                delta = mxu(pair_rows, upper, NT) + mxu(pair_rows, lower, NT)
                delta = jnp.concatenate([delta[0:1], delta[1:2]], axis=1)
                lse = jnp.concatenate([lse_ref[0, 2 * p:2 * p + 1, pl.ds(q0, BLOCK)],
                                       lse_ref[0, 2 * p + 1:2 * p + 2, pl.ds(q0, BLOCK)]], axis=1)
                keys = k_ref[pl.ds(start, WINDOW), lanes]
                scores = mxu(keys, qs, NT) + bias
                probs = jnp.exp(scores - lse)
                dprobs = mxu(v_ref[pl.ds(start, WINDOW), lanes], gs, NT)
                dscores = (probs * (dprobs - delta)).astype(jnp.bfloat16)
                dv[pl.ds(start, WINDOW), lanes] += mxu(probs.astype(jnp.bfloat16), gs, NN)
                dk[pl.ds(start, WINDOW), lanes] += mxu(dscores, qs, NN)
                part = pick(mxu(keys, dscores, TN))
                if first:
                    dq[p] = part
                else:
                    dq[p] += part

        piece(0, "diag" if causal else "from", True)

        def more(c, _):
            piece(c + 1, "left" if causal else "from", False)
            return 0

        lax.fori_loop(0, extra_ref[r, qb], more, 0)
        for p in range(4):
            dq_ref[pl.ds(q0, BLOCK), 128 * p:128 * p + 128] = (jnp.transpose(dq[p]) * 0.125).astype(jnp.bfloat16)
        return 0

    lax.fori_loop(0, length // BLOCK, block, 0)
    dk_ref[...] = dk[...].astype(jnp.bfloat16)
    dv_ref[...] = dv[...].astype(jnp.bfloat16)


def attend_backward(first, extra, queries, keys, values, mix, grad, lse, qseg, kseg, causal):
    rows, length = qseg.shape
    spec = lambda col: pl.BlockSpec((length, 512), lambda r, col=col: (r, col))
    seg = pl.BlockSpec((1, 1, length), lambda r: (r, 0, 0))
    return pl.pallas_call(
        functools.partial(backward_kernel, causal),
        grid=(rows,),
        in_specs=[smem(), smem(), spec(queries[1]), spec(keys[1]), spec(values[1]), spec(0), spec(0),
                  pl.BlockSpec((1, 8, length), lambda r: (r, 0, 0)), seg, seg],
        out_specs=[spec(0)] * 3,
        out_shape=[jax.ShapeDtypeStruct((rows * length, 512), jnp.bfloat16)] * 3,
        scratch_shapes=[pltpu.VMEM((length, 128), jnp.float32),
                        pltpu.VMEM((length, 512), jnp.float32),
                        pltpu.VMEM((length, 512), jnp.float32),
                        pltpu.VMEM((4, 128, BLOCK), jnp.float32)],
        compiler_params=pltpu.CompilerParams(vmem_limit_bytes=48 << 20),
        cost_estimate=pl.CostEstimate(flops=6 * 10**9, bytes_accessed=16 << 20, transcendentals=0),
        name="back_self" if causal else "back_cross",
    )(first, extra, queries[0], keys[0], values[0], mix, grad, lse,
      qseg[:, None, :].astype(jnp.float32), kseg[:, None, :].astype(jnp.float32))


def plan_self(seg, positions):
    rows, length = seg.shape
    starts = jnp.arange(0, length, BLOCK, dtype=jnp.int32)
    begin = starts[None, :] - positions[:, ::BLOCK]
    left = jnp.maximum(starts[None, :] + BLOCK - WINDOW - begin, 0)
    return jnp.zeros_like(begin), (left + WINDOW - 1) // WINDOW


def plan_cross(tseg, sseg):
    last = jnp.int32(1 << 20)
    tkey = jnp.where(tseg == 0, last, tseg)
    skey = jnp.where(sseg == 0, last, sseg)
    low = jnp.sum(skey[:, None, :] < tkey[:, ::BLOCK, None], axis=2, dtype=jnp.int32)
    high = jnp.sum(skey[:, None, :] <= tkey[:, BLOCK - 1::BLOCK, None], axis=2, dtype=jnp.int32)
    first = (low // 16) * 16
    return first, jnp.maximum((high - first + WINDOW - 1) // WINDOW - 1, 0)


AXES = ("wide", "narrow")


class Net:
    def __init__(self):
        self.wide = lax.axis_size("wide")
        self.narrow = lax.axis_size("narrow")
        self.count = self.wide * self.narrow
        self.wide_bits = self.wide.bit_length() - 1
        self.narrow_bits = self.narrow.bit_length() - 1
        self.bits = self.wide_bits + self.narrow_bits
        self.me = lax.axis_index("wide") * self.narrow + lax.axis_index("narrow")

    def orders(self):
        n = self.narrow_bits
        inner = list(range(n))
        core = [n] if self.wide_bits else []
        second = [n + 1] if self.wide_bits > 1 else []
        far = list(range(self.bits - 1, n + 1, -1))
        return far + inner + second + core, far + second + inner + core

    def exchange(self, x, bit):
        if bit < self.narrow_bits:
            return lax.ppermute(x, "narrow", [(i, i ^ (1 << bit)) for i in range(self.narrow)])
        bit -= self.narrow_bits
        return lax.ppermute(x, "wide", [(i, i ^ (1 << bit)) for i in range(self.wide)])

    def gather(self, x, order):
        late = 2 if len(order) >= 2 else 0
        for bit in order[:len(order) - late]:
            x = jnp.concatenate([x, self.exchange(x, bit)], axis=0)
        pieces = [x]
        for bit in order[len(order) - late:]:
            pieces = pieces + [self.exchange(piece, bit) for piece in pieces]
        return pieces

    def masks(self, order):
        return [sum(((r >> s) & 1) << bit for s, bit in enumerate(order)) for r in range(self.count)]

    def reduce(self, keep, send, order):
        for s, bit in enumerate(order):
            got = self.exchange(send, bit)
            half = keep.shape[0] // 2
            if s + 1 == len(order):
                return keep.astype(jnp.float32) + got.astype(jnp.float32)
            send = (keep[half:].astype(jnp.float32) + got[half:].astype(jnp.float32)).astype(jnp.bfloat16)
            keep = (keep[:half].astype(jnp.float32) + got[:half].astype(jnp.float32)).astype(jnp.bfloat16)
        return keep


def arrange_kernel(plan, count, me_ref, *refs):
    chains, moves = plan
    n_in = sum(len(c[0]) for c in chains)
    ins, outs = refs[:n_in], refs[n_in:]
    me = me_ref[0]
    base = 0
    for c, (sizes, masks) in enumerate(chains):
        entry = 0
        for piece, size in enumerate(sizes):
            ref = ins[base + piece]
            for j in range(size):
                owner = me ^ masks[entry]
                entry += 1
                for chain, col, width, out, out_col, blocks, which in moves:
                    if chain != c:
                        continue
                    row = pl.multiple_of((owner * blocks + which) * 16, 16)
                    outs[out][pl.ds(row, 16), out_col:out_col + width] = ref[j, :, col:col + width]
        base += len(sizes)


def arrange(net, chains, moves, shapes):
    plan = ([([p.shape[0] for p in pieces], masks) for pieces, masks in chains], moves)
    pieces = [p for chain in chains for p in chain[0]]
    whole = pl.BlockSpec(memory_space=pltpu.VMEM)
    return pl.pallas_call(
        functools.partial(arrange_kernel, plan, net.count),
        in_specs=[smem()] + [whole] * len(pieces),
        out_specs=[whole] * len(shapes),
        out_shape=[jax.ShapeDtypeStruct(s, jnp.bfloat16) for s in shapes],
        compiler_params=pltpu.CompilerParams(vmem_limit_bytes=40 << 20),
        name="arrange",
    )(net.me[None].astype(jnp.int32), *pieces)


def spread_kernel(plan, me_ref, *refs):
    masks, moves, n_in = plan
    ins, outs = refs[:n_in], refs[n_in:]
    me = me_ref[0]
    for c, chain_masks in enumerate(masks):
        half = len(chain_masks) // 2
        for r, mask in enumerate(chain_masks):
            out = outs[2 * c + r // half]
            for chain, col, width, source, source_col, blocks, which in moves:
                if chain != c:
                    continue
                row = pl.multiple_of(((me ^ mask) * blocks + which) * 16, 16)
                out[r % half, :, col:col + width] = ins[source][pl.ds(row, 16), source_col:source_col + width].astype(jnp.bfloat16)


def spread(net, grads, masks, moves, widths):
    whole = pl.BlockSpec(memory_space=pltpu.VMEM)
    half = net.count // 2
    shapes = [(half, 16, w) for w in widths for _ in range(2)]
    return pl.pallas_call(
        functools.partial(spread_kernel, (masks, moves, len(grads))),
        in_specs=[smem()] + [whole] * len(grads),
        out_specs=[whole] * len(shapes),
        out_shape=[jax.ShapeDtypeStruct(s, jnp.bfloat16) for s in shapes],
        compiler_params=pltpu.CompilerParams(vmem_limit_bytes=48 << 20),
        name="spread",
    )(net.me[None].astype(jnp.int32), *grads)


SELF_MOVES = [(0, 0, 1024, 0, 0, 1, 0), (0, 1024, 128, 2, 0, 1, 0), (1, 0, 512, 0, 1024, 1, 0), (1, 512, 512, 1, 0, 1, 0)]
CROSS_MOVES = [(0, 0, 512, 0, 0, 1, 0), (0, 512, 512, 2, 0, 1, 0), (1, 0, 1024, 1, 0, 1, 0)]
FFN_MOVES = [(0, 0, 2048, 0, 0, 1, 0)] + [(1, 512 * b, 512, 1, 0, 4, b) for b in range(4)]


def fetch_all(net, big, small):
    if big[0].shape[0] % 16 or net.count < 4:
        whole = lax.all_gather((big, small), AXES, axis=0, tiled=True)
        return whole
    self_qkv, self_out, cross_query, cross_kv, cross_out, ffn_in, ffn_out = big
    line = jnp.concatenate(small)
    per_row = line.shape[0] // 16
    table = jnp.pad(line.reshape(16, per_row), ((0, 0), (0, 128 - per_row)))
    blocks = ffn_out.shape[0] // 16
    groups = [
        ((jnp.concatenate([self_qkv[:, :1024], table], axis=1), jnp.concatenate([self_qkv[:, 1024:], self_out], axis=1)),
         SELF_MOVES, [(512, 1536), (512, 512), (512, 128)]),
        ((jnp.concatenate([cross_query, cross_out], axis=1), cross_kv),
         CROSS_MOVES, [(512, 512), (512, 1024), (512, 512)]),
        ((ffn_in, jnp.concatenate([ffn_out[16 * b:16 * b + 16] for b in range(blocks)], axis=1)),
         FFN_MOVES, [(512, 2048), (2048, 512)]),
    ]
    orders = net.orders()
    results = []
    for shards, moves, shapes in groups:
        chains = [(net.gather(shard[None], order), net.masks(order)) for shard, order in zip(shards, orders)]
        results.extend(arrange(net, chains, moves, shapes))
    qkv, s_out, gathered, c_query, c_kv, c_out, f_in, f_out = results
    lines = gathered[:, :per_row].reshape(net.count, 16 * per_row)
    vectors, at = [], 0
    for part in small:
        vectors.append(lines[:, at:at + part.shape[0]].reshape(-1))
        at += part.shape[0]
    return (qkv, s_out, c_query, c_kv, c_out, f_in, f_out), tuple(vectors)


def reduce_group(net, grads, moves, widths):
    if grads[0].shape[0] // net.count % 16 or net.count < 4:
        return tuple(lax.psum_scatter(g.astype(jnp.bfloat16), AXES, scatter_dimension=0, tiled=True).astype(jnp.float32) for g in grads)
    orders = [order[::-1] for order in net.orders()]
    masks = []
    for order in orders:
        n = len(order)
        masks.append([sum(((r >> (n - 1 - s)) & 1) << bit for s, bit in enumerate(order)) for r in range(net.count)])
    halves = spread(net, grads, masks, moves, widths)
    sums = [net.reduce(halves[2 * c], halves[2 * c + 1], orders[c])[0] for c in range(2)]
    results = []
    for g, grad in enumerate(grads):
        rows = grad.shape[0] // net.count
        parts = sorted((m for m in moves if m[3] == g), key=lambda m: (m[6], m[4]))
        cols = [sums[m[0]][:, m[1]:m[1] + m[2]] for m in parts]
        results.append(cols[0] if len(cols) == 1 else jnp.concatenate(cols, axis=0 if rows > 16 else 1))
    return tuple(results)


def reduce_small(net, grads):
    rows = jnp.concatenate([g.reshape(net.count, -1) for g in grads], axis=1).astype(jnp.bfloat16)
    if net.count < 4:
        total = lax.psum_scatter(rows, AXES, scatter_dimension=0, tiled=True).astype(jnp.float32)
    else:
        order = list(range(net.bits - 1, -1, -1))
        half = net.count // 2
        bit = net.me >> (net.bits - 1)
        keep = lax.dynamic_slice_in_dim(rows, bit * half, half)
        send = lax.dynamic_slice_in_dim(rows, (1 - bit) * half, half)
        for s, b in enumerate(order):
            got = net.exchange(send, b)
            total = keep.astype(jnp.float32) + got.astype(jnp.float32)
            if s + 1 < len(order):
                half //= 2
                bit = (net.me >> order[s + 1]) & 1
                low = total.astype(jnp.bfloat16)
                keep = lax.dynamic_slice_in_dim(low, bit * half, half)
                send = lax.dynamic_slice_in_dim(low, (1 - bit) * half, half)
    line, out, at = total.reshape(-1), [], 0
    for g in grads:
        size = g.shape[0] // net.count
        out.append(line[at:at + size])
        at += size
    return tuple(out)


EPSILON = 1e-05


def matmul_plain(a, b):
    return mxu(a, b, NN)


def matmul_left_t(a, b):
    return mxu(a, b, TN)


def matmul_right_t(a, b):
    return mxu(a, b, NT)


def column_sums(values):
    return jnp.sum(values, axis=0, dtype=jnp.float32)


def norm_forward(hidden, gain, shift):
    average = jnp.mean(hidden, axis=-1, keepdims=True)
    centred = hidden - average
    inverse = lax.rsqrt(jnp.mean(centred * centred, axis=-1, keepdims=True) + EPSILON)
    normed = centred * inverse
    return (normed * gain + shift, normed, inverse)


def norm_backward(grad_in, normed, inverse, gain):
    gain_grad = jnp.sum(grad_in * normed, axis=0)
    shift_grad = jnp.sum(grad_in, axis=0)
    scaled = grad_in * gain
    hidden_grad = inverse * (
        scaled
        - jnp.mean(scaled, axis=-1, keepdims=True)
        - normed * jnp.mean(scaled * normed, axis=-1, keepdims=True)
    )
    return (gain_grad, shift_grad, hidden_grad)


def per_device(
    target, memory, out_grad, target_segments, source_segments, target_positions,
    self_qkv, self_out, cross_query, cross_kv, cross_out, ffn_in, ffn_out,
    self_bias, self_gain, self_shift, cross_bias, cross_gain, cross_shift,
    ffn_in_bias, ffn_out_bias, ffn_gain, ffn_shift,
):
    width = target.shape[1]
    f32 = lambda x: x.astype(jnp.float32)
    low = lambda x: x.astype(jnp.bfloat16)
    net = Net()
    zeros_row = jnp.zeros((width,), jnp.float32)
    self_first, self_extra = plan_self(target_segments, target_positions)
    cross_first, cross_extra = plan_cross(target_segments, source_segments)
    big, vectors = fetch_all(
        net,
        (self_qkv, self_out, cross_query, cross_kv, cross_out, ffn_in, ffn_out),
        (self_bias, self_gain, self_shift, cross_bias, cross_gain, cross_shift,
         ffn_in_bias, ffn_out_bias, ffn_gain, ffn_shift),
    )
    self_qkv, self_out, cross_query, cross_kv, cross_out, ffn_in, ffn_out = big
    (self_bias, self_gain, self_shift, cross_bias, cross_gain, cross_shift,
     ffn_in_bias, ffn_out_bias, ffn_gain, ffn_shift) = (f32(v) for v in vectors)

    joined_bias = jnp.concatenate([self_bias[:width], zeros_row, self_bias[width:2 * width]])
    projected = low(matmul_plain(target, self_qkv) + joined_bias)
    parts = ((projected, 0), (projected, 1), (projected, 2))
    self_mix, self_lse = attend_forward(self_first, self_extra, *parts, target_segments, target_segments, True)
    hidden_one = f32(target) + matmul_plain(self_mix, self_out) + self_bias[2 * width:]
    first_out, normed_one, inverse_one = norm_forward(hidden_one, self_gain, self_shift)
    first_low = low(first_out)
    cross_q = low(matmul_plain(first_low, cross_query) + cross_bias[:width])
    pairs = low(matmul_plain(memory, cross_kv) + jnp.concatenate([zeros_row, cross_bias[width:2 * width]]))
    cross_parts = ((cross_q, 0), (pairs, 0), (pairs, 1))
    cross_mix, cross_lse = attend_forward(cross_first, cross_extra, *cross_parts, target_segments, source_segments, False)
    hidden_two = first_out + matmul_plain(cross_mix, cross_out) + cross_bias[2 * width:]
    second_out, normed_two, inverse_two = norm_forward(hidden_two, cross_gain, cross_shift)
    second_low = low(second_out)
    pre = matmul_plain(second_low, ffn_in) + ffn_in_bias
    act = low(jax.nn.silu(pre))
    hidden_three = second_out + matmul_plain(act, ffn_out) + ffn_out_bias
    final, normed_three, inverse_three = norm_forward(hidden_three, ffn_gain, ffn_shift)
    output = low(final)

    gain_three, shift_three, back_three = norm_backward(f32(out_grad), normed_three, inverse_three, ffn_gain)
    low_three = low(back_three)
    ffn_out_grad = matmul_left_t(act, low_three)
    sig = jax.nn.sigmoid(pre)
    pre_grad = low(matmul_right_t(low_three, ffn_out) * sig * (1.0 + pre * (1.0 - sig)))
    ffn_in_grad = matmul_left_t(second_low, pre_grad)
    second_grad = back_three + matmul_right_t(pre_grad, ffn_in)
    ffn_grads = reduce_group(net, (ffn_in_grad, ffn_out_grad), FFN_MOVES, (2048, 2048))

    gain_two, shift_two, back_two = norm_backward(second_grad, normed_two, inverse_two, cross_gain)
    low_two = low(back_two)
    cross_out_grad = matmul_left_t(cross_mix, low_two)
    mix_grad = low(matmul_right_t(low_two, cross_out))
    cq, ck, cv = attend_backward(cross_first, cross_extra, *cross_parts, cross_mix, mix_grad, cross_lse,
                                 target_segments, source_segments, False)
    pair_grad = jnp.concatenate([ck, cv], axis=1)
    cross_query_grad = matmul_left_t(first_low, cq)
    cross_kv_grad = matmul_left_t(memory, pair_grad)
    memory_grad = low(matmul_right_t(pair_grad, cross_kv))
    cross_bias_grad = jnp.concatenate([column_sums(cq), column_sums(cv), column_sums(low_two)])
    first_grad = back_two + matmul_right_t(cq, cross_query)
    cross_grads = reduce_group(net, (cross_query_grad, cross_kv_grad, cross_out_grad), CROSS_MOVES, (1024, 1024))

    gain_one, shift_one, back_one = norm_backward(first_grad, normed_one, inverse_one, self_gain)
    low_one = low(back_one)
    self_out_grad = matmul_left_t(self_mix, low_one)
    mix_grad = low(matmul_right_t(low_one, self_out))
    sq, sk, sv = attend_backward(self_first, self_extra, *parts, self_mix, mix_grad, self_lse,
                                 target_segments, target_segments, True)
    joined = jnp.concatenate([sq, sk, sv], axis=1)
    self_qkv_grad = matmul_left_t(target, joined)
    self_bias_grad = jnp.concatenate([column_sums(sq), column_sums(sv), column_sums(low_one)])
    self_grads = reduce_group(net, (self_qkv_grad, self_out_grad),
                              [m for m in SELF_MOVES if m[3] != 2], (1024, 1024))
    target_grad = low(back_one + matmul_right_t(joined, self_qkv))
    small = reduce_small(net, (
        self_bias_grad, gain_one, shift_one, cross_bias_grad, gain_two, shift_two,
        column_sums(pre_grad), column_sums(low_three), gain_three, shift_three))
    return (output, target_grad, memory_grad, *self_grads, *cross_grads, *ffn_grads, *small)


def solution(mesh):
    both = ("wide", "narrow")
    matrix, vector = P(both, None), P(both)
    return jax.shard_map(
        per_device,
        mesh=mesh,
        in_specs=(matrix,) * 13 + (vector,) * 10,
        out_specs=(matrix,) * 10 + (vector,) * 10,
        check_vma=False,
    )
```

time: 2130 us -> 498 us (0.23)
  waiting for transfers between devices: 590 us -> 50.2 us
  matrix products: 484 us -> 113 us
  local copies, waits for them, and re-layouts: 421 us -> 58 us
  blocking collectives: 326 us -> 0 us
  other arithmetic: 244 us -> 41.7 us
  Pallas kernels: 0 us -> 128 us
  starting transfers between devices: 0.9 us -> 97.5 us
  loops' own time: 33.7 us -> 0 us
    reduce_scatter x17 -> x0, waiting for transfers between devices: 407 us -> none  [the longest x7 328 us: reduce_each(): lax.psum_scatter(shortened(inner_sums), 'wide', scatter_dimension=0, tile...]
    dot_general x77 -> x21, matrix products: 484 us -> 113 us  [mxu(): return lax.dot_general(a, b, dims, preferred_element_type=jnp.float32)]
    all_gather x3 -> x0, blocking collectives: 222 us -> none  [fetch(): lax.all_gather(shortened(pieces), ('wide', 'narrow'), axis=0, tiled=True)]
    unnamed x23 -> x0, waiting for transfers between devices: 183 us -> none
    reshape x20 -> x12, local copies, waits for them, and re-layouts: 153 us -> 2.63 us  [the longest x10 1.48 us: reduce_small(): g.reshape(net.count, -1)]
    while x92 -> x0, local copies, waits for them, and re-layouts: 135 us -> none  [the longest x6 60.1 us: attend_backward(): lax.map(one_block, (query_blocks, grad_blocks, logsum, info_blocks, row_o...]
    pallas_call x0 -> x10, Pallas kernels: none -> 128 us  [the longest x2 60.6 us: attend_backward(): pl.pallas_call(functools.partial(backward_kernel, causal), grid=(rows,),...]
    unnamed x2 -> x0, blocking collectives: 104 us -> none
  transfers between devices with their start and end apart: 22 -> 71, of which waited for: 15 -> 22; matrix products, arithmetic and copies ran while one was open for 16% -> 17% of each run, Pallas kernels for 0% -> 13%
where the time goes in v1:
time: 498 us; the launch traced here: 490 us
  Pallas kernels  128 us (26%)
  matrix products  113 us (23%)
  starting transfers between devices  97.5 us (20%)
  local copies, waits for them, and re-layouts  58 us (12%)
  waiting for transfers between devices  50.2 us (10%)
  other arithmetic  41.7 us (8%)
    dot_general x21, matrix products, mxu(): return lax.dot_general(a, b, dims, preferred_element_type=jnp.float32)  113 us
    ppermute x58, starting transfers between devices, exchange(): lax.ppermute(x, 'wide', [(i, i ^ 1 << bit) for i in range(self.wide)])  83.8 us
    pallas_call x2, Pallas kernels, attend_backward(): pl.pallas_call(functools.partial(backward_kernel, causal), grid=(rows,),...  60.6 us
    pallas_call x2, Pallas kernels, attend_forward(): pl.pallas_call(functools.partial(forward_kernel, causal), grid=(rows,), i...  52.1 us
    unnamed x168, local copies, waits for them, and re-layouts  40.6 us
    ppermute x58, waiting for transfers between devices, exchange(): lax.ppermute(x, 'wide', [(i, i ^ 1 << bit) for i in range(self.wide)])  28 us
    ppermute x13, waiting for transfers between devices, exchange(): lax.ppermute(x, 'narrow', [(i, i ^ 1 << bit) for i in range(self.narrow)])  22.2 us
    ppermute x13, starting transfers between devices, exchange(): lax.ppermute(x, 'narrow', [(i, i ^ 1 << bit) for i in range(self.narrow)])  13.7 us
  transfers between devices with their start and end apart: 71, of which 22 were waited for; matrix products, arithmetic and copies ran while one was open for 17% of the time, Pallas kernels for 13%

profile of v1, /device:TPU:0, one launch (start us, length us, event | category | flops | bytes accessed | tf_op | source)
XLA Modules:
  0.0 490.0 jit_solution(10660784937503536259)
XLA Ops:
  1.6 6.8 %concatenate.111 = bf16[272]{0:T(512)(128)(2,1)S(1)} concatenate(bf16[48]{0:T(256)(128)(2,1)} %param.36, bf16[16]{0:T(256)(128)(2,1)} %param.37, bf16[16]{0:T(256)(128)(2,1)} %param.38, bf16[48]{0:T(256)(128)(2,1)} %param.39, bf16[16]{0:T(256)(128)(2,1)} %param.40, bf16[16]{0:T(256)(128)(2,1)} %param.41, bf16[64]{0:T(256)(128)(2,1)} %param.42, bf16[16]{0:T(256)(128)(2,1)} %param.43, ...), dimensions={0} | concatenate | bytes 1088 | tf_op jit(solution)/shard_map/concatenate | solution.py:366
  8.5 4.1 collective-permute-start
  14.8 2.9 collective-permute-start.12
  18.5 3.0 collective-permute-start.30
  46.5 3.2 collective-permute-done.32
  51.4 5.7 %collective-permute-done.9.refs_5_ = bf16[8,16,1024]{2,1,0:T(8,128)(2,1)} collective-permute-done((bf16[8,16,1024]{2,1,0:T(8,128)(2,1)}, bf16[8,16,1024]{2,1,0:T(8,128)(2,1)}, u32[]{:S(2)}, u32[]{:S(2)}) %collective-permute-start.9) | collective-permute-done | bytes 262176 | tf_op jit(solution)/shard_map/ppermute | solution.py:265
  58.9 3.9 copy.67
  62.8 3.9 copy.71
  89.5 5.5 %fusion.q_ref.k_ref.v_ref = bf16[2048,1536]{1,0:T(8,128)(2,1)S(1)} fusion(bf16[2048,512]{1,0:T(8,128)(2,1)} %param.23, bf16[512,1536]{1,0:T(8,128)(2,1)} %copy-done.39, f32[1536]{0:T(1024)S(1)} %pad_maximum_fusion.20), kind=kOutput, calls=%fused_computation.5 | convolution fusion | flops 3227516928 | bytes 9967616 | tf_op jit(solution)/shard_map/dot_general | solution.py:20
  95.1 24.4 %attend_self.1 = (bf16[2048,512]{1,0:T(8,128)(2,1)S(1)}, f32[2,8,1024]{2,1,0:T(8,128)S(1)}) custom-call(s32[2,8]{1,0:T(2,128)S(1)} %broadcast_24_first_ref.2.first_ref, s32[2,8]{1,0:T(2,128)S(1)} %and_select_fusion.2.extra_ref, bf16[2048,1536]{1,0:T(8,128)(2,1)S(1)} %fusion.q_ref.k_ref.v_ref, bf16[2048,1536]{1,0:T(8,128)(2,1)S(1)} %fusion.q_ref.k_ref.v_ref, ...), custom_call_target="tpu_custom_call" | custom-call | flops 2000000000 | bytes 10485760 | tf_op jit(solution)/shard_map/attend_self/pallas_call | solution.py:125
  123.8 2.9 fusion.9
  128.8 2.4 fusion.8.k_ref.v_ref
  131.2 27.8 %attend_cross.1 = (bf16[2048,512]{1,0:T(8,128)(2,1)S(1)}, f32[2,8,1024]{2,1,0:T(8,128)S(1)}) custom-call(s32[2,8]{1,0:T(2,128)S(1)} %get-tuple-element.160.first_ref, s32[2,8]{1,0:T(2,128)S(1)} %get-tuple-element.159.extra_ref, bf16[2048,512]{1,0:T(8,128)(2,1)S(1)} %add_convert_fusion.4.q_ref, bf16[2048,1024]{1,0:T(8,128)(2,1)S(1)} %fusion.8.k_ref.v_ref, ...), custom_call_target="tpu_custom_call" | custom-call | flops 2000000000 | bytes 10485760 | tf_op jit(solution)/shard_map/attend_cross/pallas_call | solution.py:125
  159.0 4.0 fusion.43
  165.2 2.8 multiply_reduce_fusion.5
  170.2 12.7 %multiply_convert_fusion.1 = (bf16[2048,2048]{1,0:T(8,128)(2,1)}, f32[2048,2048]{1,0:T(8,128)}) fusion(f32[2048]{0:T(1024)S(1)} %reshape.264, bf16[512,2048]{1,0:T(8,128)(2,1)S(1)} %get-tuple-element.58, f32[2048,512]{0,1:T(8,128)S(1)} %copy-done.52, f32[512]{0:T(512)S(1)} %reshape.263, f32[512]{0:T(512)S(1)} %reshape.262, f32[2048]{0:T(1024)S(1)} %add_rsqrt_fusion.1, ...), kind=kOutput, calls=%fused_computation.1 | convolution fusion | flops 4325376000 | bytes 31485952 | tf_op jit(solution)/shard_map/dot_general | solution.py:20
  182.9 7.5 %fusion.44 = (f32[2048]{0:T(1024)S(1)}, f32[2048,512]{0,1:T(8,128)S(1)}) fusion(f32[512]{0:T(512)S(1)} %reshape.265, bf16[2048,2048]{1,0:T(8,128)(2,1)} %get-tuple-element.248, bf16[2048,512]{1,0:T(8,128)(2,1)S(1)} %get-tuple-element.59, f32[512]{0:T(512)S(1)} %reshape.263, f32[512]{0:T(512)S(1)} %reshape.262, f32[2048]{0:T(1024)S(1)} %add_rsqrt_fusion.1, ...), kind=kOutput, calls=%fused_computation.226 | convolution fusion | flops 4302305280 | bytes 18905088 | tf_op jit(solution)/shard_map/dot_general | solution.py:20
  192.1 3.4 fusion.7
  197.0 14.9 %fusion.45 = (bf16[2048]{0:T(1024)(128)(2,1)S(1)}, bf16[2048,2048]{1,0:T(8,128)(2,1)}) fusion(f32[2048,2048]{1,0:T(8,128)} %get-tuple-element.249, f32[2048]{0:T(1024)S(1)} %reshape.264, bf16[2048,512]{0,1:T(8,128)(2,1)S(1)} %get-tuple-element.154, bf16[2048,512]{1,0:T(8,128)(2,1)S(1)} %get-tuple-element.59), kind=kOutput, calls=%fused_computation.227 | convolution fusion | flops 4341102592 | bytes 29372416 | tf_op jit(solution)/shard_map/dot_general | solution.py:20
  211.9 10.7 %multiply_reduce_fusion = (bf16[512]{0:T(512)(128)(2,1)S(1)}, f32[2048]{0:T(1024)S(1)}, f32[2048]{0:T(1024)S(1)}, bf16[512]{0:T(512)(128)(2,1)S(1)}, f32[2048,512]{0,1:T(8,128)S(1)}) fusion(f32[2048,512]{0,1:T(8,128)} %get-tuple-element.247, f32[2048]{0:T(1024)S(1)} %add_rsqrt_fusion.1, f32[2048]{0:T(1024)S(1)} %broadcast_multiply_fusion.7, ...), kind=kOutput, calls=%fused_computation.16 | convolution fusion | flops 4313836544 | bytes 25237504 | tf_op jit(solution)/shard_map/dot_general | solution.py:20
  224.1 2.7 convolution_convert_fusion.2.grad_ref
  226.8 32.2 %back_cross.1 = (bf16[2048,512]{1,0:T(8,128)(2,1)S(1)}, bf16[2048,512]{1,0:T(8,128)(2,1)S(1)}, bf16[2048,512]{1,0:T(8,128)(2,1)}) custom-call(s32[2,8]{1,0:T(2,128)S(1)} %get-tuple-element.160.first_ref, s32[2,8]{1,0:T(2,128)S(1)} %get-tuple-element.159.extra_ref, bf16[2048,512]{1,0:T(8,128)(2,1)} %copy-done.7, bf16[2048,1024]{1,0:T(8,128)(2,1)} %copy-done.2, ...), custom_call_target="tpu_custom_call" | custom-call | flops 6000000000 | bytes 16777216 | tf_op jit(solution)/shard_map/back_cross/pallas_call | solution.py:206
  263.6 5.4 %multiply_reduce_fusion.1 = (bf16[512]{0:T(512)(128)(2,1)S(1)}, f32[2048]{0:T(1024)S(1)}, f32[2048]{0:T(1024)S(1)}, bf16[512]{0:T(512)(128)(2,1)S(1)}, f32[2048,512]{0,1:T(8,128)S(1)}) fusion(f32[2048,512]{0,1:T(8,128)} %copy-done.44, f32[2048]{0:T(1024)S(1)} %add_rsqrt_fusion.2, f32[2048]{0:T(1024)S(1)} %broadcast_multiply_fusion.8, f32[512]{0:T(512)S(1)} %reshape.259, ...), kind=kOutput, calls=%fused_computation.17 | convolution fusion | flops 1084222464 | bytes 15241216 | tf_op jit(solution)/shard_map/dot_general | solution.py:20
  269.0 9.8 %fusion.24.refs_0_ = f32[512,2048]{1,0:T(8,128)} fusion(bf16[2048,2048]{1,0:T(8,128)(2,1)} %get-tuple-element.255, f32[2048,512]{0,1:T(8,128)S(1)} %copy-done.54, f32[512]{0:T(512)S(1)} %reshape.263, f32[512]{0:T(512)S(1)} %reshape.262, f32[2048]{0:T(1024)S(1)} %add_rsqrt_fusion.1, f32[2048]{0:T(1024)S(1)} %broadcast_multiply_fusion.7), kind=kOutput, calls=%fused_computation.210 | convolution fusion | flops 4300210176 | bytes 16797696 | tf_op jit(solution)/shard_map/dot_general | solution.py:20
  278.9 6.7 %fusion.47.refs_1_ = f32[2048,512]{1,0:T(8,128)} fusion(bf16[2048,2048]{1,0:T(8,128)(2,1)S(1)} %bitcast.98, bf16[2048,512]{0,1:T(8,128)(2,1)S(1)} %copy-done.56), kind=kOutput, calls=%fused_computation.229 | convolution fusion | flops 4294967296 | bytes 14680064 | tf_op jit(solution)/shard_map/dot_general | solution.py:20
  287.1 2.7 convolution_convert_fusion.1.grad_ref
  289.8 28.4 %back_self.1 = (bf16[2048,512]{1,0:T(8,128)(2,1)S(1)}, bf16[2048,512]{1,0:T(8,128)(2,1)S(1)}, bf16[2048,512]{1,0:T(8,128)(2,1)}) custom-call(s32[2,8]{1,0:T(2,128)S(1)} %copy-done.36, s32[2,8]{1,0:T(2,128)S(1)} %and_select_fusion.2.extra_ref, bf16[2048,1536]{1,0:T(8,128)(2,1)} %copy-done.1, bf16[2048,1536]{1,0:T(8,128)(2,1)} %copy-done.1, ...), custom_call_target="tpu_custom_call" | custom-call | flops 6000000000 | bytes 16777216 | tf_op jit(solution)/shard_map/back_self/pallas_call | solution.py:206
  320.6 5.2 %convolution_bitcast_fusion.refs_0_ = f32[512,1536]{1,0:T(8,128)} fusion(bf16[2048,1536]{1,0:T(8,128)(2,1)S(1)} %get-tuple-element.167, bf16[2048,512]{1,0:T(8,128)(2,1)S(1)} %copy-done.59), kind=kOutput, calls=%fused_computation.40 | convolution fusion | flops 3221225472 | bytes 11534336 | tf_op jit(solution)/shard_map/dot_general | solution.py:20
  325.9 4.9 add_convert_fusion.2
  336.0 6.1 %convolution_bitcast_fusion.1.refs_1_ = f32[512,1024]{1,0:T(8,128)} fusion(bf16[2048,1024]{1,0:T(8,128)(2,1)} %copy-done.63, bf16[2048,512]{1,0:T(8,128)(2,1)S(1)} %copy-done), kind=kOutput, calls=%fused_computation.46 | convolution fusion | flops 2147483648 | bytes 8388608 | tf_op jit(solution)/shard_map/dot_general | solution.py:20
  342.2 3.8 convolution_convert_fusion
  346.0 3.8 collective-permute-start.67
  351.5 20.9 %collective-permute-start.68 = (bf16[4,272]{1,0:T(4,128)(2,1)S(1)}, bf16[4,272]{1,0:T(4,128)(2,1)S(1)}, u32[]{:S(2)}, u32[]{:S(2)}) collective-permute-start(bf16[4,272]{1,0:T(4,128)(2,1)S(1)} %constant_dynamic-slice_fusion.4), channel_id=1, source_target_pairs={{0,4},{2,6},{4,0},{6,2},{8,12},{10,14},{12,8},{14,10},{16,20},{18,... | collective-permute-start | bytes 6536 | tf_op jit(solution)/shard_map/ppermute | solution.py:267
  372.3 2.3 fusion.18.refs_1_
  374.6 12.4 %collective-permute-start.69 = (bf16[2,272]{1,0:T(2,128)(2,1)S(1)}, bf16[2,272]{1,0:T(2,128)(2,1)S(1)}, u32[]{:S(2)}, u32[]{:S(2)}) collective-permute-start(bf16[2,272]{1,0:T(2,128)(2,1)S(1)} %constant_dynamic-slice_fusion.2), channel_id=1, source_target_pairs={{0,2},{2,0},{4,6},{6,4},{8,10},{10,8},{12,14},{14,12},{16,18},{18,... | collective-permute-start | bytes 3272 | tf_op jit(solution)/shard_map/ppermute | solution.py:267
  388.3 5.2 %spread.5 = (bf16[16,16,2048]{2,1,0:T(8,128)(2,1)S(1)}, bf16[16,16,2048]{2,1,0:T(8,128)(2,1)}, bf16[16,16,2048]{2,1,0:T(8,128)(2,1)S(1)}, bf16[16,16,2048]{2,1,0:T(8,128)(2,1)}) custom-call(s32[1]{0:T(128)} %bitcast.me_ref, f32[512,2048]{1,0:T(8,128)} %fusion.24.refs_0_, f32[2048,512]{1,0:T(8,128)} %fusion.47.refs_1_), custom_call_target="tpu_custom_call" | custom-call | tf_op jit(solution)/shard_map/spread/pallas_call | solution.py:346
  395.1 2.8 spread.4
  400.0 3.9 copy.78
  404.0 4.1 copy.77
  420.6 3.0 collective-permute-done.52
  427.8 5.1 %collective-permute-done.37 = bf16[8,16,1024]{2,1,0:T(8,128)(2,1)S(1)} collective-permute-done((bf16[8,16,1024]{2,1,0:T(8,128)(2,1)S(1)}, bf16[8,16,1024]{2,1,0:T(8,128)(2,1)S(1)}, u32[]{:S(2)}, u32[]{:S(2)}) %collective-permute-start.37) | collective-permute-done | bytes 262176 | tf_op jit(solution)/shard_map/ppermute | solution.py:267
  435.7 2.2 collective-permute-done.48
  443.7 2.8 collective-permute-start.55
  447.5 2.6 collective-permute-start.40
  452.4 3.0 collective-permute-done.45
  461.4 7.4 %collective-permute-done.62 = bf16[8,16,2048]{2,1,0:T(8,128)(2,1)S(1)} collective-permute-done((bf16[8,16,2048]{2,1,0:T(8,128)(2,1)S(1)}, bf16[8,16,2048]{2,1,0:T(8,128)(2,1)S(1)}, u32[]{:S(2)}, u32[]{:S(2)}) %collective-permute-start.62) | collective-permute-done | bytes 524320 | tf_op jit(solution)/shard_map/ppermute | solution.py:265
  473.0 2.4 collective-permute-done.63
  484.3 2.2 collective-permute-done.65
  (438 shorter events, 141.1 us)
Async XLA Ops:
  8.5 19.7 %collective-permute-start = (bf16[1,16,1152]{2,1,0:T(8,128)(2,1)S(1)}, bf16[1,16,1152]{2,1,0:T(8,128)(2,1)S(1)}, u32[]{:S(2)}, u32[]{:S(2)}) collective-permute-start(bf16[1,16,1152]{2,1,0:T(8,128)(2,1)S(1)} %fusion.14), channel_id=1, source_target_pairs={{0,16},{2,18},{4,20},{6,22},{8,24},{10,26},{12,28},{14,30},{16,0},... | collective-permute-start | bytes 110600 | tf_op jit(solution)/shard_map/ppermute | solution.py:267
  14.0 11.2 %collective-permute-start.6 = (bf16[1,16,1024]{2,1,0:T(8,128)(2,1)S(1)}, bf16[1,16,1024]{2,1,0:T(8,128)(2,1)S(1)}, u32[]{:S(2)}, u32[]{:S(2)}) collective-permute-start(bf16[1,16,1024]{2,1,0:T(8,128)(2,1)S(1)} %maximum_bitcast_fusion.1), channel_id=1, source_target_pairs={{0,16},{2,18},{4,20},{6,22},{8,24},{10,26},{12,28},{14,30},{16,0},... | collective-permute-start | bytes 98312 | tf_op jit(solution)/shard_map/ppermute | solution.py:267
  14.8 10.5 %collective-permute-start.12 = (bf16[1,16,1024]{2,1,0:T(8,128)(2,1)S(1)}, bf16[1,16,1024]{2,1,0:T(8,128)(2,1)S(1)}, u32[]{:S(2)}, u32[]{:S(2)}) collective-permute-start(bf16[1,16,1024]{2,1,0:T(8,128)(2,1)S(1)} %maximum_bitcast_fusion.2), channel_id=1, source_target_pairs={{0,16},{2,18},{4,20},{6,22},{8,24},{10,26},{12,28},{14,30},{16,0},... | collective-permute-start | bytes 98312 | tf_op jit(solution)/shard_map/ppermute | solution.py:267
  17.7 9.5 %collective-permute-start.18 = (bf16[1,16,1024]{2,1,0:T(8,128)(2,1)}, bf16[1,16,1024]{2,1,0:T(8,128)(2,1)S(1)}, u32[]{:S(2)}, u32[]{:S(2)}) collective-permute-start(bf16[1,16,1024]{2,1,0:T(8,128)(2,1)} %bitcast.93), channel_id=1, source_target_pairs={{0,16},{2,18},{4,20},{6,22},{8,24},{10,26},{12,28},{14,30},{16,0},... | collective-permute-start | bytes 98312 | tf_op jit(solution)/shard_map/ppermute | solution.py:267
  18.5 11.6 %collective-permute-start.30 = (bf16[1,16,2048]{2,1,0:T(8,128)(2,1)S(1)}, bf16[1,16,2048]{2,1,0:T(8,128)(2,1)S(1)}, u32[]{:S(2)}, u32[]{:S(2)}) collective-permute-start(bf16[1,16,2048]{2,1,0:T(8,128)(2,1)S(1)} %maximum_bitcast_fusion), channel_id=1, source_target_pairs={{0,16},{2,18},{4,20},{6,22},{8,24},{10,26},{12,28},{14,30},{16,0},... | collective-permute-start | bytes 196616 | tf_op jit(solution)/shard_map/ppermute | solution.py:267
  25.2 8.4 %collective-permute-start.7 = (bf16[2,16,1024]{2,1,0:T(8,128)(2,1)S(1)}, bf16[2,16,1024]{2,1,0:T(8,128)(2,1)S(1)}, u32[]{:S(2)}, u32[]{:S(2)}) collective-permute-start(bf16[2,16,1024]{2,1,0:T(8,128)(2,1)S(1)} %pad_maximum_fusion.17), channel_id=1, source_target_pairs={{0,8},{2,10},{4,12},{6,14},{8,0},{10,2},{12,4},{14,6},{16,24},{18,... | collective-permute-start | bytes 196616 | tf_op jit(solution)/shard_map/ppermute | solution.py:267
  27.2 6.5 %collective-permute-start.13 = (bf16[2,16,1024]{2,1,0:T(8,128)(2,1)S(1)}, bf16[2,16,1024]{2,1,0:T(8,128)(2,1)S(1)}, u32[]{:S(2)}, u32[]{:S(2)}) collective-permute-start(bf16[2,16,1024]{2,1,0:T(8,128)(2,1)S(1)} %pad_maximum_fusion.18), channel_id=1, source_target_pairs={{0,8},{2,10},{4,12},{6,14},{8,0},{10,2},{12,4},{14,6},{16,24},{18,... | collective-permute-start | bytes 196616 | tf_op jit(solution)/shard_map/ppermute | solution.py:267
  28.2 7.2 %collective-permute-start.19 = (bf16[2,16,1024]{2,1,0:T(8,128)(2,1)S(1)}, bf16[2,16,1024]{2,1,0:T(8,128)(2,1)S(1)}, u32[]{:S(2)}, u32[]{:S(2)}) collective-permute-start(bf16[2,16,1024]{2,1,0:T(8,128)(2,1)S(1)} %pad_maximum_fusion.19), channel_id=1, source_target_pairs={{0,8},{2,10},{4,12},{6,14},{8,0},{10,2},{12,4},{14,6},{16,24},{18,... | collective-permute-start | bytes 196616 | tf_op jit(solution)/shard_map/ppermute | solution.py:267
  30.2 7.6 %collective-permute-start.1 = (bf16[2,16,1152]{2,1,0:T(8,128)(2,1)S(1)}, bf16[2,16,1152]{2,1,0:T(8,128)(2,1)S(1)}, u32[]{:S(2)}, u32[]{:S(2)}) collective-permute-start(bf16[2,16,1152]{2,1,0:T(8,128)(2,1)S(1)} %pad_maximum_fusion.16), channel_id=1, source_target_pairs={{0,8},{2,10},{4,12},{6,14},{8,0},{10,2},{12,4},{14,6},{16,24},{18,... | collective-permute-start | bytes 221192 | tf_op jit(solution)/shard_map/ppermute | solution.py:267
  30.7 7.7 %collective-permute-start.31 = (bf16[2,16,2048]{2,1,0:T(8,128)(2,1)S(1)}, bf16[2,16,2048]{2,1,0:T(8,128)(2,1)S(1)}, u32[]{:S(2)}, u32[]{:S(2)}) collective-permute-start(bf16[2,16,2048]{2,1,0:T(8,128)(2,1)S(1)} %pad_maximum_fusion.13), channel_id=1, source_target_pairs={{0,8},{2,10},{4,12},{6,14},{8,0},{10,2},{12,4},{14,6},{16,24},{18,... | collective-permute-start | bytes 393224 | tf_op jit(solution)/shard_map/ppermute | solution.py:267
  33.7 8.3 %collective-permute-start.8 = (bf16[4,16,1024]{2,1,0:T(8,128)(2,1)S(1)}, bf16[4,16,1024]{2,1,0:T(8,128)(2,1)S(1)}, u32[]{:S(2)}, u32[]{:S(2)}) collective-permute-start(bf16[4,16,1024]{2,1,0:T(8,128)(2,1)S(1)} %pad_maximum_fusion.9), channel_id=1, source_target_pairs={{0,4},{2,6},{4,0},{6,2},{8,12},{10,14},{12,8},{14,10},{16,20},{18,... | collective-permute-start | bytes 393224 | tf_op jit(solution)/shard_map/ppermute | solution.py:267
  35.4 8.8 %collective-permute-start.14 = (bf16[4,16,1024]{2,1,0:T(8,128)(2,1)S(1)}, bf16[4,16,1024]{2,1,0:T(8,128)(2,1)S(1)}, u32[]{:S(2)}, u32[]{:S(2)}) collective-permute-start(bf16[4,16,1024]{2,1,0:T(8,128)(2,1)S(1)} %pad_maximum_fusion.10), channel_id=1, source_target_pairs={{0,1},{1,0},{2,3},{3,2},{4,5},{5,4},{6,7},{7,6},{8,9},{9,8},{10,11... | collective-permute-start | bytes 393224 | tf_op jit(solution)/shard_map/ppermute | solution.py:265
  37.7 7.2 %collective-permute-start.20 = (bf16[4,16,1024]{2,1,0:T(8,128)(2,1)S(1)}, bf16[4,16,1024]{2,1,0:T(8,128)(2,1)S(1)}, u32[]{:S(2)}, u32[]{:S(2)}) collective-permute-start(bf16[4,16,1024]{2,1,0:T(8,128)(2,1)S(1)} %pad_maximum_fusion.11), channel_id=1, source_target_pairs={{0,4},{2,6},{4,0},{6,2},{8,12},{10,14},{12,8},{14,10},{16,20},{18,... | collective-permute-start | bytes 393224 | tf_op jit(solution)/shard_map/ppermute | solution.py:267
  38.4 7.2 %collective-permute-start.2 = (bf16[4,16,1152]{2,1,0:T(8,128)(2,1)S(1)}, bf16[4,16,1152]{2,1,0:T(8,128)(2,1)S(1)}, u32[]{:S(2)}, u32[]{:S(2)}) collective-permute-start(bf16[4,16,1152]{2,1,0:T(8,128)(2,1)S(1)} %pad_maximum_fusion.8), channel_id=1, source_target_pairs={{0,1},{1,0},{2,3},{3,2},{4,5},{5,4},{6,7},{7,6},{8,9},{9,8},{10,11... | collective-permute-start | bytes 442376 | tf_op jit(solution)/shard_map/ppermute | solution.py:265
  39.6 10.2 %collective-permute-start.32 = (bf16[4,16,2048]{2,1,0:T(8,128)(2,1)S(1)}, bf16[4,16,2048]{2,1,0:T(8,128)(2,1)S(1)}, u32[]{:S(2)}, u32[]{:S(2)}) collective-permute-start(bf16[4,16,2048]{2,1,0:T(8,128)(2,1)S(1)} %pad_maximum_fusion.7), channel_id=1, source_target_pairs={{0,4},{2,6},{4,0},{6,2},{8,12},{10,14},{12,8},{14,10},{16,20},{18,... | collective-permute-start | bytes 786440 | tf_op jit(solution)/shard_map/ppermute | solution.py:267
  42.1 9.3 %collective-permute-start.26 = (bf16[4,16,2048]{2,1,0:T(8,128)(2,1)S(1)}, bf16[4,16,2048]{2,1,0:T(8,128)(2,1)S(1)}, u32[]{:S(2)}, u32[]{:S(2)}) collective-permute-start(bf16[4,16,2048]{2,1,0:T(8,128)(2,1)S(1)} %pad_maximum_fusion.6), channel_id=1, source_target_pairs={{0,1},{1,0},{2,3},{3,2},{4,5},{5,4},{6,7},{7,6},{8,9},{9,8},{10,11... | collective-permute-start | bytes 786440 | tf_op jit(solution)/shard_map/ppermute | solution.py:265
  44.2 12.9 %collective-permute-start.9 = (bf16[8,16,1024]{2,1,0:T(8,128)(2,1)}, bf16[8,16,1024]{2,1,0:T(8,128)(2,1)}, u32[]{:S(2)}, u32[]{:S(2)}) collective-permute-start(bf16[8,16,1024]{2,1,0:T(8,128)(2,1)} %pad_maximum_fusion.3.refs_4_), channel_id=1, source_target_pairs={{0,1},{1,0},{2,3},{3,2},{4,5},{5,4},{6,7},{7,6},{8,9},{9,8},{10,11... | collective-permute-start | bytes 786440 | tf_op jit(solution)/shard_map/ppermute | solution.py:265
  45.0 13.0 %collective-permute-start.15 = (bf16[8,16,1024]{2,1,0:T(8,128)(2,1)S(1)}, bf16[8,16,1024]{2,1,0:T(8,128)(2,1)S(1)}, u32[]{:S(2)}, u32[]{:S(2)}) collective-permute-start(bf16[8,16,1024]{2,1,0:T(8,128)(2,1)S(1)} %pad_maximum_fusion.4.refs_0_), channel_id=1, source_target_pairs={{0,4},{2,6},{4,0},{6,2},{8,12},{10,14},{12,8},{14,10},{16,20},{18,... | collective-permute-start | bytes 786440 | tf_op jit(solution)/shard_map/ppermute | solution.py:267
  45.6 24.4 %collective-permute-start.16 = (bf16[8,16,1024]{2,1,0:T(8,128)(2,1)S(1)}, bf16[8,16,1024]{2,1,0:T(8,128)(2,1)S(1)}, u32[]{:S(2)}, u32[]{:S(2)}) collective-permute-start(bf16[8,16,1024]{2,1,0:T(8,128)(2,1)S(1)} %pad_maximum_fusion.4.refs_0_), channel_id=1, source_target_pairs={{0,2},{2,0},{4,6},{6,4},{8,10},{10,8},{12,14},{14,12},{16,18},{18,... | collective-permute-start | bytes 786440 | tf_op jit(solution)/shard_map/ppermute | solution.py:267
  49.8 19.7 %collective-permute-start.21 = (bf16[8,16,1024]{2,1,0:T(8,128)(2,1)S(1)}, bf16[8,16,1024]{2,1,0:T(8,128)(2,1)}, u32[]{:S(2)}, u32[]{:S(2)}) collective-permute-start(bf16[8,16,1024]{2,1,0:T(8,128)(2,1)S(1)} %pad_maximum_fusion.5.refs_4_), channel_id=1, source_target_pairs={{0,1},{1,0},{2,3},{3,2},{4,5},{5,4},{6,7},{7,6},{8,9},{9,8},{10,11... | collective-permute-start | bytes 786440 | tf_op jit(solution)/shard_map/ppermute | solution.py:265
  51.4 19.4 %collective-permute-start.22 = (bf16[8,16,1024]{2,1,0:T(8,128)(2,1)S(1)}, bf16[8,16,1024]{2,1,0:T(8,128)(2,1)}, u32[]{:S(2)}, u32[]{:S(2)}) collective-permute-start(bf16[8,16,1024]{2,1,0:T(8,128)(2,1)S(1)} %pad_maximum_fusion.5.refs_4_), channel_id=1, source_target_pairs={{0,2},{2,0},{4,6},{6,4},{8,10},{10,8},{12,14},{14,12},{16,18},{18,... | collective-permute-start | bytes 786440 | tf_op jit(solution)/shard_map/ppermute | solution.py:267
  57.1 14.1 %collective-permute-start.3 = (bf16[8,16,1152]{2,1,0:T(8,128)(2,1)S(1)}, bf16[8,16,1152]{2,1,0:T(8,128)(2,1)}, u32[]{:S(2)}, u32[]{:S(2)}) collective-permute-start(bf16[8,16,1152]{2,1,0:T(8,128)(2,1)S(1)} %pad_maximum_fusion.2.refs_0_), channel_id=1, source_target_pairs={{0,4},{2,6},{4,0},{6,2},{8,12},{10,14},{12,8},{14,10},{16,20},{18,... | collective-permute-start | bytes 884744 | tf_op jit(solution)/shard_map/ppermute | solution.py:267
  58.0 13.3 %collective-permute-start.17 = (bf16[8,16,1024]{2,1,0:T(8,128)(2,1)S(1)}, bf16[8,16,1024]{2,1,0:T(8,128)(2,1)}, u32[]{:S(2)}, u32[]{:S(2)}) collective-permute-start(bf16[8,16,1024]{2,1,0:T(8,128)(2,1)S(1)} %collective-permute-done.15.refs_1_), channel_id=1, source_target_pairs={{0,2},{2,0},{4,6},{6,4},{8,10},{10,8},{12,14},{14,12},{16,18},{18,... | collective-permute-start | bytes 786440 | tf_op jit(solution)/shard_map/ppermute | solution.py:267
  69.4 13.1 %collective-permute-start.10 = (bf16[8,16,1024]{2,1,0:T(8,128)(2,1)}, bf16[8,16,1024]{2,1,0:T(8,128)(2,1)S(1)}, u32[]{:S(2)}, u32[]{:S(2)}) collective-permute-start(bf16[8,16,1024]{2,1,0:T(8,128)(2,1)} %pad_maximum_fusion.3.refs_4_), channel_id=1, source_target_pairs={{0,2},{2,0},{4,6},{6,4},{8,10},{10,8},{12,14},{14,12},{16,18},{18,... | collective-permute-start | bytes 786440 | tf_op jit(solution)/shard_map/ppermute | solution.py:267
  70.7 11.9 %collective-permute-start.4 = (bf16[8,16,1152]{2,1,0:T(8,128)(2,1)S(1)}, bf16[8,16,1152]{2,1,0:T(8,128)(2,1)S(1)}, u32[]{:S(2)}, u32[]{:S(2)}) collective-permute-start(bf16[8,16,1152]{2,1,0:T(8,128)(2,1)S(1)} %pad_maximum_fusion.2.refs_0_), channel_id=1, source_target_pairs={{0,2},{2,0},{4,6},{6,4},{8,10},{10,8},{12,14},{14,12},{16,18},{18,... | collective-permute-start | bytes 884744 | tf_op jit(solution)/shard_map/ppermute | solution.py:267
  70.7 13.3 %collective-permute-start.11 = (bf16[8,16,1024]{2,1,0:T(8,128)(2,1)}, bf16[8,16,1024]{2,1,0:T(8,128)(2,1)S(1)}, u32[]{:S(2)}, u32[]{:S(2)}) collective-permute-start(bf16[8,16,1024]{2,1,0:T(8,128)(2,1)} %collective-permute-done.9.refs_5_), channel_id=1, source_target_pairs={{0,2},{2,0},{4,6},{6,4},{8,10},{10,8},{12,14},{14,12},{16,18},{18,... | collective-permute-start | bytes 786440 | tf_op jit(solution)/shard_map/ppermute | solution.py:267
  71.3 12.9 %collective-permute-start.5 = (bf16[8,16,1152]{2,1,0:T(8,128)(2,1)}, bf16[8,16,1152]{2,1,0:T(8,128)(2,1)S(1)}, u32[]{:S(2)}, u32[]{:S(2)}) collective-permute-start(bf16[8,16,1152]{2,1,0:T(8,128)(2,1)} %collective-permute-done.3.refs_1_), channel_id=1, source_target_pairs={{0,2},{2,0},{4,6},{6,4},{8,10},{10,8},{12,14},{14,12},{16,18},{18,... | collective-permute-start | bytes 884744 | tf_op jit(solution)/shard_map/ppermute | solution.py:267
  73.9 89.1 %collective-permute-start.33 = (bf16[8,16,2048]{2,1,0:T(8,128)(2,1)S(1)}, bf16[8,16,2048]{2,1,0:T(8,128)(2,1)}, u32[]{:S(2)}, u32[]{:S(2)}) collective-permute-start(bf16[8,16,2048]{2,1,0:T(8,128)(2,1)S(1)} %pad_maximum_fusion.1.refs_4_), channel_id=1, source_target_pairs={{0,1},{1,0},{2,3},{3,2},{4,5},{5,4},{6,7},{7,6},{8,9},{9,8},{10,11... | collective-permute-start | bytes 1572872 | tf_op jit(solution)/shard_map/ppermute | solution.py:265
  82.6 85.4 %collective-permute-start.34 = (bf16[8,16,2048]{2,1,0:T(8,128)(2,1)S(1)}, bf16[8,16,2048]{2,1,0:T(8,128)(2,1)}, u32[]{:S(2)}, u32[]{:S(2)}) collective-permute-start(bf16[8,16,2048]{2,1,0:T(8,128)(2,1)S(1)} %pad_maximum_fusion.1.refs_4_), channel_id=1, source_target_pairs={{0,2},{2,0},{4,6},{6,4},{8,10},{10,8},{12,14},{14,12},{16,18},{18,... | collective-permute-start | bytes 1572872 | tf_op jit(solution)/shard_map/ppermute | solution.py:267
  82.6 82.0 %collective-permute-start.27 = (bf16[8,16,2048]{2,1,0:T(8,128)(2,1)S(1)}, bf16[8,16,2048]{2,1,0:T(8,128)(2,1)}, u32[]{:S(2)}, u32[]{:S(2)}) collective-permute-start(bf16[8,16,2048]{2,1,0:T(8,128)(2,1)S(1)} %pad_maximum_fusion.refs_0_), channel_id=1, source_target_pairs={{0,4},{2,6},{4,0},{6,2},{8,12},{10,14},{12,8},{14,10},{16,20},{18,... | collective-permute-start | bytes 1572872 | tf_op jit(solution)/shard_map/ppermute | solution.py:267
  84.0 84.0 %collective-permute-start.28 = (bf16[8,16,2048]{2,1,0:T(8,128)(2,1)S(1)}, bf16[8,16,2048]{2,1,0:T(8,128)(2,1)}, u32[]{:S(2)}, u32[]{:S(2)}) collective-permute-start(bf16[8,16,2048]{2,1,0:T(8,128)(2,1)S(1)} %pad_maximum_fusion.refs_0_), channel_id=1, source_target_pairs={{0,2},{2,0},{4,6},{6,4},{8,10},{10,8},{12,14},{14,12},{16,18},{18,... | collective-permute-start | bytes 1572872 | tf_op jit(solution)/shard_map/ppermute | solution.py:267
  336.0 10.0 %collective-permute-start.66 = (bf16[16,272]{1,0:T(8,128)(2,1)S(1)}, bf16[16,272]{1,0:T(8,128)(2,1)S(1)}, u32[]{:S(2)}, u32[]{:S(2)}) collective-permute-start(bf16[16,272]{1,0:T(8,128)(2,1)S(1)} %constant_dynamic-slice_fusion.6), channel_id=1, source_target_pairs={{0,16},{2,18},{4,20},{6,22},{8,24},{10,26},{12,28},{14,30},{16,0},... | collective-permute-start | bytes 26120 | tf_op jit(solution)/shard_map/ppermute | solution.py:267
  351.5 23.1 %collective-permute-start.68 = (bf16[4,272]{1,0:T(4,128)(2,1)S(1)}, bf16[4,272]{1,0:T(4,128)(2,1)S(1)}, u32[]{:S(2)}, u32[]{:S(2)}) collective-permute-start(bf16[4,272]{1,0:T(4,128)(2,1)S(1)} %constant_dynamic-slice_fusion.4), channel_id=1, source_target_pairs={{0,4},{2,6},{4,0},{6,2},{8,12},{10,14},{12,8},{14,10},{16,20},{18,... | collective-permute-start | bytes 6536 | tf_op jit(solution)/shard_map/ppermute | solution.py:267
  374.6 19.8 %collective-permute-start.69 = (bf16[2,272]{1,0:T(2,128)(2,1)S(1)}, bf16[2,272]{1,0:T(2,128)(2,1)S(1)}, u32[]{:S(2)}, u32[]{:S(2)}) collective-permute-start(bf16[2,272]{1,0:T(2,128)(2,1)S(1)} %constant_dynamic-slice_fusion.2), channel_id=1, source_target_pairs={{0,2},{2,0},{4,6},{6,4},{8,10},{10,8},{12,14},{14,12},{16,18},{18,... | collective-permute-start | bytes 3272 | tf_op jit(solution)/shard_map/ppermute | solution.py:267
  394.4 62.3 %collective-permute-start.61 = (bf16[16,16,2048]{2,1,0:T(8,128)(2,1)}, bf16[16,16,2048]{2,1,0:T(8,128)(2,1)}, u32[]{:S(2)}, u32[]{:S(2)}) collective-permute-start(bf16[16,16,2048]{2,1,0:T(8,128)(2,1)} %get-tuple-element.79), channel_id=1, source_target_pairs={{0,2},{2,0},{4,6},{6,4},{8,10},{10,8},{12,14},{14,12},{16,18},{18,... | collective-permute-start | bytes 3145736 | tf_op jit(solution)/shard_map/ppermute | solution.py:267
  394.5 17.0 %collective-permute-start.70 = (bf16[1,272]{1,0:T(2,128)(2,1)S(1)}, bf16[1,272]{1,0:T(2,128)(2,1)S(1)}, u32[]{:S(2)}, u32[]{:S(2)}) collective-permute-start(bf16[1,272]{1,0:T(2,128)(2,1)S(1)} %constant_dynamic-slice_fusion), channel_id=1, source_target_pairs={{0,1},{1,0},{2,3},{3,2},{4,5},{5,4},{6,7},{7,6},{8,9},{9,8},{10,11... | collective-permute-start | bytes 1640 | tf_op jit(solution)/shard_map/ppermute | solution.py:265
  394.6 64.1 %collective-permute-start.56 = (bf16[16,16,2048]{2,1,0:T(8,128)(2,1)}, bf16[16,16,2048]{2,1,0:T(8,128)(2,1)}, u32[]{:S(2)}, u32[]{:S(2)}) collective-permute-start(bf16[16,16,2048]{2,1,0:T(8,128)(2,1)} %get-tuple-element.77), channel_id=1, source_target_pairs={{0,2},{2,0},{4,6},{6,4},{8,10},{10,8},{12,14},{14,12},{16,18},{18,... | collective-permute-start | bytes 3145736 | tf_op jit(solution)/shard_map/ppermute | solution.py:267
  399.5 13.8 %collective-permute-start.51 = (bf16[16,16,1024]{2,1,0:T(8,128)(2,1)}, bf16[16,16,1024]{2,1,0:T(8,128)(2,1)}, u32[]{:S(2)}, u32[]{:S(2)}) collective-permute-start(bf16[16,16,1024]{2,1,0:T(8,128)(2,1)} %get-tuple-element.75), channel_id=1, source_target_pairs={{0,2},{2,0},{4,6},{6,4},{8,10},{10,8},{12,14},{14,12},{16,18},{18,... | collective-permute-start | bytes 1572872 | tf_op jit(solution)/shard_map/ppermute | solution.py:267
  399.6 15.5 %collective-permute-start.46 = (bf16[16,16,1024]{2,1,0:T(8,128)(2,1)}, bf16[16,16,1024]{2,1,0:T(8,128)(2,1)}, u32[]{:S(2)}, u32[]{:S(2)}) collective-permute-start(bf16[16,16,1024]{2,1,0:T(8,128)(2,1)} %get-tuple-element.73), channel_id=1, source_target_pairs={{0,2},{2,0},{4,6},{6,4},{8,10},{10,8},{12,14},{14,12},{16,18},{18,... | collective-permute-start | bytes 1572872 | tf_op jit(solution)/shard_map/ppermute | solution.py:267
  411.5 6.6 %collective-permute-start.36 = (bf16[16,16,1024]{2,1,0:T(8,128)(2,1)S(1)}, bf16[16,16,1024]{2,1,0:T(8,128)(2,1)S(1)}, u32[]{:S(2)}, u32[]{:S(2)}) collective-permute-start(bf16[16,16,1024]{2,1,0:T(8,128)(2,1)S(1)} %get-tuple-element.69), channel_id=1, source_target_pairs={{0,2},{2,0},{4,6},{6,4},{8,10},{10,8},{12,14},{14,12},{16,18},{18,... | collective-permute-start | bytes 1572872 | tf_op jit(solution)/shard_map/ppermute | solution.py:267
  415.1 8.5 %collective-permute-start.52 = (bf16[8,16,1024]{2,1,0:T(8,128)(2,1)S(1)}, bf16[8,16,1024]{2,1,0:T(8,128)(2,1)S(1)}, u32[]{:S(2)}, u32[]{:S(2)}) collective-permute-start(bf16[8,16,1024]{2,1,0:T(8,128)(2,1)S(1)} %get-tuple-element.177), channel_id=1, source_target_pairs={{0,1},{1,0},{2,3},{3,2},{4,5},{5,4},{6,7},{7,6},{8,9},{9,8},{10,11... | collective-permute-start | bytes 786440 | tf_op jit(solution)/shard_map/ppermute | solution.py:265
  418.1 9.2 %collective-permute-start.47 = (bf16[8,16,1024]{2,1,0:T(8,128)(2,1)S(1)}, bf16[8,16,1024]{2,1,0:T(8,128)(2,1)S(1)}, u32[]{:S(2)}, u32[]{:S(2)}) collective-permute-start(bf16[8,16,1024]{2,1,0:T(8,128)(2,1)S(1)} %get-tuple-element.179), channel_id=1, source_target_pairs={{0,4},{2,6},{4,0},{6,2},{8,12},{10,14},{12,8},{14,10},{16,20},{18,... | collective-permute-start | bytes 786440 | tf_op jit(solution)/shard_map/ppermute | solution.py:267
  418.8 14.1 %collective-permute-start.37 = (bf16[8,16,1024]{2,1,0:T(8,128)(2,1)S(1)}, bf16[8,16,1024]{2,1,0:T(8,128)(2,1)S(1)}, u32[]{:S(2)}, u32[]{:S(2)}) collective-permute-start(bf16[8,16,1024]{2,1,0:T(8,128)(2,1)S(1)} %get-tuple-element.181), channel_id=1, source_target_pairs={{0,4},{2,6},{4,0},{6,2},{8,12},{10,14},{12,8},{14,10},{16,20},{18,... | collective-permute-start | bytes 786440 | tf_op jit(solution)/shard_map/ppermute | solution.py:267
  423.6 9.8 %collective-permute-start.42 = (bf16[8,16,1024]{2,1,0:T(8,128)(2,1)S(1)}, bf16[8,16,1024]{2,1,0:T(8,128)(2,1)S(1)}, u32[]{:S(2)}, u32[]{:S(2)}) collective-permute-start(bf16[8,16,1024]{2,1,0:T(8,128)(2,1)S(1)} %get-tuple-element.183), channel_id=1, source_target_pairs={{0,1},{1,0},{2,3},{3,2},{4,5},{5,4},{6,7},{7,6},{8,9},{9,8},{10,11... | collective-permute-start | bytes 786440 | tf_op jit(solution)/shard_map/ppermute | solution.py:265
  427.3 7.9 %collective-permute-start.53 = (bf16[4,16,1024]{2,1,0:T(8,128)(2,1)S(1)}, bf16[4,16,1024]{2,1,0:T(8,128)(2,1)S(1)}, u32[]{:S(2)}, u32[]{:S(2)}) collective-permute-start(bf16[4,16,1024]{2,1,0:T(8,128)(2,1)S(1)} %get-tuple-element.189), channel_id=1, source_target_pairs={{0,4},{2,6},{4,0},{6,2},{8,12},{10,14},{12,8},{14,10},{16,20},{18,... | collective-permute-start | bytes 393224 | tf_op jit(solution)/shard_map/ppermute | solution.py:267
  446.5 10.2 %collective-permute-start.50 = (bf16[1,16,1024]{2,1,0:T(8,128)(2,1)S(1)}, bf16[1,16,1024]{2,1,0:T(8,128)(2,1)S(1)}, u32[]{:S(2)}, u32[]{:S(2)}) collective-permute-start(bf16[1,16,1024]{2,1,0:T(8,128)(2,1)S(1)} %add_convert_fusion.47), channel_id=1, source_target_pairs={{0,16},{2,18},{4,20},{6,22},{8,24},{10,26},{12,28},{14,30},{16,0},... | collective-permute-start | bytes 98312 | tf_op jit(solution)/shard_map/ppermute | solution.py:267
  458.2 10.6 %collective-permute-start.62 = (bf16[8,16,2048]{2,1,0:T(8,128)(2,1)S(1)}, bf16[8,16,2048]{2,1,0:T(8,128)(2,1)S(1)}, u32[]{:S(2)}, u32[]{:S(2)}) collective-permute-start(bf16[8,16,2048]{2,1,0:T(8,128)(2,1)S(1)} %get-tuple-element.169), channel_id=1, source_target_pairs={{0,1},{1,0},{2,3},{3,2},{4,5},{5,4},{6,7},{7,6},{8,9},{9,8},{10,11... | collective-permute-start | bytes 1572872 | tf_op jit(solution)/shard_map/ppermute | solution.py:265
  460.3 11.2 %collective-permute-start.57 = (bf16[8,16,2048]{2,1,0:T(8,128)(2,1)S(1)}, bf16[8,16,2048]{2,1,0:T(8,128)(2,1)S(1)}, u32[]{:S(2)}, u32[]{:S(2)}) collective-permute-start(bf16[8,16,2048]{2,1,0:T(8,128)(2,1)S(1)} %get-tuple-element.171), channel_id=1, source_target_pairs={{0,4},{2,6},{4,0},{6,2},{8,12},{10,14},{12,8},{14,10},{16,20},{18,... | collective-permute-start | bytes 1572872 | tf_op jit(solution)/shard_map/ppermute | solution.py:267
  (104 other events, 1137.1 us)

commit v2 on v1

v2 whole, which is shorter than its diff:
```python
import functools

import jax
import jax.numpy as jnp
from jax import lax
from jax.experimental import pallas as pl
from jax.experimental.pallas import tpu as pltpu
from jax.sharding import PartitionSpec as P

MASKED = -1e30
EPSILON = 1e-05
BLOCK = 128
WINDOW = 256
UNIT = 16
AXES = ("wide", "narrow")
NT = (((1,), (1,)), ((), ()))
TN = (((0,), (0,)), ((), ()))
NN = (((1,), (0,)), ((), ()))
BF = jnp.bfloat16
F32 = jnp.float32


def mxu(a, b, dims=NN):
    return lax.dot_general(a, b, dims, preferred_element_type=F32)


def low(x):
    return x.astype(BF)


def wide(x):
    return x.astype(F32)


def shape_of(shape, dtype=BF):
    return jax.ShapeDtypeStruct(shape, dtype)


def smem():
    return pl.BlockSpec(memory_space=pltpu.SMEM)


def vmem():
    return pl.BlockSpec(memory_space=pltpu.VMEM)


def fixed(shape, *index):
    return pl.BlockSpec(shape, lambda i, index=index: index, pipeline_mode=pl.Buffered(1))


def tiled(rows, cols, col=0):
    return pl.BlockSpec((rows, cols), lambda i, col=col: (i, col))


def params(mib):
    return pltpu.CompilerParams(vmem_limit_bytes=mib << 20)


def cost(micros):
    return pl.CostEstimate(flops=int(micros * 1e9), bytes_accessed=1 << 20, transcendentals=0)


def lane_masks(scale):
    lane = lax.broadcasted_iota(jnp.int32, (1, 128), 1)
    return low(jnp.where(lane < 64, scale, 0.0)), low(jnp.where(lane < 64, 0.0, scale))


def stacked(pair, masks):
    return jnp.concatenate([pair * masks[0], pair * masks[1]], axis=0)


def pick(both):
    sub = lax.broadcasted_iota(jnp.int32, (128, BLOCK), 0)
    return jnp.where(sub < 64, both[:, :BLOCK], both[:, BLOCK:])


def columns_of(row):
    return jnp.transpose(jnp.broadcast_to(row, (128, row.shape[1])))


def bias_of(seg_cols, seg_row, q0, start, bound, kind):
    allowed = seg_cols == seg_row
    key = lax.broadcasted_iota(jnp.int32, (WINDOW, BLOCK), 0) + start
    if kind == "diag":
        allowed = allowed & (key <= lax.broadcasted_iota(jnp.int32, (WINDOW, BLOCK), 1) + q0)
    elif kind == "left":
        allowed = allowed & (key < bound)
    else:
        allowed = allowed & (key >= bound)
    return jnp.where(allowed, 0.0, MASKED)


def window(causal, first_ref, r, qb, c, length):
    if causal:
        end = (qb + 1) * BLOCK - c * WINDOW
        return pl.multiple_of(jnp.maximum(end - WINDOW, 0), BLOCK), end
    begin = first_ref[r, qb] + c * WINDOW
    return pl.multiple_of(jnp.minimum(begin, length - WINDOW), 16), begin


def lanes_at(offset, p):
    return slice(offset + 128 * p, offset + 128 * p + 128)


def attend(causal, r, first_ref, extra_ref, q, k, v, qseg_ref, cols, out_ref, lse_ref, top, total, mix):
    length = q[0].shape[0]
    masks = lane_masks(0.125)

    def block(qb, _):
        q0 = pl.multiple_of(qb * BLOCK, BLOCK)
        seg_row = qseg_ref[0, :, pl.ds(q0, BLOCK)]

        def pieces(c, kind):
            start, bound = window(causal, first_ref, r, qb, c, length)
            bias = bias_of(cols[pl.ds(start, WINDOW), :], seg_row, q0, start, bound, kind)
            bias = jnp.concatenate([bias, bias], axis=1)
            scores = []
            for p in range(4):
                qs = stacked(q[0][pl.ds(q0, BLOCK), lanes_at(q[1], p)], masks)
                keys = k[0][pl.ds(start, WINDOW), lanes_at(k[1], p)]
                scores.append(mxu(keys, qs, NT) + bias)
            return scores, [v[0][pl.ds(start, WINDOW), lanes_at(v[1], p)] for p in range(4)]

        scores, values = pieces(0, "diag" if causal else "from")
        for p in range(4):
            high = jnp.max(scores[p], axis=0, keepdims=True)
            weights = jnp.exp(scores[p] - high)
            top[p] = high
            total[p] = jnp.sum(weights, axis=0, keepdims=True)
            mix[p] = pick(mxu(values[p], low(weights), TN))

        def more(c, _):
            scores, values = pieces(c + 1, "left" if causal else "from")
            for p in range(4):
                old = top[p]
                high = jnp.maximum(old, jnp.max(scores[p], axis=0, keepdims=True))
                weights = jnp.exp(scores[p] - high)
                fade = jnp.exp(old - high)
                top[p] = high
                total[p] = total[p] * fade + jnp.sum(weights, axis=0, keepdims=True)
                mix[p] = mix[p] * pick(jnp.broadcast_to(fade, (128, 2 * BLOCK))) + pick(mxu(values[p], low(weights), TN))
            return 0

        lax.fori_loop(0, extra_ref[r, qb], more, 0)
        for p in range(4):
            sums = total[p]
            inverse = pick(jnp.broadcast_to(1.0 / sums, (128, 2 * BLOCK)))
            out_ref[pl.ds(q0, BLOCK), lanes_at(0, p)] = low(jnp.transpose(mix[p] * inverse))
            lse = top[p] + jnp.log(sums)
            lse_ref[0, 2 * p:2 * p + 1, pl.ds(q0, BLOCK)] = lse[:, :BLOCK]
            lse_ref[0, 2 * p + 1:2 * p + 2, pl.ds(q0, BLOCK)] = lse[:, BLOCK:]
        return 0

    lax.fori_loop(0, length // BLOCK, block, 0)


ATTEND_SCRATCH = lambda length: [
    pltpu.VMEM((length, 128), F32), pltpu.VMEM((4, 1, 2 * BLOCK), F32),
    pltpu.VMEM((4, 1, 2 * BLOCK), F32), pltpu.VMEM((4, 128, BLOCK), F32)]


def norm(hidden):
    average = jnp.mean(hidden, axis=-1, keepdims=True)
    centred = hidden - average
    inverse = lax.rsqrt(jnp.mean(centred * centred, axis=-1, keepdims=True) + EPSILON)
    return centred * inverse, inverse


def norm_back(grad, normed, inverse, gain):
    scaled = grad * gain
    return inverse * (scaled - jnp.mean(scaled, axis=-1, keepdims=True)
                      - normed * jnp.mean(scaled * normed, axis=-1, keepdims=True))


def sum_rows(x):
    return jnp.sum(wide(x), axis=0, keepdims=True)


S_BIAS, S_GAIN, S_SHIFT, C_BIAS, C_GAIN, C_SHIFT, I_BIAS, O_BIAS, F_GAIN, F_SHIFT = range(10)


def vec(ref, row, block=0, size=512):
    return ref[row:row + 1, block * size:(block + 1) * size]


def self_kernel(first_ref, extra_ref, x_ref, w_ref, vec_ref, seg_ref, qkv_ref, mix_ref, lse_ref, cols, *state):
    r = pl.program_id(0)
    cols[...] = columns_of(seg_ref[0])
    x = x_ref[...]
    qkv_ref[:, :512] = low(mxu(x, w_ref[:, :512]) + vec(vec_ref, S_BIAS, 0))
    qkv_ref[:, 512:1024] = low(mxu(x, w_ref[:, 512:1024]))
    qkv_ref[:, 1024:] = low(mxu(x, w_ref[:, 1024:]) + vec(vec_ref, S_BIAS, 1))
    attend(True, r, first_ref, extra_ref, (qkv_ref, 0), (qkv_ref, 512), (qkv_ref, 1024), seg_ref, cols, mix_ref, lse_ref, *state)


def self_forward(plan, x, w, vectors, seg):
    rows, _, length = seg.shape
    return pl.pallas_call(
        self_kernel, grid=(rows,),
        in_specs=[smem(), smem(), tiled(length, 512), fixed((512, 1536), 0, 0), fixed((16, 2048), 0, 0),
                  pl.BlockSpec((1, 1, length), lambda i: (i, 0, 0))],
        out_specs=[tiled(length, 1536), tiled(length, 512), pl.BlockSpec((1, 8, length), lambda i: (i, 0, 0))],
        out_shape=[shape_of((rows * length, 1536)), shape_of((rows * length, 512)), shape_of((rows, 8, length), F32)],
        scratch_shapes=ATTEND_SCRATCH(length), compiler_params=params(40), cost_estimate=cost(20), name="self_forward",
    )(*plan, x, w, vectors, seg)


def cross_kernel(first_ref, extra_ref, x_ref, mix_ref, mem_ref, wo_ref, wq_ref, wkv_ref, vec_ref, qseg_ref, kseg_ref,
                 hid_ref, q_ref, kv_ref, out_ref, lse_ref, cols, *state):
    r = pl.program_id(0)
    cols[...] = columns_of(kseg_ref[0])
    hidden = wide(x_ref[...]) + mxu(mix_ref[...], wo_ref[...]) + vec(vec_ref, S_BIAS, 2)
    hid_ref[...] = hidden
    first = low(norm(hidden)[0] * vec(vec_ref, S_GAIN) + vec(vec_ref, S_SHIFT))
    q_ref[...] = low(mxu(first, wq_ref[...]) + vec(vec_ref, C_BIAS, 0))
    mem = mem_ref[...]
    kv_ref[:, :512] = low(mxu(mem, wkv_ref[:, :512]))
    kv_ref[:, 512:] = low(mxu(mem, wkv_ref[:, 512:]) + vec(vec_ref, C_BIAS, 1))
    attend(False, r, first_ref, extra_ref, (q_ref, 0), (kv_ref, 0), (kv_ref, 512), qseg_ref, cols, out_ref, lse_ref, *state)


def cross_forward(plan, x, mix, mem, rest, vectors, qseg, kseg):
    rows, _, length = qseg.shape
    seg = pl.BlockSpec((1, 1, length), lambda i: (i, 0, 0))
    total = rows * length
    return pl.pallas_call(
        cross_kernel, grid=(rows,),
        in_specs=[smem(), smem(), tiled(length, 512), tiled(length, 512), tiled(length, 512),
                  fixed((512, 512), 0, 10), fixed((512, 512), 0, 11), fixed((512, 1024), 0, 4), fixed((16, 2048), 0, 0), seg, seg],
        out_specs=[tiled(length, 512), tiled(length, 512), tiled(length, 1024), tiled(length, 512),
                   pl.BlockSpec((1, 8, length), lambda i: (i, 0, 0))],
        out_shape=[shape_of((total, 512), F32), shape_of((total, 512)), shape_of((total, 1024)), shape_of((total, 512)),
                   shape_of((rows, 8, length), F32)],
        scratch_shapes=ATTEND_SCRATCH(length), compiler_params=params(48), cost_estimate=cost(25), name="cross_forward",
    )(*plan, x, mix, mem, rest, rest, rest, vectors, qseg, kseg)


def back_kernel(causal, row, first_ref, extra_ref, q_ref, k_ref, v_ref, mix_ref, grad_ref, lse_ref, qseg_ref, kseg_ref, *refs):
    dq_ref, dk_ref, dv_ref, cols, dk, dv, dq = refs[-7:]
    r = row
    length = q_ref.shape[0]
    cols[...] = columns_of(kseg_ref[0])
    dk[...] = jnp.zeros_like(dk)
    dv[...] = jnp.zeros_like(dv)
    masks = lane_masks(0.125)
    ones = lane_masks(1.0)
    pair_rows = jnp.concatenate([ones[0], ones[1], jnp.zeros((14, 128), BF)], axis=0)

    def block(qb, _):
        q0 = pl.multiple_of(qb * BLOCK, BLOCK)
        seg_row = qseg_ref[0, :, pl.ds(q0, BLOCK)]

        def piece(c, kind, first):
            start, bound = window(causal, first_ref, r, qb, c, length)
            bias = bias_of(cols[pl.ds(start, WINDOW), :], seg_row, q0, start, bound, kind)
            bias = jnp.concatenate([bias, bias], axis=1)
            here = pl.ds(start, WINDOW)
            parts, new_dv, new_dk = [], [], []
            for p in range(4):
                lanes = lanes_at(0, p)
                qs = stacked(q_ref[pl.ds(q0, BLOCK), lanes], masks)
                grad = grad_ref[pl.ds(q0, BLOCK), lanes]
                gs = stacked(grad, ones)
                prod = wide(grad) * wide(mix_ref[pl.ds(q0, BLOCK), lanes])
                upper = low(prod)
                delta = mxu(pair_rows, upper, NT) + mxu(pair_rows, low(prod - wide(upper)), NT)
                delta = jnp.concatenate([delta[0:1], delta[1:2]], axis=1)
                lse = jnp.concatenate([lse_ref[0, 2 * p:2 * p + 1, pl.ds(q0, BLOCK)],
                                       lse_ref[0, 2 * p + 1:2 * p + 2, pl.ds(q0, BLOCK)]], axis=1)
                keys = k_ref[here, lanes]
                probs = jnp.exp(mxu(keys, qs, NT) + bias - lse)
                dprobs = mxu(v_ref[here, lanes], gs, NT)
                dscores = low(probs * (dprobs - delta))
                new_dv.append(mxu(low(probs), gs))
                new_dk.append(mxu(dscores, qs))
                parts.append(pick(mxu(keys, dscores, TN)))
            for p in range(4):
                lanes = lanes_at(0, p)
                dv[here, lanes] += new_dv[p]
                dk[here, lanes] += new_dk[p]
                if first:
                    dq[p] = parts[p]
                else:
                    dq[p] += parts[p]

        piece(0, "diag" if causal else "from", True)

        def more(c, _):
            piece(c + 1, "left" if causal else "from", False)
            return 0

        lax.fori_loop(0, extra_ref[r, qb], more, 0)
        for p in range(4):
            dq_ref[pl.ds(q0, BLOCK), lanes_at(0, p)] = low(jnp.transpose(dq[p]) * 0.125)
        return 0

    lax.fori_loop(0, length // BLOCK, block, 0)
    dk_ref[...] = low(dk[...])
    dv_ref[...] = low(dv[...])


def attend_back(causal, row, plan, q, k, v, mix, grad, lse, qseg, kseg, before, after=()):
    rows, _, length = qseg.shape
    spec = lambda col: pl.BlockSpec((length, 512), lambda i, col=col: (row, col))
    seg = pl.BlockSpec((1, 1, length), lambda i: (row, 0, 0))
    out = pl.BlockSpec((length, 512), lambda i: (row, 0))
    extra = tuple(before) + tuple(after)
    return pl.pallas_call(
        functools.partial(back_kernel, causal, row), grid=(1,),
        in_specs=[smem(), smem(), spec(q[1]), spec(k[1]), spec(v[1]), spec(0), spec(0),
                  pl.BlockSpec((1, 8, length), lambda i: (row, 0, 0)), seg, seg]
        + [pl.BlockSpec(memory_space=pl.ANY)] * len(extra),
        out_specs=[out] * 3, out_shape=[shape_of((rows * length, 512))] * 3,
        input_output_aliases={10 + i: i for i in range(len(before))},
        scratch_shapes=[pltpu.VMEM((length, 128), F32), pltpu.VMEM((length, 512), F32),
                        pltpu.VMEM((length, 512), F32), pltpu.VMEM((4, 128, BLOCK), F32)],
        compiler_params=params(40), cost_estimate=cost(14), name="self_back" if causal else "cross_back",
    )(*plan, q[0], k[0], v[0], mix, grad, lse, qseg, kseg, *extra)


def emit(out_ref, col, acc, index_ref, acc_col, width, blocks=1, which=0):
    for r in range(512 // UNIT):
        row = pl.multiple_of((index_ref[r] * blocks + which) * UNIT, UNIT)
        out_ref[r, :, col:col + width] = low(acc[pl.ds(row, UNIT), acc_col:acc_col + width])


MID_TILE = 256
CHUNK = 512


def mid_kernel(index_a, index_b, hid_ref, mix_ref, grad_ref, win_ref, gout_ref, wco_ref, vec_ref,
               out_ref, h2_ref, mg_ref, a_ref, b_ref, co_ref, small_ref,
               wout, dwin, dwout, dwco, act, slope):
    step = pl.program_id(0)
    hidden_width = win_ref.shape[1]
    tokens = hid_ref.shape[0]

    @pl.when(step == 0)
    def _():
        for d in range(512 // UNIT):
            for b in range(4):
                wout[(4 * d + b) * UNIT:(4 * d + b + 1) * UNIT, :] = gout_ref[d * UNIT:(d + 1) * UNIT, 512 * b:512 * b + 512]
        dwin[...] = jnp.zeros_like(dwin)
        dwout[...] = jnp.zeros_like(dwout)
        dwco[...] = jnp.zeros_like(dwco)
        small_ref[...] = jnp.zeros_like(small_ref)

    chunks = [slice(c, c + CHUNK) for c in range(0, hidden_width, CHUNK)]
    first = norm(hid_ref[...])[0] * vec(vec_ref, S_GAIN) + vec(vec_ref, S_SHIFT)
    mix = mix_ref[...]
    normed2, inverse2 = norm(first + mxu(mix, wco_ref[...]) + vec(vec_ref, C_BIAS, 2))
    second = normed2 * vec(vec_ref, C_GAIN) + vec(vec_ref, C_SHIFT)
    second_low = low(second)
    hidden3 = second + vec(vec_ref, O_BIAS)
    for c in chunks:
        pre = mxu(second_low, win_ref[:, c]) + vec_ref[I_BIAS:I_BIAS + 1, c]
        sig = 1.0 / (1.0 + jnp.exp(-pre))
        active = low(pre * sig)
        act[:, c] = active
        slope[:, c] = sig * (1.0 + pre * (1.0 - sig))
        hidden3 += mxu(active, wout[c, :])
    normed3, inverse3 = norm(hidden3)
    out_ref[...] = low(normed3 * vec(vec_ref, F_GAIN) + vec(vec_ref, F_SHIFT))
    grad = wide(grad_ref[...])
    back3 = norm_back(grad, normed3, inverse3, vec(vec_ref, F_GAIN))
    b3 = low(back3)
    small_ref[1:2, :512] += sum_rows(b3)
    small_ref[2:3, :512] += sum_rows(grad * normed3)
    small_ref[3:4, :512] += sum_rows(grad)
    second_t = jnp.transpose(second_low)
    b3_t = jnp.transpose(b3)
    grad2 = back3
    for c in chunks:
        u = low(mxu(b3, wout[c, :], NT) * slope[:, c])
        dwin[:, c] += mxu(second_t, u)
        dwout[:, c] += mxu(b3_t, act[:, c])
        small_ref[0:1, c] += sum_rows(u)
        grad2 += mxu(u, win_ref[:, c], NT)
    h2 = norm_back(grad2, normed2, inverse2, vec(vec_ref, C_GAIN))
    h2_ref[...] = h2
    b2 = low(h2)
    small_ref[4:5, :512] += sum_rows(grad2 * normed2)
    small_ref[5:6, :512] += sum_rows(grad2)
    small_ref[6:7, :512] += sum_rows(b2)
    dwco[...] += mxu(jnp.transpose(mix), b2)
    mg_ref[...] = low(mxu(b2, wco_ref[...], NT))

    @pl.when(step == pl.num_programs(0) - 1)
    def _():
        emit(a_ref, 0, dwin, index_a, 0, hidden_width)
        for c in chunks:
            wout[c, :] = low(jnp.transpose(dwout[:, c]))
        for r in range(512 // UNIT):
            for b in range(4):
                row = pl.multiple_of((index_b[r] * 4 + b) * UNIT, UNIT)
                b_ref[r, :, 512 * b:512 * b + 512] = wout[pl.ds(row, UNIT), :]
        co_ref[...] = dwco[...]


def middle(index_a, index_b, hid, mix, grad, rest, vectors):
    total = hid.shape[0]
    t = MID_TILE
    blocks = 512 // UNIT
    return pl.pallas_call(
        mid_kernel, grid=(total // t,),
        in_specs=[smem(), smem(), tiled(t, 512), tiled(t, 512), tiled(t, 512),
                  fixed((512, 2048), 0, 0), fixed((512, 2048), 0, 1), fixed((512, 512), 0, 12), fixed((16, 2048), 0, 0)],
        out_specs=[tiled(t, 512), tiled(t, 512), tiled(t, 512), fixed((blocks, UNIT, 2048), 0, 0, 0),
                   fixed((blocks, UNIT, 2048), 0, 0, 0), fixed((512, 512), 0, 0), fixed((8, 2048), 0, 0)],
        out_shape=[shape_of((total, 512)), shape_of((total, 512), F32), shape_of((total, 512)),
                   shape_of((blocks, UNIT, 2048)), shape_of((blocks, UNIT, 2048)), shape_of((512, 512), F32), shape_of((8, 2048), F32)],
        scratch_shapes=[pltpu.VMEM((2048, 512), BF), pltpu.VMEM((512, 2048), F32), pltpu.VMEM((512, 2048), F32),
                        pltpu.VMEM((512, 512), F32), pltpu.VMEM((t, 2048), BF), pltpu.VMEM((t, 2048), F32)],
        compiler_params=params(56), cost_estimate=cost(40), name="middle",
    )(index_a, index_b, hid, mix, grad, rest, rest, rest, vectors)


def cross_dense_kernel(index_a, index_b, cq_ref, ck_ref, cv_ref, mem_ref, hid_ref, h2_ref, mix_ref,
                       wq_ref, wkv_ref, wo_ref, co_ref, vec_ref,
                       memgrad_ref, h1_ref, mg_ref, a_ref, b_ref, small_ref, dq, dkv, do):
    step = pl.program_id(0)

    @pl.when(step == 0)
    def _():
        dq[...] = jnp.zeros_like(dq)
        dkv[...] = jnp.zeros_like(dkv)
        do[...] = jnp.zeros_like(do)
        small_ref[...] = jnp.zeros_like(small_ref)

    cq, ck, cv = cq_ref[...], ck_ref[...], cv_ref[...]
    normed, inverse = norm(hid_ref[...])
    first = low(normed * vec(vec_ref, S_GAIN) + vec(vec_ref, S_SHIFT))
    grad1 = h2_ref[...] + mxu(cq, wq_ref[...], NT)
    h1 = norm_back(grad1, normed, inverse, vec(vec_ref, S_GAIN))
    h1_ref[...] = h1
    b1 = low(h1)
    mg_ref[...] = low(mxu(b1, wo_ref[...], NT))
    memgrad_ref[...] = low(mxu(ck, wkv_ref[:, :512], NT) + mxu(cv, wkv_ref[:, 512:], NT))
    dq[...] += mxu(jnp.transpose(first), cq)
    mem_t = jnp.transpose(mem_ref[...])
    dkv[:, :512] += mxu(mem_t, ck)
    dkv[:, 512:] += mxu(mem_t, cv)
    do[...] += mxu(jnp.transpose(mix_ref[...]), b1)
    small_ref[0:1, :] += sum_rows(cq)
    small_ref[1:2, :] += sum_rows(cv)
    small_ref[2:3, :] += sum_rows(grad1 * normed)
    small_ref[3:4, :] += sum_rows(grad1)
    small_ref[4:5, :] += sum_rows(b1)

    @pl.when(step == pl.num_programs(0) - 1)
    def _():
        emit(a_ref, 0, dq, index_a, 0, 512)
        emit(a_ref, 512, co_ref, index_a, 0, 512)
        emit(a_ref, 1024, do, index_a, 0, 256)
        emit(b_ref, 0, dkv, index_b, 0, 1024)
        emit(b_ref, 1024, do, index_b, 256, 256)


def cross_dense(index_a, index_b, grads, mem, hid, h2, mix, rest, dco, vectors):
    total = hid.shape[0]
    t = 256
    blocks = 512 // UNIT
    return pl.pallas_call(
        cross_dense_kernel, grid=(total // t,),
        in_specs=[smem(), smem()] + [tiled(t, 512)] * 7
        + [fixed((512, 512), 0, 11), fixed((512, 1024), 0, 4), fixed((512, 512), 0, 10), fixed((512, 512), 0, 0), fixed((16, 2048), 0, 0)],
        out_specs=[tiled(t, 512)] * 3 + [fixed((blocks, UNIT, 1280), 0, 0, 0)] * 2 + [fixed((8, 512), 0, 0)],
        out_shape=[shape_of((total, 512)), shape_of((total, 512), F32), shape_of((total, 512)),
                   shape_of((blocks, UNIT, 1280)), shape_of((blocks, UNIT, 1280)), shape_of((8, 512), F32)],
        scratch_shapes=[pltpu.VMEM((512, 512), F32), pltpu.VMEM((512, 1024), F32), pltpu.VMEM((512, 512), F32)],
        compiler_params=params(40), cost_estimate=cost(12), name="cross_dense",
    )(index_a, index_b, *grads, mem, hid, h2, mix, rest, rest, rest, dco, vectors)


VECTORS = (1536, 512, 512, 1536, 512, 512, 2048, 512, 512, 512)


def places(n, per, count, axis):
    shape = (1, n)
    at = wide(lax.broadcasted_iota(jnp.int32, shape, 1))
    owner = jnp.floor((at + 0.5) * (1.0 / per))
    return owner, at - owner * per


def one_hot(n, per):
    _, place = places(n, per, n // per, 1)
    return low(jnp.where(wide(lax.broadcasted_iota(jnp.int32, (128, n), 0)) == place, 1.0, 0.0))


def owned(n, per, count):
    owner, _ = places(n, per, count, 1)
    return wide(lax.broadcasted_iota(jnp.int32, (count, n), 0)) == owner


def self_grad_kernel(count, index_a, index_b, dq_ref, dk_ref, dv_ref, x_ref, mid_ref, small_ref, a_ref, b_ref, lines_ref, dw, table):
    step = pl.program_id(0)

    @pl.when(step == 0)
    def _():
        dw[...] = jnp.zeros_like(dw)
        lines_ref[...] = jnp.zeros_like(lines_ref)

    x_t = jnp.transpose(x_ref[...])
    dw[:, :512] += mxu(x_t, dq_ref[...])
    dw[:, 512:1024] += mxu(x_t, dk_ref[...])
    dw[:, 1024:] += mxu(x_t, dv_ref[...])
    lines_ref[S_BIAS:S_BIAS + 1, :512] += sum_rows(dq_ref[...])
    lines_ref[S_BIAS:S_BIAS + 1, 512:1024] += sum_rows(dv_ref[...])

    @pl.when(step == pl.num_programs(0) - 1)
    def _():
        emit(a_ref, 0, dw, index_a, 0, 768)
        emit(b_ref, 0, dw, index_b, 768, 768)
        for row, col, source, source_row in (
            (S_BIAS, 1024, small_ref, 4), (S_GAIN, 0, small_ref, 2), (S_SHIFT, 0, small_ref, 3),
            (C_BIAS, 0, small_ref, 0), (C_BIAS, 512, small_ref, 1), (C_BIAS, 1024, mid_ref, 6),
            (C_GAIN, 0, mid_ref, 4), (C_SHIFT, 0, mid_ref, 5),
            (O_BIAS, 0, mid_ref, 1), (F_GAIN, 0, mid_ref, 2), (F_SHIFT, 0, mid_ref, 3),
        ):
            lines_ref[row:row + 1, col:col + 512] = source[source_row:source_row + 1, :512]
        lines_ref[I_BIAS:I_BIAS + 1, :] = mid_ref[0:1, :]
        if count:
            table[...] = jnp.zeros_like(table)
            for n in (512, 1536, 2048):
                hot, mine = one_hot(n, n // count), owned(n, n // count, count)
                for j, size in enumerate(VECTORS):
                    if size == n:
                        line = jnp.broadcast_to(lines_ref[j:j + 1, :n], (count, n))
                        table[:, j, :] = mxu(low(jnp.where(mine, line, 0.0)), hot, NT)
            for r in range(count):
                a_ref[r, :, 768:896] = low(table[index_a[r]])


def self_grad(count, index_a, index_b, grads, x, mid_small, small):
    total = x.shape[0]
    t = 256
    blocks = 512 // UNIT
    return pl.pallas_call(
        functools.partial(self_grad_kernel, count), grid=(total // t,),
        in_specs=[smem(), smem()] + [tiled(t, 512)] * 4 + [fixed((8, 2048), 0, 0), fixed((8, 512), 0, 0)],
        out_specs=[fixed((blocks, UNIT, 896), 0, 0, 0), fixed((blocks, UNIT, 768), 0, 0, 0), fixed((16, 2048), 0, 0)],
        out_shape=[shape_of((blocks, UNIT, 896)), shape_of((blocks, UNIT, 768)), shape_of((16, 2048), F32)],
        scratch_shapes=[pltpu.VMEM((512, 1536), F32), pltpu.VMEM((max(count, 8), 16, 128), F32)],
        compiler_params=params(40), cost_estimate=cost(5), name="self_grad",
    )(index_a, index_b, *grads, x, mid_small, small)


def target_kernel(h1_ref, dq_ref, dk_ref, dv_ref, w_ref, *refs):
    out_ref = refs[-1]
    total = h1_ref[...] + mxu(dq_ref[...], w_ref[:, :512], NT)
    total += mxu(dk_ref[...], w_ref[:, 512:1024], NT)
    out_ref[...] = low(total + mxu(dv_ref[...], w_ref[:, 1024:], NT))


def target_grad(h1, grads, w, after=()):
    total = h1.shape[0]
    t = 512
    return pl.pallas_call(
        target_kernel, grid=(total // t,), in_specs=[tiled(t, 512)] * 4 + [fixed((512, 1536), 0, 0)]
        + [pl.BlockSpec(memory_space=pl.ANY)] * len(after),
        out_specs=tiled(t, 512), out_shape=shape_of((total, 512)), compiler_params=params(40), cost_estimate=cost(5), name="target_grad",
    )(h1, *grads, w, *after)


class Net:
    def __init__(self):
        self.wide = lax.axis_size("wide")
        self.narrow = lax.axis_size("narrow")
        self.count = self.wide * self.narrow
        self.wide_bits = self.wide.bit_length() - 1
        self.narrow_bits = self.narrow.bit_length() - 1
        self.bits = self.wide_bits + self.narrow_bits
        self.me = lax.axis_index("wide") * self.narrow + lax.axis_index("narrow")
        inner = list(range(self.narrow_bits))
        core, second = [self.narrow_bits], [self.narrow_bits + 1]
        far = list(range(self.narrow_bits + 2, self.bits))
        self.orders = (core + second + inner + far, core + inner + second + far)

    def exchange(self, x, bit):
        if bit < self.narrow_bits:
            return lax.ppermute(x, "narrow", [(i, i ^ (1 << bit)) for i in range(self.narrow)])
        bit -= self.narrow_bits
        return lax.ppermute(x, "wide", [(i, i ^ (1 << bit)) for i in range(self.wide)])

    def index(self, chain):
        order, n = self.orders[chain], self.bits
        mask = [sum(((r >> (n - 1 - s)) & 1) << bit for s, bit in enumerate(order)) for r in range(self.count)]
        return jnp.array(mask, jnp.int32) ^ self.me

    def gather_index(self, chain):
        order = self.orders[chain][::-1]
        mask = [sum(((r >> s) & 1) << bit for s, bit in enumerate(order)) for r in range(self.count)]
        return jnp.array(mask, jnp.int32) ^ self.me


def pack_kernel(*refs):
    vectors, (qkv, so, cq, ckv, co, fin, fout, a_ref, b_ref, rest_ref) = refs[:10], refs[10:20]
    lines, sem = refs[20:30], refs[30]
    moves = list(zip(vectors, lines))
    moves += [(qkv.at[:, :768], a_ref.at[0, :, :768]), (qkv.at[:, 768:], b_ref.at[0]), (fin, rest_ref.at[:, :2048])]
    moves += [(fout.at[UNIT * b:UNIT * b + UNIT, :], rest_ref.at[:, 2048 + 512 * b:2560 + 512 * b]) for b in range(4)]
    moves += [(ckv, rest_ref.at[:, 4096:5120]), (so, rest_ref.at[:, 5120:5632]),
              (cq, rest_ref.at[:, 5632:6144]), (co, rest_ref.at[:, 6144:])]
    copies = [pltpu.make_async_copy(src, dst, sem.at[i]) for i, (src, dst) in enumerate(moves)]
    for copy in copies:
        copy.start()
    for copy in copies:
        copy.wait()
    rows = []
    for v in lines:
        line = wide(v[...])
        rows.append(jnp.concatenate([line, jnp.zeros((1, 128 - line.shape[1]), F32)], axis=1))
    rows.append(jnp.zeros((6, 128), F32))
    a_ref[0, :, 768:] = low(jnp.concatenate(rows, axis=0))


def unpack_kernel(count, index_a, index_b, *refs):
    n = (len(refs) - 3) // 2
    pieces_a, pieces_b, (w_ref, vec_ref, table) = refs[:n], refs[n:2 * n], refs[2 * n:]
    for pieces, index, col, width in ((pieces_a, index_a, 0, 768), (pieces_b, index_b, 768, 768)):
        r = 0
        for piece in pieces:
            for j in range(piece.shape[0]):
                owner = index[r]
                w_ref[pl.ds(pl.multiple_of(owner * UNIT, UNIT), UNIT), col:col + width] = piece[j, :, :width]
                if col == 0:
                    table[owner] = wide(piece[j, :, 768:896])
                r += 1
    vec_ref[...] = jnp.zeros_like(vec_ref)
    for n in (512, 1536, 2048):
        hot, mine = one_hot(n, n // count), owned(n, n // count, count)
        for j, size in enumerate(VECTORS):
            if size == n:
                spread = mxu(low(table[:, j, :]), hot)
                vec_ref[j:j + 1, :n] = jnp.sum(jnp.where(mine, spread, 0.0), axis=0, keepdims=True)


def gather_weights(net, small, big):
    qkv, so, cq, ckv, co, fin, fout = big
    if qkv.shape[0] % UNIT or net.bits < 5:
        small, big = lax.all_gather((small, big), AXES, axis=0, tiled=True) if net.count > 1 else (small, big)
        qkv, so, cq, ckv, co, fin, fout = big
        fout = fout.reshape(-1, 4, UNIT, 512).transpose(0, 2, 1, 3).reshape(512, 2048)
        rows = [jnp.pad(wide(v), (0, 2048 - v.shape[0])) for v in small]
        vectors = jnp.stack(rows + [jnp.zeros((2048,), F32)] * 6)
        return qkv, vectors, jnp.concatenate([fin, fout, ckv, so, cq, co], axis=1)
    a, b, rest = pl.pallas_call(
        pack_kernel, in_specs=[pl.BlockSpec(memory_space=pl.ANY)] * 17, out_specs=[vmem()] * 3,
        out_shape=[shape_of((1, UNIT, 896)), shape_of((1, UNIT, 768)), shape_of((UNIT, 6656))],
        scratch_shapes=[pltpu.VMEM((1, v.shape[0]), BF) for v in small] + [pltpu.SemaphoreType.DMA((21,))],
        compiler_params=params(60), cost_estimate=cost(2), name="pack",
    )(*[v[None] for v in small], *big)
    rest = lax.all_gather(rest, AXES, axis=0, tiled=True)
    orders = [order[::-1] for order in net.orders]
    far = net.bits - 3
    both = [a, b]
    for s in range(far):
        both = [jnp.concatenate([x, net.exchange(x, order[s])], axis=0) for x, order in zip(both, orders)]
    both = [jnp.concatenate([x, net.exchange(x, order[far])], axis=0) for x, order in zip(both, orders)]
    pieces = [[x] for x in both]
    for s in (far + 1, far + 2):
        got = [[net.exchange(x, order[s]) for x in chain] for chain, order in zip(pieces, orders)]
        pieces = [chain + more for chain, more in zip(pieces, got)]
    w, vectors = pl.pallas_call(
        functools.partial(unpack_kernel, net.count), in_specs=[smem(), smem()] + [vmem()] * (len(pieces[0]) * 2), out_specs=[vmem()] * 2,
        out_shape=[shape_of((512, 1536)), shape_of((16, 2048), F32)],
        scratch_shapes=[pltpu.VMEM((net.count, 16, 128), F32)],
        compiler_params=params(40), cost_estimate=cost(2), name="unpack",
    )(net.gather_index(0), net.gather_index(1), *pieces[0], *pieces[1])
    return w, vectors, rest


class Reduction:
    def __init__(self, net, blocks):
        self.net = net
        half = net.count // 2
        self.keep = [x[:half] for x in blocks]
        self.send = [x[half:] for x in blocks]
        self.stage = 0
        self.sums = None

    def state(self):
        return tuple(self.send) if self.sums is None else ()

    def start(self):
        if self.sums is None:
            self.got = [self.net.exchange(x, order[self.stage]) for x, order in zip(self.send, self.net.orders)]

    def add(self):
        if self.sums is not None:
            return
        self.stage += 1
        sums = [wide(k) + wide(g) for k, g in zip(self.keep, self.got)]
        if self.stage == self.net.bits:
            self.sums = [s[0] for s in sums]
            return
        half = sums[0].shape[0] // 2
        self.keep = [low(s[:half]) for s in sums]
        self.send = [low(s[half:]) for s in sums]


def together(groups):
    if groups:
        state = lax.optimization_barrier([(group.keep, group.send) for group in groups])
        for group, (keep, send) in zip(groups, state):
            group.keep, group.send = keep, send


def plan_self(seg, positions):
    rows, length = seg.shape
    starts = jnp.arange(0, length, BLOCK, dtype=jnp.int32)
    begin = starts[None, :] - positions[:, ::BLOCK]
    left = jnp.maximum(starts[None, :] + BLOCK - WINDOW - begin, 0)
    return jnp.zeros_like(begin), (left + WINDOW - 1) // WINDOW


def plan_cross(tseg, sseg):
    last = jnp.int32(1 << 20)
    tkey = jnp.where(tseg == 0, last, tseg)
    skey = jnp.where(sseg == 0, last, sseg)
    begin = jnp.sum(skey[:, None, :] < tkey[:, ::BLOCK, None], axis=2, dtype=jnp.int32)
    end = jnp.sum(skey[:, None, :] <= tkey[:, BLOCK - 1::BLOCK, None], axis=2, dtype=jnp.int32)
    first = (begin // 16) * 16
    return first, jnp.maximum((end - first + WINDOW - 1) // WINDOW - 1, 0)


def per_device(
    target, memory, out_grad, target_segments, source_segments, target_positions,
    self_qkv, self_out, cross_query, cross_kv, cross_out, ffn_in, ffn_out, *small,
):
    net = Net()
    rows = target_segments.shape[0]
    fast = self_qkv.shape[0] % UNIT == 0 and net.bits >= 5
    self_plan = plan_self(target_segments, target_positions)
    cross_plan = plan_cross(target_segments, source_segments)
    tseg = wide(target_segments)[:, None, :]
    sseg = wide(source_segments)[:, None, :]
    w_qkv, vectors, rest = gather_weights(net, small, (self_qkv, self_out, cross_query, cross_kv, cross_out, ffn_in, ffn_out))
    if fast:
        index_a, index_b = net.index(0), net.index(1)
    else:
        index_a = index_b = jnp.arange(512 // UNIT, dtype=jnp.int32)

    qkv, self_mix, self_lse = self_forward(self_plan, target, w_qkv, vectors, tseg)
    hid, cq, pairs, cross_mix, cross_lse = cross_forward(cross_plan, target, self_mix, memory, rest, vectors, tseg, sseg)
    output, h2, cross_mg, ffn_a, ffn_b, dco, mid_small = middle(index_a, index_b, hid, cross_mix, out_grad, rest, vectors)

    groups = [Reduction(net, (ffn_a, ffn_b))] if fast else []

    def backward(causal, plan, q, k, v, mix, grad, lse, kseg):
        out = ()
        for row in range(rows):
            tied = tuple(x for group in groups for x in group.state())
            for group in groups:
                group.start()
            out = attend_back(causal, row, plan, q, k, v, mix, grad, lse, tseg, kseg, out, tied)
            for group in groups:
                group.add()
        return out

    cross_grads = backward(False, cross_plan, (cq, 0), (pairs, 0), (pairs, 1), cross_mix, cross_mg, cross_lse, sseg)
    for group in groups:
        group.start()
    memory_grad, h1, self_mg, cross_a, cross_b, small_sums = cross_dense(
        index_a, index_b, cross_grads, memory, hid, h2, self_mix, rest, dco, vectors)
    for group in groups:
        group.add()
    if fast:
        groups.append(Reduction(net, (cross_a, cross_b)))
    self_grads = backward(True, self_plan, (qkv, 0), (qkv, 1), (qkv, 2), self_mix, self_mg, self_lse, tseg)
    self_a, self_b, lines = self_grad(net.count if fast else 0, index_a, index_b, self_grads, target, mid_small, small_sums)

    if not fast:
        target_out = target_grad(h1, self_grads, w_qkv)
        total = lambda x: lax.psum_scatter(low(x), AXES, scatter_dimension=0, tiled=True).astype(F32) if net.count > 1 else wide(x)
        whole = lambda x: x.reshape(512, -1)
        a, b = whole(cross_a), whole(cross_b)
        d_out = whole(ffn_b).reshape(-1, UNIT, 4, 512).transpose(0, 2, 1, 3).reshape(2048, 512)
        weights = (jnp.concatenate([whole(self_a)[:, :768], whole(self_b)], axis=1), jnp.concatenate([a[:, 1024:], b[:, 1024:]], axis=1),
                   a[:, :512], b[:, :1024], a[:, 512:1024], whole(ffn_a), d_out)
        return (output, target_out, memory_grad, *[total(w) for w in weights], *[total(lines[j, :n]) for j, n in enumerate(VECTORS)])

    groups.append(Reduction(net, (self_a, self_b)))
    target_out = None
    while any(group.sums is None for group in groups):
        open_groups = [group for group in groups if group.sums is None]
        tied = tuple(x for group in open_groups for x in group.state())
        for group in open_groups:
            group.start()
        if groups[-1].stage == 1:
            target_out = target_grad(h1, self_grads, w_qkv, tied)
        for group in open_groups:
            group.add()
        together([group for group in open_groups if group.sums is None])
    (ffn_a, ffn_b), (cross_a, cross_b), (self_a, self_b) = (group.sums for group in groups)
    table = self_a[:, 768:]
    vectors_out = [table[j, :n // net.count] for j, n in enumerate(VECTORS)]
    return (
        output, target_out, memory_grad,
        jnp.concatenate([self_a[:, :768], self_b], axis=1),
        jnp.concatenate([cross_a[:, 1024:], cross_b[:, 1024:]], axis=1),
        cross_a[:, :512], cross_b[:, :1024], cross_a[:, 512:1024],
        ffn_a, jnp.concatenate([ffn_b[:, 512 * b:512 * b + 512] for b in range(4)], axis=0),
        *vectors_out,
    )


def solution(mesh):
    both = ("wide", "narrow")
    matrix, vector = P(both, None), P(both)
    return jax.shard_map(
        per_device, mesh=mesh,
        in_specs=(matrix,) * 13 + (vector,) * 10,
        out_specs=(matrix,) * 10 + (vector,) * 10,
        check_vma=False,
    )
```

time: 498 us -> 360 us (0.72)
  matrix products: 113 us -> 0 us
  Pallas kernels: 128 us -> 192 us
  starting transfers between devices: 97.5 us -> 56.8 us
  local copies, waits for them, and re-layouts: 58 us -> 18.6 us
  other arithmetic: 41.7 us -> 9.25 us
  between operations: 2.31 us -> 15.4 us
  waiting for transfers between devices: 50.2 us -> 61.7 us
    dot_general x21 -> x0, matrix products: 113 us -> none  [mxu(): return lax.dot_general(a, b, dims, preferred_element_type=jnp.float32)]
    pallas_call x10 -> x12, Pallas kernels: 128 us -> 192 us  [the longest x4 61 us: attend_back(): pl.pallas_call(functools.partial(back_kernel, causal, row), grid=(1,), in...]
    ppermute x58 -> x34, starting transfers between devices: 83.8 us -> 45.6 us  [exchange(): lax.ppermute(x, 'wide', [(i, i ^ 1 << bit) for i in range(self.wide)])]
    unnamed x168 -> x64, local copies, waits for them, and re-layouts: 40.6 us -> 11.3 us
    reduce_sum x12 -> x0, other arithmetic: 17.4 us -> none  [the longest x7 8.19 us: column_sums(): return jnp.sum(values, axis=0, dtype=jnp.float32)]
    all_gather x0 -> x1, waiting for transfers between devices: none -> 15.8 us  [gather_weights(): rest = lax.all_gather(rest, AXES, axis=0, tiled=True)]
    convert_element_type x34 -> x2, other arithmetic: 12.1 us -> 0.01 us  [wide(): return x.astype(F32)]
    ppermute x13 -> x8, waiting for transfers between devices: 22.2 us -> 13 us  [exchange(): lax.ppermute(x, 'narrow', [(i, i ^ 1 << bit) for i in range(self.narrow)])]
  transfers between devices with their start and end apart: 71 -> 43, of which waited for: 22 -> 20; matrix products, arithmetic and copies ran while one was open for 17% -> 4% of each run, Pallas kernels for 13% -> 31%
where the time goes in v2:
time: 360 us; the launch traced here: 354 us
  Pallas kernels  192 us (53%)
  waiting for transfers between devices  61.7 us (17%)
  starting transfers between devices  56.8 us (16%)
  local copies, waits for them, and re-layouts  18.6 us (5%)
  between operations  15.4 us (4%)
  other arithmetic  9.25 us (3%)
    pallas_call x4, Pallas kernels, attend_back(): pl.pallas_call(functools.partial(back_kernel, causal, row), grid=(1,), in...  61 us
    pallas_call x1, Pallas kernels, middle(): pl.pallas_call(mid_kernel, grid=(total // t,), in_specs=[smem(), smem(),...  57.4 us
    ppermute x34, starting transfers between devices, exchange(): lax.ppermute(x, 'wide', [(i, i ^ 1 << bit) for i in range(self.wide)])  45.6 us
    ppermute x34, waiting for transfers between devices, exchange(): lax.ppermute(x, 'wide', [(i, i ^ 1 << bit) for i in range(self.wide)])  32.8 us
    pallas_call x1, Pallas kernels, cross_forward(): pl.pallas_call(cross_kernel, grid=(rows,), in_specs=[smem(), smem(), tile...  25 us
    pallas_call x1, Pallas kernels, cross_dense(): pl.pallas_call(cross_dense_kernel, grid=(total // t,), in_specs=[smem(),...  16.8 us
    pallas_call x1, Pallas kernels, self_forward(): pl.pallas_call(self_kernel, grid=(rows,), in_specs=[smem(), smem(), tiled...  16.5 us
    all_gather x1, waiting for transfers between devices, gather_weights(): rest = lax.all_gather(rest, AXES, axis=0, tiled=True)  15.8 us
  transfers between devices with their start and end apart: 43, of which 20 were waited for; matrix products, arithmetic and copies ran while one was open for 4% of the time, Pallas kernels for 31%

profile of v2, /device:TPU:0, one launch (start us, length us, event | category | flops | bytes accessed | tf_op | source)
XLA Modules:
  0.0 354.0 jit_solution(2597393038286862181)
XLA Ops:
  7.3 1.9 pack.1
  9.2 4.1 %collective-permute-start.6 = (bf16[1,16,768]{2,1,0:T(8,128)(2,1)}, bf16[1,16,768]{2,1,0:T(8,128)(2,1)S(1)}, u32[]{:S(2)}, u32[]{:S(2)}) collective-permute-start(bf16[1,16,768]{2,1,0:T(8,128)(2,1)} %get-tuple-element.85), channel_id=1, source_target_pairs={{0,16},{2,18},{4,20},{6,22},{8,24},{10,26},{12,28},{14,30},{16,0},... | collective-permute-start | bytes 73736 | tf_op jit(solution)/shard_map/ppermute | solution.py:583
  16.9 1.8 collective-permute-start.7
  20.7 3.1 collective-permute-done.1
  24.5 1.6 collective-permute-start.2
  26.1 3.3 collective-permute-done.2
  29.4 1.6 collective-permute-start.3
  32.3 5.4 %collective-permute-done.8 = bf16[4,16,768]{2,1,0:T(8,128)(2,1)S(1)} collective-permute-done((bf16[4,16,768]{2,1,0:T(8,128)(2,1)S(1)}, bf16[4,16,768]{2,1,0:T(8,128)(2,1)S(1)}, u32[]{:S(2)}, u32[]{:S(2)}) %collective-permute-start.8) | collective-permute-done | bytes 98336 | tf_op jit(solution)/shard_map/ppermute | solution.py:583
  39.2 6.1 %collective-permute-done.9.refs_5_ = bf16[8,16,768]{2,1,0:T(8,128)(2,1)S(1)} collective-permute-done((bf16[8,16,768]{2,1,0:T(8,128)(2,1)S(1)}, bf16[8,16,768]{2,1,0:T(8,128)(2,1)S(1)}, u32[]{:S(2)}, u32[]{:S(2)}) %collective-permute-start.9) | collective-permute-done | bytes 196640 | tf_op jit(solution)/shard_map/ppermute | solution.py:581
  45.4 1.4 collective-permute-done.11.refs_7_
  46.8 1.3 unpack.1
  48.4 16.5 %self_forward.1 = (bf16[2048,1536]{1,0:T(8,128)(2,1)S(1)}, bf16[2048,512]{1,0:T(8,128)(2,1)S(1)}, f32[2,8,1024]{2,1,0:T(8,128)S(1)}) custom-call(s32[2,8]{1,0:T(2,128)S(1)} %broadcast.64.first_ref, s32[2,8]{1,0:T(2,128)S(1)} %and_select_fusion.extra_ref, bf16[2048,512]{1,0:T(8,128)(2,1)S(1)} %copy-done.5, bf16[512,1536]{1,0:T(8,128)(2,1)S(1)} %get-tuple-element.86.w_ref, ...), custom_call_target="tpu_custom_call" | custom-call | flops 20000000000 | bytes 1048576 | tf_op jit(solution)/shard_map/self_forward/pallas_call | solution.py:198
  64.9 1.3 copy-done.8
  67.4 2.7 copy-done.13
  70.8 15.8 %all-gather.2.cloned.1.call-done.wo_ref.wq_ref.wkv_ref.win_ref.gout_ref.wco_ref = bf16[512,6656]{1,0:T(8,128)(2,1)} async-done(((bf16[16,6656]{1,0:T(8,128)(2,1)}), bf16[512,6656]{1,0:T(8,128)(2,1)}) %all-gather.2.cloned.1.call-update) | async-done | bytes 6815760 | tf_op jit(solution)/shard_map/all_gather | solution.py:653
  87.5 25.0 %cross_forward.1 = (f32[2048,512]{1,0:T(8,128)}, bf16[2048,512]{1,0:T(8,128)(2,1)S(1)}, bf16[2048,1024]{1,0:T(8,128)(2,1)}, bf16[2048,512]{1,0:T(8,128)(2,1)S(1)}, f32[2,8,1024]{2,1,0:T(8,128)S(1)}) custom-call(s32[2,8]{1,0:T(2,128)S(1)} %get-tuple-element.151.first_ref, s32[2,8]{1,0:T(2,128)S(1)} %get-tuple-element.150.extra_ref, bf16[2048,512]{1,0:T(8,128)(2,1)} %x_ref.5, ...), custom_call_target="tpu_custom_call" | custom-call | flops 24999999488 | bytes 1048576 | tf_op jit(solution)/shard_map/cross_forward/pallas_call | solution.py:226
  112.5 1.3 copy-done.17
  113.8 1.3 copy-done.19
  115.1 57.4 %middle.1 = (bf16[2048,512]{1,0:T(8,128)(2,1)}, f32[2048,512]{1,0:T(8,128)}, bf16[2048,512]{1,0:T(8,128)(2,1)}, bf16[32,16,2048]{2,1,0:T(8,128)(2,1)}, bf16[32,1...) custom-call(s32[32]{0:T(128)} %copy-done.2, s32[32]{0:T(128)} %copy-done, ...), custom_call_target="tpu_custom_call" | custom-call | flops 40000000000 | bytes 1048576 | tf_op jit(solution)/shard_map/middle/pallas_call | solution.py:404
  172.5 1.4 slice.311.refs_0_
  174.0 1.4 slice.312.refs_1_
  176.0 15.6 %cross_back.2 = (bf16[2048,512]{1,0:T(8,128)(2,1)S(1)}, bf16[2048,512]{1,0:T(8,128)(2,1)S(1)}, bf16[2048,512]{1,0:T(8,128)(2,1)S(1)}) custom-call(s32[2,8]{1,0:T(2,128)S(1)} %get-tuple-element.151.first_ref, s32[2,8]{1,0:T(2,128)S(1)} %get-tuple-element.150.extra_ref, bf16[2048,512]{1,0:T(8,128)(2,1)S(1)} %copy-done.18, ...), custom_call_target="tpu_custom_call" | custom-call | flops 14000000000 | bytes 1048576 | tf_op jit(solution)/shard_map/cross_back/pallas_call | solution.py:308
  192.0 2.8 collective-permute-start.16
  195.3 2.9 collective-permute-start.14
  198.2 16.8 %cross_back.3 = (bf16[2048,512]{1,0:T(8,128)(2,1)S(1)}, bf16[2048,512]{1,0:T(8,128)(2,1)S(1)}, bf16[2048,512]{1,0:T(8,128)(2,1)S(1)}) custom-call(s32[2,8]{1,0:T(2,128)S(1)} %get-tuple-element.151.first_ref, s32[2,8]{1,0:T(2,128)S(1)} %get-tuple-element.150.extra_ref, ...), custom_call_target="tpu_custom_call", output_to_operand_aliasing={{0}: (10, {}), {1}: (11, {}), {2}: (12, {})} | custom-call | flops 14000000000 | bytes 1048576 | tf_op jit(solution)/shard_map/cross_back/pallas_call | solution.py:308
  215.1 16.8 %cross_dense.1 = (bf16[2048,512]{1,0:T(8,128)(2,1)}, f32[2048,512]{1,0:T(8,128)}, bf16[2048,512]{1,0:T(8,128)(2,1)S(1)}, bf16[32,16,1280]{2,1,0:T(8,128)(2,1)S(1...) custom-call(s32[32]{0:T(128)S(1)} %copy-done.3, s32[32]{0:T(128)S(1)} %copy-done.1, ...), custom_call_target="tpu_custom_call" | custom-call | flops 12000000000 | bytes 1048576 | tf_op jit(solution)/shard_map/cross_dense/pallas_call | solution.py:463
  234.3 2.0 collective-permute-start.24
  236.5 2.1 collective-permute-start.22
  238.6 3.3 collective-permute-done.17
  244.2 14.1 %self_back.2 = (bf16[2048,512]{1,0:T(8,128)(2,1)S(1)}, bf16[2048,512]{1,0:T(8,128)(2,1)S(1)}, bf16[2048,512]{1,0:T(8,128)(2,1)S(1)}) custom-call(s32[2,8]{1,0:T(2,128)S(1)} %broadcast.64.first_ref, s32[2,8]{1,0:T(2,128)S(1)} %and_select_fusion.extra_ref, bf16[2048,1536]{1,0:T(8,128)(2,1)} %copy-done.13, bf16[2048,1536]{1,0:T(8,128)(2,1)} %copy-done.13, ...), custom_call_target="tpu_custom_call" | custom-call | flops 14000000000 | bytes 1048576 | tf_op jit(solution)/shard_map/self_back/pallas_call | solution.py:308
  259.3 2.2 collective-permute-start.40
  261.5 14.5 %self_back.3 = (bf16[2048,512]{1,0:T(8,128)(2,1)S(1)}, bf16[2048,512]{1,0:T(8,128)(2,1)S(1)}, bf16[2048,512]{1,0:T(8,128)(2,1)S(1)}) custom-call(s32[2,8]{1,0:T(2,128)S(1)} %broadcast.64.first_ref, s32[2,8]{1,0:T(2,128)S(1)} %and_select_fusion.extra_ref, ...), custom_call_target="tpu_custom_call", output_to_operand_aliasing={{0}: (10, {}), {1}: (11, {}), {2}: (12, {})} | custom-call | flops 14000000000 | bytes 1048576 | tf_op jit(solution)/shard_map/self_back/pallas_call | solution.py:308
  276.1 7.6 %self_grad.1 = (bf16[32,16,896]{2,1,0:T(8,128)(2,1)S(1)}, bf16[32,16,768]{2,1,0:T(8,128)(2,1)S(1)}, f32[16,2048]{1,0:T(8,128)}) custom-call(s32[32]{0:T(128)S(1)} %copy-done.3, s32[32]{0:T(128)S(1)} %copy-done.1, bf16[2048,512]{1,0:T(8,128)(2,1)S(1)} %get-tuple-element.116.dq_ref, bf16[2048,512]{1,0:T(8,128)(2,1)S(1)} %get-tuple-element.117.dk_ref, ...), custom_call_target="tpu_custom_call" | custom-call | flops 5000000000 | bytes 1048576 | tf_op jit(solution)/shard_map/self_grad/pallas_call | solution.py:538
  284.5 1.2 collective-permute-start.25
  285.9 1.5 collective-permute-start.23
  288.1 2.6 collective-permute-done.25
  292.2 14.7 %collective-permute-start.28 = (bf16[2,16,1280]{2,1,0:T(8,128)(2,1)S(1)}, bf16[2,16,1280]{2,1,0:T(8,128)(2,1)S(1)}, u32[]{:S(2)}, u32[]{:S(2)}) collective-permute-start(bf16[2,16,1280]{2,1,0:T(8,128)(2,1)S(1)} %get-tuple-element.123.refs_0_), channel_id=1, source_target_pairs={{0,8},{2,10},{4,12},{6,14},{8,0},{10,2},{12,4},{14,6},{16,24},{18,... | collective-permute-start | bytes 245768 | tf_op jit(solution)/shard_map/ppermute | solution.py:583
  307.6 1.7 collective-permute-start.31
  309.7 2.3 collective-permute-done.29
  313.3 2.0 collective-permute-done.30
  315.4 2.9 collective-permute-start.38
  318.4 4.9 %target_grad.1 = bf16[2048,512]{1,0:T(8,128)(2,1)} custom-call(f32[2048,512]{1,0:T(8,128)S(1)} %copy-done.7, bf16[2048,512]{1,0:T(8,128)(2,1)S(1)} %get-tuple-element.116.dq_ref, bf16[2048,512]{1,0:T(8,128)(2,1)S(1)} %get-tuple-element.117.dk_ref, bf16[2048,512]{1,0:T(8,128)(2,1)S(1)} %get-tuple-element.118.dv_ref, bf16[512,1536]{1,0:T(8,128)(2,1)S(1)} %copy-done.11, ...), custom_call_target="tpu_custom_call" | custom-call | flops 5000000000 | bytes 1048576 | tf_op jit(solution)/shard_map/target_grad/pallas_call | solution.py:558
  324.3 3.8 %collective-permute-done.39 = bf16[1,16,1280]{2,1,0:T(8,128)(2,1)S(1)} collective-permute-done((bf16[1,16,1280]{2,1,0:T(8,128)(2,1)S(1)}, bf16[1,16,1280]{2,1,0:T(8,128)(2,1)S(1)}, u32[]{:S(2)}, u32[]{:S(2)}) %collective-permute-start.39) | collective-permute-done | bytes 40992 | tf_op jit(solution)/shard_map/ppermute | solution.py:583
  328.5 2.2 collective-permute-start.35
  331.4 1.4 collective-permute-done.35
  332.8 2.7 collective-permute-done.34
  335.6 2.9 collective-permute-start.37
  340.4 4.1 %collective-permute-done.36 = bf16[1,16,896]{2,1,0:T(8,128)(2,1)S(1)} collective-permute-done((bf16[1,16,896]{2,1,0:T(8,128)(2,1)S(1)}, bf16[1,16,896]{2,1,0:T(8,128)(2,1)S(1)}, u32[]{:S(2)}, u32[]{:S(2)}) %collective-permute-start.36) | collective-permute-done | bytes 28704 | tf_op jit(solution)/shard_map/ppermute | solution.py:583
  (206 shorter events, 31.2 us)
Async XLA Ops:
  7.2 79.4 %all-gather.2.cloned.1.call-start = ((), (), s32[]{:S(2)}) async-start(), calls=%async_computation | async-start | bytes 7028736 | tf_op jit(solution)/shard_map/all_gather | solution.py:653
  7.3 38.1 %copy-start.27 = (s32[32]{0:T(128)S(1)}, s32[32]{0:T(128)}, u32[]{:S(2)}) copy-start(s32[32]{0:T(128)} %constant.70.clone) | copy-start | bytes 388
  7.3 38.1 %copy-start.28 = (s32[32]{0:T(128)S(1)}, s32[32]{0:T(128)}, u32[]{:S(2)}) copy-start(s32[32]{0:T(128)} %constant.69.clone) | copy-start | bytes 388
  9.2 7.0 %collective-permute-start.6 = (bf16[1,16,768]{2,1,0:T(8,128)(2,1)}, bf16[1,16,768]{2,1,0:T(8,128)(2,1)S(1)}, u32[]{:S(2)}, u32[]{:S(2)}) collective-permute-start(bf16[1,16,768]{2,1,0:T(8,128)(2,1)} %get-tuple-element.85), channel_id=1, source_target_pairs={{0,16},{2,18},{4,20},{6,22},{8,24},{10,26},{12,28},{14,30},{16,0},... | collective-permute-start | bytes 73736 | tf_op jit(solution)/shard_map/ppermute | solution.py:583
  13.3 5.4 %collective-permute-start = (bf16[1,16,896]{2,1,0:T(8,128)(2,1)}, bf16[1,16,896]{2,1,0:T(8,128)(2,1)S(1)}, u32[]{:S(2)}, u32[]{:S(2)}) collective-permute-start(bf16[1,16,896]{2,1,0:T(8,128)(2,1)} %get-tuple-element.84), channel_id=1, source_target_pairs={{0,16},{2,18},{4,20},{6,22},{8,24},{10,26},{12,28},{14,30},{16,0},... | collective-permute-start | bytes 86024 | tf_op jit(solution)/shard_map/ppermute | solution.py:583
  16.9 14.1 %collective-permute-start.7 = (bf16[2,16,768]{2,1,0:T(8,128)(2,1)S(1)}, bf16[2,16,768]{2,1,0:T(8,128)(2,1)S(1)}, u32[]{:S(2)}, u32[]{:S(2)}) collective-permute-start(bf16[2,16,768]{2,1,0:T(8,128)(2,1)S(1)} %pad_maximum_fusion.5), channel_id=1, source_target_pairs={{0,8},{2,10},{4,12},{6,14},{8,0},{10,2},{12,4},{14,6},{16,24},{18,... | collective-permute-start | bytes 147464 | tf_op jit(solution)/shard_map/ppermute | solution.py:583
  19.5 4.2 %collective-permute-start.1 = (bf16[2,16,896]{2,1,0:T(8,128)(2,1)S(1)}, bf16[2,16,896]{2,1,0:T(8,128)(2,1)S(1)}, u32[]{:S(2)}, u32[]{:S(2)}) collective-permute-start(bf16[2,16,896]{2,1,0:T(8,128)(2,1)S(1)} %pad_maximum_fusion.4), channel_id=1, source_target_pairs={{0,8},{2,10},{4,12},{6,14},{8,0},{10,2},{12,4},{14,6},{16,24},{18,... | collective-permute-start | bytes 172040 | tf_op jit(solution)/shard_map/ppermute | solution.py:583
  24.5 4.9 %collective-permute-start.2 = (bf16[4,16,896]{2,1,0:T(8,128)(2,1)S(1)}, bf16[4,16,896]{2,1,0:T(8,128)(2,1)S(1)}, u32[]{:S(2)}, u32[]{:S(2)}) collective-permute-start(bf16[4,16,896]{2,1,0:T(8,128)(2,1)S(1)} %pad_maximum_fusion.1), channel_id=1, source_target_pairs={{0,1},{1,0},{2,3},{3,2},{4,5},{5,4},{6,7},{7,6},{8,9},{9,8},{10,11... | collective-permute-start | bytes 344072 | tf_op jit(solution)/shard_map/ppermute | solution.py:581
  29.4 9.2 %collective-permute-start.3 = (bf16[8,16,896]{2,1,0:T(8,128)(2,1)S(1)}, bf16[8,16,896]{2,1,0:T(8,128)(2,1)S(1)}, u32[]{:S(2)}, u32[]{:S(2)}) collective-permute-start(bf16[8,16,896]{2,1,0:T(8,128)(2,1)S(1)} %constant_dynamic-update-slice_fusion.refs_0_), channel_id=1, source_target_pairs={{0,4},{2,6},{4,0},{6,2},{8,12},{10,14},{12,8},{14,10},{16,20},{18,... | collective-permute-start | bytes 688136 | tf_op jit(solution)/shard_map/ppermute | solution.py:583
  31.7 6.0 %collective-permute-start.8 = (bf16[4,16,768]{2,1,0:T(8,128)(2,1)S(1)}, bf16[4,16,768]{2,1,0:T(8,128)(2,1)S(1)}, u32[]{:S(2)}, u32[]{:S(2)}) collective-permute-start(bf16[4,16,768]{2,1,0:T(8,128)(2,1)S(1)} %pad_maximum_fusion.2), channel_id=1, source_target_pairs={{0,4},{2,6},{4,0},{6,2},{8,12},{10,14},{12,8},{14,10},{16,20},{18,... | collective-permute-start | bytes 294920 | tf_op jit(solution)/shard_map/ppermute | solution.py:583
  37.7 7.6 %collective-permute-start.9 = (bf16[8,16,768]{2,1,0:T(8,128)(2,1)S(1)}, bf16[8,16,768]{2,1,0:T(8,128)(2,1)S(1)}, u32[]{:S(2)}, u32[]{:S(2)}) collective-permute-start(bf16[8,16,768]{2,1,0:T(8,128)(2,1)S(1)} %constant_dynamic-update-slice_fusion.4.refs_4_), channel_id=1, source_target_pairs={{0,1},{1,0},{2,3},{3,2},{4,5},{5,4},{6,7},{7,6},{8,9},{9,8},{10,11... | collective-permute-start | bytes 589832 | tf_op jit(solution)/shard_map/ppermute | solution.py:581
  38.6 6.8 %collective-permute-start.4 = (bf16[8,16,896]{2,1,0:T(8,128)(2,1)S(1)}, bf16[8,16,896]{2,1,0:T(8,128)(2,1)S(1)}, u32[]{:S(2)}, u32[]{:S(2)}) collective-permute-start(bf16[8,16,896]{2,1,0:T(8,128)(2,1)S(1)} %constant_dynamic-update-slice_fusion.refs_0_), channel_id=1, source_target_pairs={{0,2},{2,0},{4,6},{6,4},{8,10},{10,8},{12,14},{14,12},{16,18},{18,... | collective-permute-start | bytes 688136 | tf_op jit(solution)/shard_map/ppermute | solution.py:583
  38.6 8.2 %collective-permute-start.5 = (bf16[8,16,896]{2,1,0:T(8,128)(2,1)S(1)}, bf16[8,16,896]{2,1,0:T(8,128)(2,1)S(1)}, u32[]{:S(2)}, u32[]{:S(2)}) collective-permute-start(bf16[8,16,896]{2,1,0:T(8,128)(2,1)S(1)} %collective-permute-done.3.refs_1_), channel_id=1, source_target_pairs={{0,2},{2,0},{4,6},{6,4},{8,10},{10,8},{12,14},{14,12},{16,18},{18,... | collective-permute-start | bytes 688136 | tf_op jit(solution)/shard_map/ppermute | solution.py:583
  39.1 6.2 %collective-permute-start.10 = (bf16[8,16,768]{2,1,0:T(8,128)(2,1)S(1)}, bf16[8,16,768]{2,1,0:T(8,128)(2,1)S(1)}, u32[]{:S(2)}, u32[]{:S(2)}) collective-permute-start(bf16[8,16,768]{2,1,0:T(8,128)(2,1)S(1)} %constant_dynamic-update-slice_fusion.4.refs_4_), channel_id=1, source_target_pairs={{0,2},{2,0},{4,6},{6,4},{8,10},{10,8},{12,14},{14,12},{16,18},{18,... | collective-permute-start | bytes 589832 | tf_op jit(solution)/shard_map/ppermute | solution.py:583
  45.3 1.4 collective-permute-start.11
  175.4 16.2 %collective-permute-start.13 = (bf16[16,16,2048]{2,1,0:T(8,128)(2,1)S(1)}, bf16[16,16,2048]{2,1,0:T(8,128)(2,1)S(1)}, u32[]{:S(2)}, u32[]{:S(2)}) collective-permute-start(bf16[16,16,2048]{2,1,0:T(8,128)(2,1)S(1)} %slice.312.refs_1_), channel_id=1, source_target_pairs={{0,2},{2,0},{4,6},{6,4},{8,10},{10,8},{12,14},{14,12},{16,18},{18,... | collective-permute-start | bytes 3145736 | tf_op jit(solution)/shard_map/ppermute | solution.py:583
  175.5 19.4 %collective-permute-start.12 = (bf16[16,16,2048]{2,1,0:T(8,128)(2,1)S(1)}, bf16[16,16,2048]{2,1,0:T(8,128)(2,1)S(1)}, u32[]{:S(2)}, u32[]{:S(2)}) collective-permute-start(bf16[16,16,2048]{2,1,0:T(8,128)(2,1)S(1)} %slice.311.refs_0_), channel_id=1, source_target_pairs={{0,2},{2,0},{4,6},{6,4},{8,10},{10,8},{12,14},{14,12},{16,18},{18,... | collective-permute-start | bytes 3145736 | tf_op jit(solution)/shard_map/ppermute | solution.py:583
  192.0 40.5 %collective-permute-start.16 = (bf16[8,16,2048]{2,1,0:T(8,128)(2,1)S(1)}, bf16[8,16,2048]{2,1,0:T(8,128)(2,1)S(1)}, u32[]{:S(2)}, u32[]{:S(2)}) collective-permute-start(bf16[8,16,2048]{2,1,0:T(8,128)(2,1)S(1)} %slice.392.refs_4_), channel_id=1, source_target_pairs={{0,1},{1,0},{2,3},{3,2},{4,5},{5,4},{6,7},{7,6},{8,9},{9,8},{10,11... | collective-permute-start | bytes 1572872 | tf_op jit(solution)/shard_map/ppermute | solution.py:581
  195.3 37.4 %collective-permute-start.14 = (bf16[8,16,2048]{2,1,0:T(8,128)(2,1)S(1)}, bf16[8,16,2048]{2,1,0:T(8,128)(2,1)}, u32[]{:S(2)}, u32[]{:S(2)}) collective-permute-start(bf16[8,16,2048]{2,1,0:T(8,128)(2,1)S(1)} %slice.391.refs_3_), channel_id=1, source_target_pairs={{0,4},{2,6},{4,0},{6,2},{8,12},{10,14},{12,8},{14,10},{16,20},{18,... | collective-permute-start | bytes 1572872 | tf_op jit(solution)/shard_map/ppermute | solution.py:583
  198.2 16.9 %copy-start.12 = (f32[512,512]{1,0:T(8,128)S(1)}, f32[512,512]{1,0:T(8,128)}, u32[]{:S(2)}) copy-start(f32[512,512]{1,0:T(8,128)} %get-tuple-element.106.co_ref) | copy-start | bytes 3145732
  231.9 2.2 collective-permute-start.21
  232.0 4.3 %collective-permute-start.20 = (bf16[16,16,1280]{2,1,0:T(8,128)(2,1)S(1)}, bf16[16,16,1280]{2,1,0:T(8,128)(2,1)S(1)}, u32[]{:S(2)}, u32[]{:S(2)}) collective-permute-start(bf16[16,16,1280]{2,1,0:T(8,128)(2,1)S(1)} %slice.325.refs_2_), channel_id=1, source_target_pairs={{0,2},{2,0},{4,6},{6,4},{8,10},{10,8},{12,14},{14,12},{16,18},{18,... | collective-permute-start | bytes 1966088 | tf_op jit(solution)/shard_map/ppermute | solution.py:583
  232.7 9.2 %collective-permute-start.17 = (bf16[4,16,2048]{2,1,0:T(8,128)(2,1)S(1)}, bf16[4,16,2048]{2,1,0:T(8,128)(2,1)S(1)}, u32[]{:S(2)}, u32[]{:S(2)}) collective-permute-start(bf16[4,16,2048]{2,1,0:T(8,128)(2,1)S(1)} %slice.399), channel_id=1, source_target_pairs={{0,4},{2,6},{4,0},{6,2},{8,12},{10,14},{12,8},{14,10},{16,20},{18,... | collective-permute-start | bytes 786440 | tf_op jit(solution)/shard_map/ppermute | solution.py:583
  233.9 9.2 %collective-permute-start.15 = (bf16[4,16,2048]{2,1,0:T(8,128)(2,1)S(1)}, bf16[4,16,2048]{2,1,0:T(8,128)(2,1)S(1)}, u32[]{:S(2)}, u32[]{:S(2)}) collective-permute-start(bf16[4,16,2048]{2,1,0:T(8,128)(2,1)S(1)} %slice.395), channel_id=1, source_target_pairs={{0,1},{1,0},{2,3},{3,2},{4,5},{5,4},{6,7},{7,6},{8,9},{9,8},{10,11... | collective-permute-start | bytes 786440 | tf_op jit(solution)/shard_map/ppermute | solution.py:581
  234.3 49.6 %collective-permute-start.24 = (bf16[8,16,1280]{2,1,0:T(8,128)(2,1)S(1)}, bf16[8,16,1280]{2,1,0:T(8,128)(2,1)S(1)}, u32[]{:S(2)}, u32[]{:S(2)}) collective-permute-start(bf16[8,16,1280]{2,1,0:T(8,128)(2,1)S(1)} %slice.406.refs_6_), channel_id=1, source_target_pairs={{0,1},{1,0},{2,3},{3,2},{4,5},{5,4},{6,7},{7,6},{8,9},{9,8},{10,11... | collective-permute-start | bytes 983048 | tf_op jit(solution)/shard_map/ppermute | solution.py:581
  236.5 48.0 %collective-permute-start.22 = (bf16[8,16,1280]{2,1,0:T(8,128)(2,1)S(1)}, bf16[8,16,1280]{2,1,0:T(8,128)(2,1)S(1)}, u32[]{:S(2)}, u32[]{:S(2)}) collective-permute-start(bf16[8,16,1280]{2,1,0:T(8,128)(2,1)S(1)} %slice.405.refs_5_), channel_id=1, source_target_pairs={{0,4},{2,6},{4,0},{6,2},{8,12},{10,14},{12,8},{14,10},{16,20},{18,... | collective-permute-start | bytes 983048 | tf_op jit(solution)/shard_map/ppermute | solution.py:583
  242.0 16.4 %collective-permute-start.19 = (bf16[2,16,2048]{2,1,0:T(8,128)(2,1)S(1)}, bf16[2,16,2048]{2,1,0:T(8,128)(2,1)S(1)}, u32[]{:S(2)}, u32[]{:S(2)}) collective-permute-start(bf16[2,16,2048]{2,1,0:T(8,128)(2,1)S(1)} %slice.400.refs_1_), channel_id=1, source_target_pairs={{0,8},{2,10},{4,12},{6,14},{8,0},{10,2},{12,4},{14,6},{16,24},{18,... | collective-permute-start | bytes 393224 | tf_op jit(solution)/shard_map/ppermute | solution.py:583
  243.3 16.0 %collective-permute-start.18 = (bf16[2,16,2048]{2,1,0:T(8,128)(2,1)S(1)}, bf16[2,16,2048]{2,1,0:T(8,128)(2,1)S(1)}, u32[]{:S(2)}, u32[]{:S(2)}) collective-permute-start(bf16[2,16,2048]{2,1,0:T(8,128)(2,1)S(1)} %slice.396.refs_0_), channel_id=1, source_target_pairs={{0,8},{2,10},{4,12},{6,14},{8,0},{10,2},{12,4},{14,6},{16,24},{18,... | collective-permute-start | bytes 393224 | tf_op jit(solution)/shard_map/ppermute | solution.py:583
  258.4 27.5 %collective-permute-start.41 = (bf16[1,16,2048]{2,1,0:T(8,128)(2,1)S(1)}, bf16[1,16,2048]{2,1,0:T(8,128)(2,1)S(1)}, u32[]{:S(2)}, u32[]{:S(2)}) collective-permute-start(bf16[1,16,2048]{2,1,0:T(8,128)(2,1)S(1)} %slice.404.refs_4_), channel_id=1, source_target_pairs={{0,16},{2,18},{4,20},{6,22},{8,24},{10,26},{12,28},{14,30},{16,0},... | collective-permute-start | bytes 196616 | tf_op jit(solution)/shard_map/ppermute | solution.py:583
  259.3 28.1 %collective-permute-start.40 = (bf16[1,16,2048]{2,1,0:T(8,128)(2,1)S(1)}, bf16[1,16,2048]{2,1,0:T(8,128)(2,1)S(1)}, u32[]{:S(2)}, u32[]{:S(2)}) collective-permute-start(bf16[1,16,2048]{2,1,0:T(8,128)(2,1)S(1)} %slice.402.refs_3_), channel_id=1, source_target_pairs={{0,16},{2,18},{4,20},{6,22},{8,24},{10,26},{12,28},{14,30},{16,0},... | collective-permute-start | bytes 196616 | tf_op jit(solution)/shard_map/ppermute | solution.py:583
  283.7 8.2 %collective-permute-start.27 = (bf16[16,16,768]{2,1,0:T(8,128)(2,1)S(1)}, bf16[16,16,768]{2,1,0:T(8,128)(2,1)S(1)}, u32[]{:S(2)}, u32[]{:S(2)}) collective-permute-start(bf16[16,16,768]{2,1,0:T(8,128)(2,1)S(1)} %slice.349), channel_id=1, source_target_pairs={{0,2},{2,0},{4,6},{6,4},{8,10},{10,8},{12,14},{14,12},{16,18},{18,... | collective-permute-start | bytes 1179656 | tf_op jit(solution)/shard_map/ppermute | solution.py:583
  283.9 8.2 %collective-permute-start.26 = (bf16[16,16,896]{2,1,0:T(8,128)(2,1)S(1)}, bf16[16,16,896]{2,1,0:T(8,128)(2,1)S(1)}, u32[]{:S(2)}, u32[]{:S(2)}) collective-permute-start(bf16[16,16,896]{2,1,0:T(8,128)(2,1)S(1)} %slice.346), channel_id=1, source_target_pairs={{0,2},{2,0},{4,6},{6,4},{8,10},{10,8},{12,14},{14,12},{16,18},{18,... | collective-permute-start | bytes 1376264 | tf_op jit(solution)/shard_map/ppermute | solution.py:583
  284.5 6.2 %collective-permute-start.25 = (bf16[4,16,1280]{2,1,0:T(8,128)(2,1)S(1)}, bf16[4,16,1280]{2,1,0:T(8,128)(2,1)S(1)}, u32[]{:S(2)}, u32[]{:S(2)}) collective-permute-start(bf16[4,16,1280]{2,1,0:T(8,128)(2,1)S(1)} %slice.413), channel_id=1, source_target_pairs={{0,4},{2,6},{4,0},{6,2},{8,12},{10,14},{12,8},{14,10},{16,20},{18,... | collective-permute-start | bytes 491528 | tf_op jit(solution)/shard_map/ppermute | solution.py:583
  285.9 5.9 %collective-permute-start.23 = (bf16[4,16,1280]{2,1,0:T(8,128)(2,1)S(1)}, bf16[4,16,1280]{2,1,0:T(8,128)(2,1)S(1)}, u32[]{:S(2)}, u32[]{:S(2)}) collective-permute-start(bf16[4,16,1280]{2,1,0:T(8,128)(2,1)S(1)} %slice.409), channel_id=1, source_target_pairs={{0,1},{1,0},{2,3},{3,2},{4,5},{5,4},{6,7},{7,6},{8,9},{9,8},{10,11... | collective-permute-start | bytes 491528 | tf_op jit(solution)/shard_map/ppermute | solution.py:581
  292.0 26.4 %copy-start.11 = (bf16[512,1536]{1,0:T(8,128)(2,1)S(1)}, bf16[512,1536]{1,0:T(8,128)(2,1)}, u32[]{:S(2)}) copy-start(bf16[512,1536]{1,0:T(8,128)(2,1)} %copy-done.10) | copy-start | bytes 4718596
  292.1 26.3 %copy-start.7 = (f32[2048,512]{1,0:T(8,128)S(1)}, f32[2048,512]{1,0:T(8,128)}, u32[]{:S(2)}) copy-start(f32[2048,512]{1,0:T(8,128)} %get-tuple-element.107.h1_ref) | copy-start | bytes 12582916
  292.2 17.4 %collective-permute-start.28 = (bf16[2,16,1280]{2,1,0:T(8,128)(2,1)S(1)}, bf16[2,16,1280]{2,1,0:T(8,128)(2,1)S(1)}, u32[]{:S(2)}, u32[]{:S(2)}) collective-permute-start(bf16[2,16,1280]{2,1,0:T(8,128)(2,1)S(1)} %get-tuple-element.123.refs_0_), channel_id=1, source_target_pairs={{0,8},{2,10},{4,12},{6,14},{8,0},{10,2},{12,4},{14,6},{16,24},{18,... | collective-permute-start | bytes 245768 | tf_op jit(solution)/shard_map/ppermute | solution.py:583
  307.6 4.4 %collective-permute-start.29 = (bf16[2,16,1280]{2,1,0:T(8,128)(2,1)S(1)}, bf16[2,16,1280]{2,1,0:T(8,128)(2,1)S(1)}, u32[]{:S(2)}, u32[]{:S(2)}) collective-permute-start(bf16[2,16,1280]{2,1,0:T(8,128)(2,1)S(1)} %get-tuple-element.124.refs_1_), channel_id=1, source_target_pairs={{0,8},{2,10},{4,12},{6,14},{8,0},{10,2},{12,4},{14,6},{16,24},{18,... | collective-permute-start | bytes 245768 | tf_op jit(solution)/shard_map/ppermute | solution.py:583
  307.6 5.7 %collective-permute-start.31 = (bf16[8,16,768]{2,1,0:T(8,128)(2,1)S(1)}, bf16[8,16,768]{2,1,0:T(8,128)(2,1)S(1)}, u32[]{:S(2)}, u32[]{:S(2)}) collective-permute-start(bf16[8,16,768]{2,1,0:T(8,128)(2,1)S(1)} %get-tuple-element.126.refs_3_), channel_id=1, source_target_pairs={{0,1},{1,0},{2,3},{3,2},{4,5},{5,4},{6,7},{7,6},{8,9},{9,8},{10,11... | collective-permute-start | bytes 589832 | tf_op jit(solution)/shard_map/ppermute | solution.py:581
  309.3 6.0 %collective-permute-start.30 = (bf16[8,16,896]{2,1,0:T(8,128)(2,1)S(1)}, bf16[8,16,896]{2,1,0:T(8,128)(2,1)S(1)}, u32[]{:S(2)}, u32[]{:S(2)}) collective-permute-start(bf16[8,16,896]{2,1,0:T(8,128)(2,1)S(1)} %get-tuple-element.125.refs_2_), channel_id=1, source_target_pairs={{0,4},{2,6},{4,0},{6,2},{8,12},{10,14},{12,8},{14,10},{16,20},{18,... | collective-permute-start | bytes 688136 | tf_op jit(solution)/shard_map/ppermute | solution.py:583
  315.4 8.9 %collective-permute-start.38 = (bf16[1,16,1280]{2,1,0:T(8,128)(2,1)S(1)}, bf16[1,16,1280]{2,1,0:T(8,128)(2,1)S(1)}, u32[]{:S(2)}, u32[]{:S(2)}) collective-permute-start(bf16[1,16,1280]{2,1,0:T(8,128)(2,1)S(1)} %get-tuple-element.145), channel_id=1, source_target_pairs={{0,16},{2,18},{4,20},{6,22},{8,24},{10,26},{12,28},{14,30},{16,0},... | collective-permute-start | bytes 122888 | tf_op jit(solution)/shard_map/ppermute | solution.py:583
  323.2 4.9 %collective-permute-start.39 = (bf16[1,16,1280]{2,1,0:T(8,128)(2,1)S(1)}, bf16[1,16,1280]{2,1,0:T(8,128)(2,1)S(1)}, u32[]{:S(2)}, u32[]{:S(2)}) collective-permute-start(bf16[1,16,1280]{2,1,0:T(8,128)(2,1)S(1)} %get-tuple-element.147), channel_id=1, source_target_pairs={{0,16},{2,18},{4,20},{6,22},{8,24},{10,26},{12,28},{14,30},{16,0},... | collective-permute-start | bytes 122888 | tf_op jit(solution)/shard_map/ppermute | solution.py:583
  323.3 4.9 %collective-permute-start.33 = (bf16[4,16,768]{2,1,0:T(8,128)(2,1)S(1)}, bf16[4,16,768]{2,1,0:T(8,128)(2,1)S(1)}, u32[]{:S(2)}, u32[]{:S(2)}) collective-permute-start(bf16[4,16,768]{2,1,0:T(8,128)(2,1)S(1)} %get-tuple-element.135), channel_id=1, source_target_pairs={{0,4},{2,6},{4,0},{6,2},{8,12},{10,14},{12,8},{14,10},{16,20},{18,... | collective-permute-start | bytes 294920 | tf_op jit(solution)/shard_map/ppermute | solution.py:583
  323.7 4.8 %collective-permute-start.32 = (bf16[4,16,896]{2,1,0:T(8,128)(2,1)S(1)}, bf16[4,16,896]{2,1,0:T(8,128)(2,1)S(1)}, u32[]{:S(2)}, u32[]{:S(2)}) collective-permute-start(bf16[4,16,896]{2,1,0:T(8,128)(2,1)S(1)} %get-tuple-element.133), channel_id=1, source_target_pairs={{0,1},{1,0},{2,3},{3,2},{4,5},{5,4},{6,7},{7,6},{8,9},{9,8},{10,11... | collective-permute-start | bytes 344072 | tf_op jit(solution)/shard_map/ppermute | solution.py:581
  328.5 4.3 %collective-permute-start.35 = (bf16[2,16,768]{2,1,0:T(8,128)(2,1)S(1)}, bf16[2,16,768]{2,1,0:T(8,128)(2,1)S(1)}, u32[]{:S(2)}, u32[]{:S(2)}) collective-permute-start(bf16[2,16,768]{2,1,0:T(8,128)(2,1)S(1)} %get-tuple-element.139), channel_id=1, source_target_pairs={{0,8},{2,10},{4,12},{6,14},{8,0},{10,2},{12,4},{14,6},{16,24},{18,... | collective-permute-start | bytes 147464 | tf_op jit(solution)/shard_map/ppermute | solution.py:583
  331.4 4.2 %collective-permute-start.34 = (bf16[2,16,896]{2,1,0:T(8,128)(2,1)S(1)}, bf16[2,16,896]{2,1,0:T(8,128)(2,1)S(1)}, u32[]{:S(2)}, u32[]{:S(2)}) collective-permute-start(bf16[2,16,896]{2,1,0:T(8,128)(2,1)S(1)} %get-tuple-element.137), channel_id=1, source_target_pairs={{0,8},{2,10},{4,12},{6,14},{8,0},{10,2},{12,4},{14,6},{16,24},{18,... | collective-permute-start | bytes 172040 | tf_op jit(solution)/shard_map/ppermute | solution.py:583
  335.6 4.8 %collective-permute-start.37 = (bf16[1,16,768]{2,1,0:T(8,128)(2,1)S(1)}, bf16[1,16,768]{2,1,0:T(8,128)(2,1)S(1)}, u32[]{:S(2)}, u32[]{:S(2)}) collective-permute-start(bf16[1,16,768]{2,1,0:T(8,128)(2,1)S(1)} %get-tuple-element.143), channel_id=1, source_target_pairs={{0,16},{2,18},{4,20},{6,22},{8,24},{10,26},{12,28},{14,30},{16,0},... | collective-permute-start | bytes 73736 | tf_op jit(solution)/shard_map/ppermute | solution.py:583
  339.7 4.8 %collective-permute-start.36 = (bf16[1,16,896]{2,1,0:T(8,128)(2,1)S(1)}, bf16[1,16,896]{2,1,0:T(8,128)(2,1)S(1)}, u32[]{:S(2)}, u32[]{:S(2)}) collective-permute-start(bf16[1,16,896]{2,1,0:T(8,128)(2,1)S(1)} %get-tuple-element.141), channel_id=1, source_target_pairs={{0,16},{2,18},{4,20},{6,22},{8,24},{10,26},{12,28},{14,30},{16,0},... | collective-permute-start | bytes 86024 | tf_op jit(solution)/shard_map/ppermute | solution.py:583
  (24 other events, 168.8 us)
Sparse Core Ops, SparseCore 0:
  11.4 75.0 all-gather.1
